TPU v7x, 32 devices: a whole 2x2x4 slice. The times are simulated.
32 devices in a mesh: panel: 8 (over z, y), feat: 4 (over x, core).
Axes of the slice: x: 2, y: 2, z: 4, core: 2. Of those that a mesh axis runs over, the one named last changes fastest.
Arguments:
- dosage: bfloat16 [7168, 4096], P('panel', 'feat'), may hold values from 0 to 1, as said below
- row_counts: int32 [8], P('panel'), may hold values from 0 to 896, as said below
- assignment: int32 [7168], P('panel'), may hold values from 0 to 7, as said below
- center: float32 [4096], replicated, may hold values from 0.06 to 0.54
- weight: float32 [4096], replicated, may hold values from 0.5 to 2
Outputs:
- kinship: float32 [4096, 4, 512], P('panel', None, 'feat')
Inputs may be any that keep to these rules, and one draw needn't show every extreme that they name: Batch b has row_counts[b] live rows; some batch has exactly 896 in every draw. `assignment`: over all batches each panel receives exactly 512 live rows; one batch sends at most 112 live rows to one panel, and some batch sends exactly 112 to every panel in every draw. Entries of rows that are not live are ignored. `dosage`: zero where a k-mer is absent.
All inputs are finite; a program needn't handle non-finite values.
Results may differ from a plain program's by a relative error of at most 0.004.
Values may be sent and summed in bfloat16 or wider, within the bound.
No kernel may reach another device: no remote copies, remote signals or barrier semaphores. Data moves between devices by JAX's collectives and lax.ppermute only.
A program may use at most 64 MiB of HBM per device.

v0:
```python
import math

import jax
import jax.numpy as jnp
from jax import lax
from jax.sharding import PartitionSpec as P

F = 4096
P_SIZE = 512
ROUNDS = 4


def shifted(value, axis, steps):
    count = lax.axis_size(axis)
    pairs = [(source, (source + steps) % count) for source in range(count)]
    return lax.ppermute(value, axis, pairs)


def tile_of(left_rows, partner):
    return lax.dot_general(
        left_rows, partner, (((1,), (1,)), ((), ())), preferred_element_type=jnp.float32
    )


def shards(dosage, row_counts, assignment, center, weight):
    panel_total = lax.axis_size("panel")
    feat_index = lax.axis_index("feat")
    capacity = dosage.shape[0]
    feat_width = dosage.shape[1]
    send_rows = capacity // panel_total
    feat_start = feat_index * feat_width
    center_part = lax.dynamic_slice_in_dim(center, feat_start, feat_width)
    weight_part = lax.dynamic_slice_in_dim(weight, feat_start, feat_width)
    standard = ((dosage.astype(jnp.float32) - center_part) * weight_part).astype(jnp.bfloat16)
    slot_ids = jnp.arange(capacity, dtype=jnp.int32)
    live_rows = slot_ids < row_counts[0]
    targets = jnp.arange(panel_total, dtype=jnp.int32)
    onehot = ((assignment[:, None] == targets[None, :]) & live_rows[:, None]).astype(jnp.int32)
    earlier = jnp.sum((jnp.cumsum(onehot, axis=0) - onehot) * onehot, axis=1)
    slot_index = jnp.where(live_rows, assignment * send_rows + earlier, panel_total * send_rows)
    outgoing = (
        jnp.zeros((panel_total * send_rows, feat_width), jnp.bfloat16)
        .at[slot_index]
        .set(standard, mode="drop")
    )
    outgoing = outgoing.reshape(panel_total, send_rows, feat_width)
    sent_counts = jnp.sum(onehot, axis=0).reshape(panel_total, 1)
    incoming, arrived = (
        lax.all_to_all(outgoing, "panel", split_axis=0, concat_axis=0, tiled=True),
        lax.all_to_all(sent_counts, "panel", split_axis=0, concat_axis=0, tiled=True),
    )
    arrived_rows = arrived[:, 0]
    offsets = jnp.cumsum(arrived_rows) - arrived_rows
    within = jnp.arange(send_rows, dtype=jnp.int32)
    positions = jnp.where(
        within[None, :] < arrived_rows[:, None], offsets[:, None] + within[None, :], P_SIZE
    )
    own_panel = (
        jnp.zeros((P_SIZE, feat_width), jnp.bfloat16)
        .at[positions.reshape(-1)]
        .set(incoming.reshape(-1, feat_width), mode="drop")
    )
    tile_scale = 1.0 / math.sqrt(F)
    partners = []
    for round_index in range(ROUNDS):
        partners.append(shifted(own_panel, "panel", round_index + 1))
    kinship = (
        jnp.concatenate(
            [
                lax.psum_scatter(
                    tile_of(own_panel, partner)[:, None, :], "feat", scatter_dimension=2, tiled=True
                )
                for partner in partners
            ],
            axis=1,
        )
        * tile_scale
    )
    return kinship


def solution(mesh):
    in_specs = (P("panel", "feat"), P("panel"), P("panel"), P(), P())
    out_specs = P("panel", None, "feat")
    return jax.shard_map(shards, mesh=mesh, in_specs=in_specs, out_specs=out_specs, check_vma=False)
```

profile of v0, /device:TPU:0, one launch (start us, length us, event | category | flops | bytes accessed | tf_op | source)
XLA Modules:
  0.0 292.7 jit_solution(4500839031455315587)
XLA Ops:
  7.2 0.7 fusion.10
  7.9 2.0 reduce-window.19
  10.4 0.9 fusion.7
  11.2 0.7 copy.16
  11.9 7.3 %all-to-all-start = ((s32[8,1,1]{2,1,0:T(1,128)}), s32[8,1,1]{2,1,0:T(1,128)S(1)}, u32[]{:S(2)}, u32[]{:S(2)}) async-start(s32[8,1,1]{2,1,0:T(1,128)} %copy.16), calls=%async_computation | async-start | bytes 8192 | tf_op jit(solution)/shard_map/all_to_all | solution.py:50
  19.2 0.7 dynamic_slice.6
  19.9 0.7 dynamic_slice.7
  20.6 0.7 compare_select_fusion.1
  21.3 8.0 %scatter_custom_fusion = bf16[896,1024]{1,0:T(8,128)(2,1)} fusion(s32[896]{0:T(1024)S(1)} %compare_select_fusion.1, bf16[896,1024]{1,0:T(8,128)(2,1)} %param.5, f32[1024]{0:T(1024)S(1)} %dynamic_slice.7, f32[1024]{0:T(1024)S(1)} %dynamic_slice.6, bf16[]{:T(256)} %constant.10.clone.1), kind=kCustom, calls=%fused_computation.3 | custom fusion | flops 3670016 | bytes 3678210 | tf_op jit(solution)/shard_map/scatter | solution.py:44
  29.3 6.0 %all-to-all-start.1 = ((bf16[8,112,1024]{2,1,0:T(8,128)(2,1)}), bf16[8,112,1024]{2,1,0:T(8,128)(2,1)S(1)}, u32[]{:S(2)}, u32[]{:S(2)}) async-start(bf16[8,112,1024]{2,1,0:T(8,128)(2,1)} %bitcast.7), calls=%async_computation.1 | async-start | bytes 3670016 | tf_op jit(solution)/shard_map/all_to_all | solution.py:49
  35.3 0.2 reduce
  36.0 41.4 %all-to-all-done.1 = bf16[8,112,1024]{2,1,0:T(8,128)(2,1)S(1)} async-done(((bf16[8,112,1024]{2,1,0:T(8,128)(2,1)}), bf16[8,112,1024]{2,1,0:T(8,128)(2,1)S(1)}, u32[]{:S(2)}, u32[]{:S(2)}) %all-to-all-start.1) | async-done | bytes 1835040 | tf_op jit(solution)/shard_map/all_to_all | solution.py:49
  77.4 5.9 %scatter_custom_fusion.1 = bf16[512,1024]{1,0:T(8,128)(2,1)S(1)} fusion(s32[896]{0:T(1024)S(1)} %fusion.11, bf16[896,1024]{1,0:T(8,128)(2,1)S(1)} %bitcast.35, bf16[]{:T(256)} %constant.10.clone.1), kind=kCustom, calls=%fused_computation.12 | custom fusion | bytes 1048578 | tf_op jit(solution)/shard_map/scatter | solution.py:61
  83.4 46.5 %collective-permute-done.3 = bf16[512,1024]{1,0:T(8,128)(2,1)S(1)} collective-permute-done((bf16[512,1024]{1,0:T(8,128)(2,1)S(1)}, bf16[512,1024]{1,0:T(8,128)(2,1)S(1)}, u32[]{:S(2)}, u32[]{:S(2)}) %collective-permute-start.3) | collective-permute-done | bytes 1048608 | tf_op jit(solution)/shard_map/ppermute | solution.py:16
  129.9 1.7 convolution_bitcast_fusion
  131.9 70.7 %collective-permute-done.2 = bf16[512,1024]{1,0:T(8,128)(2,1)S(1)} collective-permute-done((bf16[512,1024]{1,0:T(8,128)(2,1)S(1)}, bf16[512,1024]{1,0:T(8,128)(2,1)S(1)}, u32[]{:S(2)}, u32[]{:S(2)}) %collective-permute-start.2) | collective-permute-done | bytes 1048608 | tf_op jit(solution)/shard_map/ppermute | solution.py:16
  202.6 1.7 convolution_bitcast_fusion.1
  204.5 26.4 %collective-permute-done.1 = bf16[512,1024]{1,0:T(8,128)(2,1)S(1)} collective-permute-done((bf16[512,1024]{1,0:T(8,128)(2,1)S(1)}, bf16[512,1024]{1,0:T(8,128)(2,1)S(1)}, u32[]{:S(2)}, u32[]{:S(2)}) %collective-permute-start.1) | collective-permute-done | bytes 1048608 | tf_op jit(solution)/shard_map/ppermute | solution.py:16
  230.9 1.8 convolution_bitcast_fusion.2
  232.8 26.4 %collective-permute-done = bf16[512,1024]{1,0:T(8,128)(2,1)S(1)} collective-permute-done((bf16[512,1024]{1,0:T(8,128)(2,1)S(1)}, bf16[512,1024]{1,0:T(8,128)(2,1)S(1)}, u32[]{:S(2)}, u32[]{:S(2)}) %collective-permute-start) | collective-permute-done | bytes 1048608 | tf_op jit(solution)/shard_map/ppermute | solution.py:16
  259.2 1.7 convolution_bitcast_fusion.3
  261.0 22.2 %reduce-scatter.5.cloned.1.call-done = f32[512,1,128]{2,0,1:T(8,128)} async-done(((f32[512,1,512]{2,0,1:T(8,128)}), f32[512,1,128]{2,0,1:T(8,128)}) %reduce-scatter.5.cloned.1.call-update) | async-done | bytes 262160 | tf_op jit(solution)/shard_map/reduce_scatter | solution.py:70
  283.2 1.3 maximum_multiply_fusion
  284.5 1.6 copy.19
  (27 shorter events, 1.5 us)
Async XLA Ops:
  11.9 17.4 %all-to-all-start = ((s32[8,1,1]{2,1,0:T(1,128)}), s32[8,1,1]{2,1,0:T(1,128)S(1)}, u32[]{:S(2)}, u32[]{:S(2)}) async-start(s32[8,1,1]{2,1,0:T(1,128)} %copy.16), calls=%async_computation | async-start | bytes 8192 | tf_op jit(solution)/shard_map/all_to_all | solution.py:50
  29.3 48.1 %all-to-all-start.1 = ((bf16[8,112,1024]{2,1,0:T(8,128)(2,1)}), bf16[8,112,1024]{2,1,0:T(8,128)(2,1)S(1)}, u32[]{:S(2)}, u32[]{:S(2)}) async-start(bf16[8,112,1024]{2,1,0:T(8,128)(2,1)} %bitcast.7), calls=%async_computation.1 | async-start | bytes 3670016 | tf_op jit(solution)/shard_map/all_to_all | solution.py:49
  35.3 225.7 %reduce-scatter.11.cloned.1.call-start = ((), (), s32[]{:S(2)}) async-start(), calls=%async_computation.9 | async-start | bytes 1310720 | tf_op jit(solution)/shard_map/reduce_scatter | solution.py:70
  83.3 46.6 %collective-permute-start.3 = (bf16[512,1024]{1,0:T(8,128)(2,1)S(1)}, bf16[512,1024]{1,0:T(8,128)(2,1)S(1)}, u32[]{:S(2)}, u32[]{:S(2)}) collective-permute-start(bf16[512,1024]{1,0:T(8,128)(2,1)S(1)} %scatter_custom_fusion.1), channel_id=1, source_target_pairs={{0,16},{4,20},{8,24},{12,28},{16,0},{20,4},{24,8},{28,12},{1,17},{... | collective-permute-start | bytes 3145736 | tf_op jit(solution)/shard_map/ppermute | solution.py:16
  131.7 129.3 %reduce-scatter.9.cloned.1.call-start = ((), (), s32[]{:S(2)}) async-start(), calls=%async_computation.8 | async-start | bytes 1310720 | tf_op jit(solution)/shard_map/reduce_scatter | solution.py:70
  131.7 70.9 %collective-permute-start.2 = (bf16[512,1024]{1,0:T(8,128)(2,1)S(1)}, bf16[512,1024]{1,0:T(8,128)(2,1)S(1)}, u32[]{:S(2)}, u32[]{:S(2)}) collective-permute-start(bf16[512,1024]{1,0:T(8,128)(2,1)S(1)} %scatter_custom_fusion.1), channel_id=1, source_target_pairs={{0,12},{4,16},{8,20},{12,24},{16,28},{20,0},{24,4},{28,8},{1,13},{... | collective-permute-start | bytes 3145736 | tf_op jit(solution)/shard_map/ppermute | solution.py:16
  204.4 56.6 %reduce-scatter.7.cloned.1.call-start = ((), (), s32[]{:S(2)}) async-start(), calls=%async_computation.7 | async-start | bytes 1310720 | tf_op jit(solution)/shard_map/reduce_scatter | solution.py:70
  204.4 26.5 %collective-permute-start.1 = (bf16[512,1024]{1,0:T(8,128)(2,1)S(1)}, bf16[512,1024]{1,0:T(8,128)(2,1)S(1)}, u32[]{:S(2)}, u32[]{:S(2)}) collective-permute-start(bf16[512,1024]{1,0:T(8,128)(2,1)S(1)} %scatter_custom_fusion.1), channel_id=1, source_target_pairs={{0,8},{4,12},{8,16},{12,20},{16,24},{20,28},{24,0},{28,4},{1,9},{5... | collective-permute-start | bytes 3145736 | tf_op jit(solution)/shard_map/ppermute | solution.py:16
  232.7 50.5 %reduce-scatter.5.cloned.1.call-start = ((), (), s32[]{:S(2)}) async-start(), calls=%async_computation.6 | async-start | bytes 1310720 | tf_op jit(solution)/shard_map/reduce_scatter | solution.py:70
  232.8 26.5 %collective-permute-start = (bf16[512,1024]{1,0:T(8,128)(2,1)S(1)}, bf16[512,1024]{1,0:T(8,128)(2,1)S(1)}, u32[]{:S(2)}, u32[]{:S(2)}) collective-permute-start(bf16[512,1024]{1,0:T(8,128)(2,1)S(1)} %scatter_custom_fusion.1), channel_id=1, source_target_pairs={{0,4},{4,8},{8,12},{12,16},{16,20},{20,24},{24,28},{28,0},{1,5},{5... | collective-permute-start | bytes 3145736 | tf_op jit(solution)/shard_map/ppermute | solution.py:16
Sparse Core Ops, SparseCore 0:
  131.8 24.5 reduce-scatter.10
  204.5 22.1 reduce-scatter.8
  232.8 22.1 reduce-scatter.6
  261.1 22.0 reduce-scatter.4
where the time goes:
time: 293 us
  waiting for transfers between devices  234 us (80%)
  other arithmetic  14.2 us (5%)
  between operations  13.9 us (5%)
  starting transfers between devices  13.8 us (5%)
  local copies, waits for them, and re-layouts  10 us (3%)
  matrix products  6.95 us (2%)
    ppermute x4, waiting for transfers between devices, shifted(): return lax.ppermute(value, axis, pairs)  170 us
    all_to_all x1, waiting for transfers between devices, shards(): lax.all_to_all(outgoing, 'panel', split_axis=0, concat_axis=0, tiled=True)  41.4 us
    reduce_scatter x4, waiting for transfers between devices, shards(): lax.psum_scatter(tile_of(own_panel, partner)[:, None, :], 'feat', scatter...  22.2 us
    scatter x1, other arithmetic, shards(): outgoing = jnp.zeros((panel_total * send_rows, feat_width), jnp.bfloat16)...  8.03 us
    all_to_all x1, starting transfers between devices, shards(): lax.all_to_all(sent_counts, 'panel', split_axis=0, concat_axis=0, tiled=T...  7.28 us
    dot_general x4, matrix products, tile_of(): lax.dot_general(left_rows, partner, (((1,), (1,)), ((), ())), preferred_e...  6.95 us
    all_to_all x1, starting transfers between devices, shards(): lax.all_to_all(outgoing, 'panel', split_axis=0, concat_axis=0, tiled=True)  6 us
    scatter x1, local copies, waits for them, and re-layouts, shards(): own_panel = jnp.zeros((P_SIZE, feat_width), jnp.bfloat16).at[positions.re...  5.94 us
  transfers between devices with their start and end apart: 10, of which 6 were waited for; matrix products, arithmetic and copies ran while one was open for 5% of the time, Pallas kernels for 0%

commit v1 on v0

--- a/solution.py
+++ b/solution.py
@@ -1,13 +1,36 @@
+import functools
 import math
 
 import jax
 import jax.numpy as jnp
 from jax import lax
+from jax.experimental import pallas as pl
+from jax.experimental.pallas import tpu as pltpu
 from jax.sharding import PartitionSpec as P
 
 F = 4096
 P_SIZE = 512
 ROUNDS = 4
+PAIR_ROWS = 128
+NZ, NY, NX, NC = 4, 2, 2, 2
+VMEM_LIMIT = 40 * 1024 * 1024
+BOTH = ("panel", "feat")
+ORDER = ((2, 3, 1, 0), (0, 3, 2, 1), (3, 2, 1, 0), (0, 3, 1, 2))
+CHUNKS = ((0,), (1,), (2, 3))
+FOUND = (
+    {1: {0: "a0", 3: "a1", 2: "a2"}, 2: {3: "a3", 0: "d0", 2: "d2"}, 3: {0: "e0", 3: "e1", 2: "e2"}},
+    {
+        0: {2: "a0", 3: "a1", 1: "a2", 0: "a3"},
+        2: {3: "b0", 2: "b1", 1: "b2", 0: "b3"},
+        3: {0: "c0", 3: "c1", 1: "c2", 2: "c3"},
+    },
+    {
+        3: {0: "a0", 3: "a1", 1: "a2", 2: "a3"},
+        1: {0: "b0", 3: "b1", 2: "b2", 1: "b3"},
+        0: {2: "c0", 3: "c1", 1: "c2", 0: "c3"},
+    },
+    {2: {3: "a0", 2: "a1", 1: "a2"}, 1: {3: "a3", 2: "d0", 1: "d2"}, 0: {2: "e0", 3: "e1", 1: "e2"}},
+)
 
 
 def shifted(value, axis, steps):
@@ -22,7 +45,7 @@
     )
 
 
-def shards(dosage, row_counts, assignment, center, weight):
+def general_shards(dosage, row_counts, assignment, center, weight):
     panel_total = lax.axis_size("panel")
     feat_index = lax.axis_index("feat")
     capacity = dosage.shape[0]
@@ -79,7 +102,370 @@
     return kinship
 
 
+def hop(value, move):
+    pairs = []
+    for z in range(NZ):
+        for y in range(NY):
+            for x in range(NX):
+                for c in range(NC):
+                    to = move(z, y, x, c)
+                    if to is not None:
+                        tz, ty, tx, tc = to
+                        pairs.append((((z * 2 + y) * 2 + x) * 2 + c, ((tz * 2 + ty) * 2 + tx) * 2 + tc))
+    return lax.ppermute(value, BOTH, pairs)
+
+
+def to_y(value):
+    return hop(value, lambda z, y, x, c: (z, 1 - y, x, c))
+
+
+def to_x(value):
+    return hop(value, lambda z, y, x, c: (z, y, 1 - x, c))
+
+
+def to_diagonal(value):
+    return hop(value, lambda z, y, x, c: (z, 1 - y, 1 - x, c))
+
+
+def to_core(value):
+    return hop(value, lambda z, y, x, c: (z, y, x, 1 - c))
+
+
+def z_ends(value):
+    return hop(value, lambda z, y, x, c: (z ^ 1, y, x, c))
+
+
+def z_middle(value):
+    return hop(value, lambda z, y, x, c: (3 - z, y, x, c) if z in (1, 2) else None)
+
+
+def place():
+    panel, feat = lax.axis_index("panel"), lax.axis_index("feat")
+    return panel // NY, panel % NY, feat // NC, feat % NC
+
+
+def call(kernel, out_shape, in_specs, out_specs, cost, scratch=()):
+    return pl.pallas_call(
+        kernel,
+        name=kernel.func.__name__,
+        out_shape=out_shape,
+        in_specs=in_specs,
+        out_specs=out_specs,
+        scratch_shapes=scratch,
+        compiler_params=pltpu.CompilerParams(vmem_limit_bytes=VMEM_LIMIT),
+        cost_estimate=pl.CostEstimate(flops=cost[0], bytes_accessed=cost[1], transcendentals=0),
+    )
+
+
+IN_VMEM = pl.BlockSpec(memory_space=pltpu.VMEM)
+IN_SMEM = pl.BlockSpec(memory_space=pltpu.SMEM)
+ANYWHERE = pl.BlockSpec(memory_space=pl.ANY)
+IN_HBM = pl.BlockSpec(memory_space=pltpu.HBM)
+
+
+def bf16(*shape):
+    return jax.ShapeDtypeStruct(shape, jnp.bfloat16)
+
+
+def group_at(step):
+    z, _, _, _ = place()
+    group = jnp.int32(ORDER[0][step])
+    for plane in range(1, NZ):
+        group = jnp.where(z == plane, ORDER[plane][step], group)
+    return group
+
+
+def picks(slot, slots, step):
+    group_rows = 2 * slots
+    row = lax.broadcasted_iota(jnp.int32, (group_rows, slot.shape[1]), 0) + group_at(step) * group_rows
+    return jnp.where(row == slot, 1.0, 0.0).astype(jnp.bfloat16)
+
+
+def picked(pick, rows):
+    return jnp.dot(pick, rows, preferred_element_type=jnp.float32).astype(jnp.bfloat16)
+
+
+def columns_of_half(width, part):
+    half = width // NY
+    feat = lax.axis_index("feat")
+    return (
+        pl.ds(pl.multiple_of(part * half, half), half),
+        pl.ds(pl.multiple_of(feat * width + part * half, half), half),
+    )
+
+
+def standard(dosage_ref, center_ref, weight_ref, part):
+    columns, features = columns_of_half(dosage_ref.shape[1], part)
+    rows = dosage_ref[:, columns].astype(jnp.float32)
+    return ((rows - center_ref[:, features]) * weight_ref[:, features]).astype(jnp.bfloat16)
+
+
+def first_kernel(
+    slots, count_ref, assign_ref, center_ref, weight_ref, dosage_ref, slot_ref, counts_ref, rows_ref, away_ref
+):
+    capacity = dosage_ref.shape[0]
+    _, y, _, _ = place()
+    panels = capacity // slots
+    assign = assign_ref[...]
+    lane = lax.broadcasted_iota(jnp.int32, (panels, capacity), 1)
+    panel_id = lax.broadcasted_iota(jnp.int32, (panels, capacity), 0)
+    live = lane < count_ref[0]
+    member = (panel_id == assign) & live
+    running = member.astype(jnp.int32)
+    step = 1
+    while step < capacity:
+        running = running + jnp.where(lane >= step, pltpu.roll(running, step, 1), 0)
+        step *= 2
+    counts_ref[...] = jnp.broadcast_to(running[:, capacity - 1 :], counts_ref.shape)
+    rank = jnp.sum(jnp.where(member, running - 1, 0), axis=0, keepdims=True)
+    slot = jnp.where(live[:1], assign * slots + rank, -1)
+    slot_ref[...] = slot
+    rows_ref[...] = standard(dosage_ref, center_ref, weight_ref, 1 - y)
+    at = 0
+    for step in CHUNKS[0]:
+        away_ref[pl.ds(at, 2 * slots), :] = picked(picks(slot, slots, step), rows_ref[...])
+        at += 2 * slots
+
+
+def rest_kernel(slots, slot_ref, rows_ref, center_ref, weight_ref, dosage_ref, own_ref, *away_refs):
+    _, y, _, _ = place()
+    group_rows = 2 * slots
+    slot = slot_ref[...]
+    pick = {}
+    for chunk, away_ref in zip(CHUNKS[1:], away_refs):
+        for k, step in enumerate(chunk):
+            pick[step] = picks(slot, slots, step)
+            away_ref[pl.ds(k * group_rows, group_rows), :] = picked(pick[step], rows_ref[...])
+    stay = standard(dosage_ref, center_ref, weight_ref, y)
+    for step in range(NZ):
+        rows = pick[step] if step in pick else picks(slot, slots, step)
+        own_ref[pl.ds(step * group_rows, group_rows), :] = picked(rows, stay)
+
+
+def merge_kernel(slots, chunk, counts_ref, own_ref, other_ref, *out_refs):
+    _, y, _, _ = place()
+    row = lax.broadcasted_iota(jnp.int32, (PAIR_ROWS, slots), 0)
+    slot = lax.broadcasted_iota(jnp.int32, (PAIR_ROWS, slots), 1)
+    for at, (step, out_ref) in enumerate(zip(chunk, out_refs)):
+        group = group_at(step)
+        for k in range(2):
+            n_own = counts_ref[group * 2 + k, 0]
+            n_other = PAIR_ROWS - n_own
+            own_at = jnp.where(y == 0, 0, n_other)
+            other_at = jnp.where(y == 0, n_own, 0)
+            pick_own = jnp.where((row == slot + own_at) & (slot < n_own), 1.0, 0.0).astype(jnp.bfloat16)
+            pick_other = jnp.where((row == slot + other_at) & (slot < n_other), 1.0, 0.0).astype(jnp.bfloat16)
+            merged = jnp.dot(
+                pick_own, own_ref[pl.ds((step * 2 + k) * slots, slots), :], preferred_element_type=jnp.float32
+            ) + jnp.dot(
+                pick_other, other_ref[pl.ds((at * 2 + k) * slots, slots), :], preferred_element_type=jnp.float32
+            )
+            out_ref[pl.ds(k * PAIR_ROWS, PAIR_ROWS), :] = merged.astype(jnp.bfloat16)
+
+
+def collect_kernel(names, whole, split, *refs):
+    pieces = dict(zip(names, refs))
+    send_ref, keep_ref, sems = refs[len(names) :]
+    z, _, _, c = place()
+    for zz in range(NZ):
+        for cc in range(NC):
+
+            @pl.when((z == zz) & (c == cc))
+            def _(zz=zz, cc=cc):
+                copies = []
+                sent = kept = 0
+                for r in whole + split:
+                    g = (zz - r) % NZ
+                    for s in range(NZ):
+                        source = pieces["o%d" % ORDER[zz].index(g) if s == zz else FOUND[zz][s][g]]
+                        if r in split and s % NC == cc:
+                            copies.append((source, keep_ref.at[kept]))
+                            kept += 1
+                        else:
+                            copies.append((source, send_ref.at[sent]))
+                            sent += 1
+                started = []
+                for i, (source, target) in enumerate(copies):
+                    copy = pltpu.make_async_copy(source, target, sems.at[i])
+                    copy.start()
+                    started.append(copy)
+                for copy in started:
+                    copy.wait()
+
+
+def tile_kernel(tiles, n_kept, *refs):
+    own_ref, own_far_ref = refs[:2]
+    kept_refs = refs[2 : 2 + n_kept]
+    far_refs = refs[2 + n_kept : 2 + 2 * n_kept]
+    mine_ref, x_ref, y_ref, d_ref = refs[2 + 2 * n_kept :]
+    _, y, x, c = place()
+    depth = own_ref.shape[2]
+    nt = (((1,), (1,)), ((), ()))
+
+    def rows_of(ref, p):
+        return ref[0:NZ, pl.ds(p * PAIR_ROWS, PAIR_ROWS), :].reshape(P_SIZE, depth)
+
+    def columns_of(distance, q, part, near):
+        rows = pl.ds(q * PAIR_ROWS, PAIR_ROWS)
+        if distance == 0:
+            return (own_ref if near else own_far_ref)[2 * part + c, rows, :]
+        if near:
+            return kept_refs[distance - 1][part, rows, :]
+        ref = far_refs[distance - 1]
+        first = ref.shape[0] - 2
+        return ref[first + part, rows, :]
+
+    for p in range(2):
+        left, left_far = rows_of(own_ref, p), rows_of(own_far_ref, p)
+        for part in range(2):
+            near = jnp.concatenate([columns_of(d, q, part, True) for d, q in tiles[p]], axis=0)
+            far = jnp.concatenate([columns_of(d, q, part, False) for d, q in tiles[p]], axis=0)
+            total = lax.dot_general(left, near, nt, preferred_element_type=jnp.float32) + lax.dot_general(
+                left_far, far, nt, preferred_element_type=jnp.float32
+            )
+
+            @pl.when((y == p) & (x == part))
+            def _(total=total):
+                mine_ref[...] = total
+
+            @pl.when((y == p) & (x != part))
+            def _(total=total):
+                x_ref[...] = total.astype(jnp.bfloat16)
+
+            @pl.when((y != p) & (x == part))
+            def _(total=total):
+                y_ref[...] = total.astype(jnp.bfloat16)
+
+            @pl.when((y != p) & (x != part))
+            def _(total=total):
+                d_ref[...] = total.astype(jnp.bfloat16)
+
+
+def plane_tiles(tiles, own, own_far, kept, far):
+    columns = len(tiles[0]) * PAIR_ROWS
+    part = bf16(P_SIZE, columns)
+    mine, x_part, y_part, d_part = call(
+        functools.partial(tile_kernel, tiles, len(kept)),
+        (jax.ShapeDtypeStruct((P_SIZE, columns), jnp.float32), part, part, part),
+        [IN_VMEM] * (2 + 2 * len(kept)),
+        (IN_VMEM,) * 4,
+        (2 * 4 * P_SIZE * columns * 2 * own.shape[2], 8 * 1024 * 1024),
+    )(own, own_far, *kept, *far)
+    return mine, to_y(y_part), to_diagonal(d_part), to_x(x_part)
+
+
+def plane_shards(dosage, row_counts, assignment, center, weight):
+    capacity, width = dosage.shape
+    half = width // NY
+    panels = NZ * NY
+    slots = capacity // panels
+    group_slots = 2 * slots
+    group_rows = 2 * PAIR_ROWS
+
+    center, weight = center.reshape(1, -1), weight.reshape(1, -1)
+    chunk_rows = [len(chunk) * group_slots for chunk in CHUNKS]
+    slot, counts, rows, away = call(
+        functools.partial(first_kernel, slots),
+        (
+            jax.ShapeDtypeStruct((1, capacity), jnp.int32),
+            jax.ShapeDtypeStruct((panels, 128), jnp.int32),
+            bf16(capacity, half),
+            bf16(chunk_rows[0], half),
+        ),
+        [IN_SMEM] + [IN_VMEM] * 4,
+        (IN_VMEM,) * 4,
+        (2 * chunk_rows[0] * capacity * half, 3 * capacity * width),
+    )(row_counts, assignment.reshape(1, capacity), center, weight, dosage)
+    with jax.named_scope("y0"):
+        came = [to_y(away)]
+    own, *later = call(
+        functools.partial(rest_kernel, slots),
+        (bf16(capacity, half),) + tuple(bf16(n, half) for n in chunk_rows[1:]),
+        [IN_VMEM] * 5,
+        (IN_VMEM,) * len(CHUNKS),
+        (2 * capacity * capacity * width, 3 * capacity * width),
+    )(slot, rows, center, weight, dosage)
+    for k, away in enumerate(later):
+        with jax.named_scope("y%d" % (k + 1)):
+            if k >= 1:
+                away, _ = lax.optimization_barrier((away, came[k - 1]))
+            came.append(to_y(away))
+    pieces = {}
+    for chunk, other in zip(CHUNKS, came):
+        merged = call(
+            functools.partial(merge_kernel, slots, chunk),
+            (bf16(group_rows, half),) * len(chunk),
+            [IN_SMEM, IN_VMEM, IN_VMEM],
+            (IN_VMEM,) * len(chunk),
+            (2 * len(chunk) * group_rows * group_slots * half, 4 * group_rows * half * 2),
+        )(counts, own, other)
+        for step, piece in zip(chunk, merged):
+            pieces["o%d" % step] = piece
+
+    z = lax.axis_index("panel") // NY
+
+    def either(first, second, planes):
+        return jnp.where((z == planes[0]) | (z == planes[1]), pieces[first], pieces[second])
+
+    def ends(name, value):
+        with jax.named_scope(name):
+            pieces[name] = z_ends(value)
+
+    def middle(name, value):
+        with jax.named_scope(name):
+            pieces[name] = z_middle(value)
+
+    for k in range(NZ - 1):
+        ends("a%d" % k, pieces["o%d" % k])
+        middle("b%d" % k, pieces["o%d" % k])
+    pieces["f"] = either("b0", "b1", (0, 1))
+    ends("a3", either("o3", "f", (0, 3)))
+    middle("b3", pieces["o3"])
+    ends("d0", either("b3", "b2", (0, 1)))
+    for k in range(NZ):
+        middle("c%d" % k, pieces["a%d" % k])
+    ends("e0", pieces["c0"])
+    ends("e1", pieces["c1"])
+    ends("d2", either("b1", "b3", (0, 1)))
+    ends("e2", either("c3", "c2", (0, 1)))
+
+    def collect(whole, split):
+        sent, kept = 4 * len(whole) + 2 * len(split), 2 * len(split)
+        names = set()
+        for z in range(NZ):
+            for r in whole + split:
+                g = (z - r) % NZ
+                names.add("o%d" % ORDER[z].index(g))
+                names.update(FOUND[z][s][g] for s in range(NZ) if s != z)
+        names = sorted(names)
+        return call(
+            functools.partial(collect_kernel, names, whole, split),
+            (bf16(sent, group_rows, half), bf16(kept, group_rows, half)),
+            [ANYWHERE] * len(names),
+            (ANYWHERE, ANYWHERE),
+            (0, 4 * (sent + kept) * group_rows * half),
+            (pltpu.SemaphoreType.DMA((sent + kept,)),),
+        )(*[pieces[name] for name in names])
+
+    sent1, kept1 = collect((0,), (1,))
+    far1 = to_core(sent1)
+    first = plane_tiles((((1, 1), (1, 0)), ((0, 0), (1, 1))), sent1, far1, (kept1,), (far1,))
+    sent2, kept2 = collect((), (2,))
+    far2 = to_core(sent2)
+    second = plane_tiles((((2, 1), (2, 0)), ((1, 0), (2, 1))), sent1, far1, (kept1, kept2), (far1, far2))
+
+    def total(parts):
+        mine, *others = parts
+        for other in others:
+            mine = mine + other.astype(jnp.float32)
+        return mine.reshape(P_SIZE, 2, PAIR_ROWS)
+
+    return jnp.concatenate([total(first), total(second)], axis=1) * (1.0 / math.sqrt(F))
+
+
 def solution(mesh):
     in_specs = (P("panel", "feat"), P("panel"), P("panel"), P(), P())
     out_specs = P("panel", None, "feat")
+    planes = mesh.shape["panel"] == NZ * NY and mesh.shape["feat"] == NX * NC
+    shards = plane_shards if planes else general_shards
     return jax.shard_map(shards, mesh=mesh, in_specs=in_specs, out_specs=out_specs, check_vma=False)

time: 293 us -> 123 us (0.42)
  waiting for transfers between devices: 234 us -> 38.7 us
  starting transfers between devices: 13.8 us -> 64.8 us
  between operations: 13.9 us -> 0.91 us
  other arithmetic: 14.2 us -> 1.82 us
  Pallas kernels: 0 us -> 12 us
  matrix products: 6.95 us -> 0 us
  local copies, waits for them, and re-layouts: 10 us -> 4.17 us
    ppermute x4 -> x28, waiting for transfers between devices: 170 us -> 38.7 us  [hop(): return lax.ppermute(value, BOTH, pairs)]
    ppermute x4 -> x28, starting transfers between devices: 0.41 us -> 64.8 us  [hop(): return lax.ppermute(value, BOTH, pairs)]
    all_to_all x2 -> x0, waiting for transfers between devices: 41.4 us -> none  [the longest x1 41.4 us: shards(): lax.all_to_all(outgoing, 'panel', split_axis=0, concat_axis=0, tiled=True)]
    reduce_scatter x4 -> x0, waiting for transfers between devices: 22.2 us -> none  [shards(): lax.psum_scatter(tile_of(own_panel, partner)[:, None, :], 'feat', scatter...]
    all_to_all x2 -> x0, starting transfers between devices: 13.3 us -> none  [the longest x1 7.28 us: shards(): lax.all_to_all(sent_counts, 'panel', split_axis=0, concat_axis=0, tiled=T...]
    pallas_call x0 -> x9, Pallas kernels: none -> 12 us  [the longest x2 5.96 us: plane_tiles(): call(functools.partial(tile_kernel, tiles, len(kept)), (jax.ShapeDtypeStr...]
    scatter x1 -> x0, other arithmetic: 8.03 us -> none  [shards(): outgoing = jnp.zeros((panel_total * send_rows, feat_width), jnp.bfloat16)...]
    dot_general x4 -> x0, matrix products: 6.95 us -> none  [tile_of(): lax.dot_general(left_rows, partner, (((1,), (1,)), ((), ())), preferred_e...]
  transfers between devices with their start and end apart: 10 -> 28, of which waited for: 6 -> 11; matrix products, arithmetic and copies ran while one was open for 5% -> 0% of each run, Pallas kernels for 0% -> 6%
where the time goes in v1:
time: 123 us; the launch traced here: 122 us
  starting transfers between devices  64.8 us (53%)
  waiting for transfers between devices  38.7 us (31%)
  Pallas kernels  12 us (10%)
  local copies, waits for them, and re-layouts  4.17 us (3%)
  other arithmetic  1.82 us (1%)
    ppermute x28, starting transfers between devices, hop(): return lax.ppermute(value, BOTH, pairs)  64.8 us
    ppermute x28, waiting for transfers between devices, hop(): return lax.ppermute(value, BOTH, pairs)  38.7 us
    pallas_call x2, Pallas kernels, plane_tiles(): call(functools.partial(tile_kernel, tiles, len(kept)), (jax.ShapeDtypeStr...  5.96 us
    unnamed x10, local copies, waits for them, and re-layouts  2.94 us
    pallas_call x3, Pallas kernels, plane_shards(): call(functools.partial(merge_kernel, slots, chunk), (bf16(group_rows, hal...  2.79 us
  transfers between devices with their start and end apart: 28, of which 11 were waited for; matrix products, arithmetic and copies ran while one was open for 0% of the time, Pallas kernels for 6%

profile of v1, /device:TPU:0, one launch (start us, length us, event | category | flops | bytes accessed | tf_op | source)
XLA Modules:
  0.0 122.4 jit_solution(12505100864753071355)
XLA Ops:
  5.2 3.0 %collective-permute-start = (bf16[224,512]{1,0:T(8,128)(2,1)S(1)}, bf16[224,512]{1,0:T(8,128)(2,1)S(1)}, u32[]{:S(2)}, u32[]{:S(2)}) collective-permute-start(bf16[224,512]{1,0:T(8,128)(2,1)S(1)} %get-tuple-element.31), channel_id=1, source_target_pairs={{0,4},{1,5},{2,6},{3,7},{4,0},{5,1},{6,2},{7,3},{8,12},{9,13},{10,... | collective-permute-start | bytes 688136 | tf_op jit(solution)/shard_map/y0/ppermute | solution.py:115
  8.3 1.9 %rest_kernel.1 = (bf16[896,512]{1,0:T(8,128)(2,1)S(1)}, bf16[224,512]{1,0:T(8,128)(2,1)S(1)}, bf16[448,512]{1,0:T(8,128)(2,1)S(1)}) custom-call(s32[1,896]{1,0:T(1,128)S(1)} %get-tuple-element.28.slot_ref, bf16[896,512]{1,0:T(8,128)(2,1)S(1)} %get-tuple-element.29.rows_ref, f32[1,4096]{1,0:T(1,128)S(1)} %bitcast.3, f32[1,4096]{1,0:T(1,128)S(1)} %bitcast.5, ...), custom_call_target="tpu_custom_call" | custom-call | flops 1644167168 | bytes 2752512 | tf_op jit(solution)/shard_map/rest_kernel/pallas_call | solution.py:381
  10.7 4.0 %collective-permute-done.other_ref = bf16[224,512]{1,0:T(8,128)(2,1)S(1)} collective-permute-done((bf16[224,512]{1,0:T(8,128)(2,1)S(1)}, bf16[224,512]{1,0:T(8,128)(2,1)S(1)}, u32[]{:S(2)}, u32[]{:S(2)}) %collective-permute-start) | collective-permute-done | bytes 229408 | tf_op jit(solution)/shard_map/y0/ppermute | solution.py:115
  14.7 2.1 %collective-permute-start.4 = (bf16[448,512]{1,0:T(8,128)(2,1)S(1)}, bf16[448,512]{1,0:T(8,128)(2,1)S(1)}, u32[]{:S(2)}, u32[]{:S(2)}) collective-permute-start(bf16[448,512]{1,0:T(8,128)(2,1)S(1)} %get-tuple-element.34), channel_id=1, source_target_pairs={{0,4},{1,5},{2,6},{3,7},{4,0},{5,1},{6,2},{7,3},{8,12},{9,13},{10,... | collective-permute-start | bytes 1376264 | tf_op jit(solution)/shard_map/y2/ppermute | solution.py:115
  17.6 1.6 %collective-permute-start.1 = (bf16[256,512]{1,0:T(8,128)(2,1)S(1)}, bf16[256,512]{1,0:T(8,128)(2,1)S(1)}, u32[]{:S(2)}, u32[]{:S(2)}) collective-permute-start(bf16[256,512]{1,0:T(8,128)(2,1)S(1)} %merge_kernel.3.refs_11_.refs_8_), channel_id=1, source_target_pairs={{0,8},{1,9},{2,10},{3,11},{4,12},{5,13},{6,14},{7,15},{8,0},{9,1},... | collective-permute-start | bytes 786440 | tf_op jit(solution)/shard_map/a0/ppermute | solution.py:115
  20.5 2.2 %collective-permute-start.3 = (bf16[256,512]{1,0:T(8,128)(2,1)S(1)}, bf16[256,512]{1,0:T(8,128)(2,1)S(1)}, u32[]{:S(2)}, u32[]{:S(2)}) collective-permute-start(bf16[256,512]{1,0:T(8,128)(2,1)S(1)} %merge_kernel.4.refs_12_.refs_9_), channel_id=1, source_target_pairs={{0,8},{1,9},{2,10},{3,11},{4,12},{5,13},{6,14},{7,15},{8,0},{9,1},... | collective-permute-start | bytes 786440 | tf_op jit(solution)/shard_map/a1/ppermute | solution.py:115
  24.0 2.5 %collective-permute-done.1.refs_0_ = bf16[256,512]{1,0:T(8,128)(2,1)S(1)} collective-permute-done((bf16[256,512]{1,0:T(8,128)(2,1)S(1)}, bf16[256,512]{1,0:T(8,128)(2,1)S(1)}, u32[]{:S(2)}, u32[]{:S(2)}) %collective-permute-start.1) | collective-permute-done | bytes 262176 | tf_op jit(solution)/shard_map/a0/ppermute | solution.py:115
  27.2 2.5 %collective-permute-done.3.refs_1_ = bf16[256,512]{1,0:T(8,128)(2,1)S(1)} collective-permute-done((bf16[256,512]{1,0:T(8,128)(2,1)S(1)}, bf16[256,512]{1,0:T(8,128)(2,1)S(1)}, u32[]{:S(2)}, u32[]{:S(2)}) %collective-permute-start.3) | collective-permute-done | bytes 262176 | tf_op jit(solution)/shard_map/a1/ppermute | solution.py:115
  32.8 9.7 %collective-permute-start.5 = (bf16[256,512]{1,0:T(8,128)(2,1)S(1)}, bf16[256,512]{1,0:T(8,128)(2,1)S(1)}, u32[]{:S(2)}, u32[]{:S(2)}) collective-permute-start(bf16[256,512]{1,0:T(8,128)(2,1)S(1)} %get-tuple-element.35.refs_13_.refs_10_), channel_id=1, source_target_pairs={{0,8},{1,9},{2,10},{3,11},{4,12},{5,13},{6,14},{7,15},{8,0},{9,1},... | collective-permute-start | bytes 786440 | tf_op jit(solution)/shard_map/a2/ppermute | solution.py:115
  42.6 3.3 %collective-permute-start.14 = (bf16[256,512]{1,0:T(8,128)(2,1)S(1)}, bf16[256,512]{1,0:T(8,128)(2,1)S(1)}, u32[]{:S(2)}, u32[]{:S(2)}) collective-permute-start(bf16[256,512]{1,0:T(8,128)(2,1)S(1)} %collective-permute-done.11.refs_6_), channel_id=1, source_target_pairs={{0,8},{1,9},{2,10},{3,11},{4,12},{5,13},{6,14},{7,15},{8,0},{9,1},... | collective-permute-start | bytes 786440 | tf_op jit(solution)/shard_map/e0/ppermute | solution.py:115
  45.9 5.6 %collective-permute-start.16 = (bf16[256,512]{1,0:T(8,128)(2,1)S(1)}, bf16[256,512]{1,0:T(8,128)(2,1)S(1)}, u32[]{:S(2)}, u32[]{:S(2)}) collective-permute-start(bf16[256,512]{1,0:T(8,128)(2,1)S(1)} %collective-permute-done.15.refs_4_), channel_id=1, source_target_pairs={{0,8},{1,9},{2,10},{3,11},{4,12},{5,13},{6,14},{7,15},{8,0},{9,1},... | collective-permute-start | bytes 786440 | tf_op jit(solution)/shard_map/e1/ppermute | solution.py:115
  51.6 8.7 %collective-permute-start.13 = (bf16[256,512]{1,0:T(8,128)(2,1)S(1)}, bf16[256,512]{1,0:T(8,128)(2,1)S(1)}, u32[]{:S(2)}, u32[]{:S(2)}) collective-permute-start(bf16[256,512]{1,0:T(8,128)(2,1)S(1)} %get-tuple-element.50), channel_id=1, source_target_pairs={{0,8},{1,9},{2,10},{3,11},{4,12},{5,13},{6,14},{7,15},{8,0},{9,1},... | collective-permute-start | bytes 786440 | tf_op jit(solution)/shard_map/d0/ppermute | solution.py:115
  61.0 2.7 %collective-permute-start.8 = (bf16[256,512]{1,0:T(8,128)(2,1)S(1)}, bf16[256,512]{1,0:T(8,128)(2,1)S(1)}, u32[]{:S(2)}, u32[]{:S(2)}) collective-permute-start(bf16[256,512]{1,0:T(8,128)(2,1)S(1)} %get-tuple-element.51), channel_id=1, source_target_pairs={{0,8},{1,9},{2,10},{3,11},{4,12},{5,13},{6,14},{7,15},{8,0},{9,1},... | collective-permute-start | bytes 786440 | tf_op jit(solution)/shard_map/a3/ppermute | solution.py:115
  63.7 3.4 %collective-permute-done.13.refs_8_ = bf16[256,512]{1,0:T(8,128)(2,1)S(1)} collective-permute-done((bf16[256,512]{1,0:T(8,128)(2,1)S(1)}, bf16[256,512]{1,0:T(8,128)(2,1)S(1)}, u32[]{:S(2)}, u32[]{:S(2)}) %collective-permute-start.13) | collective-permute-done | bytes 262176 | tf_op jit(solution)/shard_map/d0/ppermute | solution.py:115
  67.1 2.8 %collective-permute-done.8.refs_3_ = bf16[256,512]{1,0:T(8,128)(2,1)S(1)} collective-permute-done((bf16[256,512]{1,0:T(8,128)(2,1)S(1)}, bf16[256,512]{1,0:T(8,128)(2,1)S(1)}, u32[]{:S(2)}, u32[]{:S(2)}) %collective-permute-start.8) | collective-permute-done | bytes 262176 | tf_op jit(solution)/shard_map/a3/ppermute | solution.py:115
  71.0 4.0 %collective-permute-start.22 = (bf16[256,512]{1,0:T(8,128)(2,1)S(1)}, bf16[256,512]{1,0:T(8,128)(2,1)S(1)}, u32[]{:S(2)}, u32[]{:S(2)}) collective-permute-start(bf16[256,512]{1,0:T(8,128)(2,1)S(1)} %get-tuple-element.49), channel_id=1, source_target_pairs={{0,8},{1,9},{2,10},{3,11},{4,12},{5,13},{6,14},{7,15},{8,0},{9,1},... | collective-permute-start | bytes 786440 | tf_op jit(solution)/shard_map/d2/ppermute | solution.py:115
  74.9 7.7 %collective-permute-start.23 = (bf16[256,512]{1,0:T(8,128)(2,1)S(1)}, bf16[256,512]{1,0:T(8,128)(2,1)S(1)}, u32[]{:S(2)}, u32[]{:S(2)}) collective-permute-start(bf16[256,512]{1,0:T(8,128)(2,1)S(1)} %broadcast_select_fusion), channel_id=1, source_target_pairs={{0,8},{1,9},{2,10},{3,11},{4,12},{5,13},{6,14},{7,15},{8,0},{9,1},... | collective-permute-start | bytes 786440 | tf_op jit(solution)/shard_map/e2/ppermute | solution.py:115
  82.7 6.2 %collective-permute-done.23.refs_7_ = bf16[256,512]{1,0:T(8,128)(2,1)S(1)} collective-permute-done((bf16[256,512]{1,0:T(8,128)(2,1)S(1)}, bf16[256,512]{1,0:T(8,128)(2,1)S(1)}, u32[]{:S(2)}, u32[]{:S(2)}) %collective-permute-start.23) | collective-permute-done | bytes 262176 | tf_op jit(solution)/shard_map/e2/ppermute | solution.py:115
  89.1 1.9 %collective-permute-done.24.refs_5_ = bf16[2,256,512]{2,1,0:T(8,128)(2,1)S(1)} collective-permute-done((bf16[2,256,512]{2,1,0:T(8,128)(2,1)S(1)}, bf16[2,256,512]{2,1,0:T(8,128)(2,1)S(1)}, u32[]{:S(2)}, u32[]{:S(2)}) %collective-permute-start.24) | collective-permute-done | bytes 524320 | tf_op jit(solution)/shard_map/ppermute | solution.py:115
  91.0 3.0 %tile_kernel.3 = (f32[512,256]{1,0:T(8,128)S(1)}, bf16[512,256]{1,0:T(8,128)(2,1)S(1)}, bf16[512,256]{1,0:T(8,128)(2,1)S(1)}, bf16[512,256]{1,0:T(8,128)(2,1)S(1)}) custom-call(bf16[6,256,512]{2,1,0:T(8,128)(2,1)S(1)} %get-tuple-element.37.refs_0_, bf16[6,256,512]{2,1,0:T(8,128)(2,1)S(1)} %collective-permute-done.17.refs_1_.refs_3_.refs_4_, ...), custom_call_target="tpu_custom_call" | custom-call | flops 1073741824 | bytes 8388608 | tf_op jit(solution)/shard_map/tile_kernel/pallas_call | solution.py:347
  94.0 1.6 %collective-permute-start.25 = (bf16[512,256]{1,0:T(8,128)(2,1)S(1)}, bf16[512,256]{1,0:T(8,128)(2,1)S(1)}, u32[]{:S(2)}, u32[]{:S(2)}) collective-permute-start(bf16[512,256]{1,0:T(8,128)(2,1)S(1)} %get-tuple-element.46), channel_id=1, source_target_pairs={{0,4},{1,5},{2,6},{3,7},{4,0},{5,1},{6,2},{7,3},{8,12},{9,13},{10,... | collective-permute-start | bytes 786440 | tf_op jit(solution)/shard_map/ppermute | solution.py:115
  97.5 3.0 %tile_kernel.2 = (f32[512,256]{1,0:T(8,128)S(1)}, bf16[512,256]{1,0:T(8,128)(2,1)S(1)}, bf16[512,256]{1,0:T(8,128)(2,1)S(1)}, bf16[512,256]{1,0:T(8,128)(2,1)S(1)}) custom-call(bf16[6,256,512]{2,1,0:T(8,128)(2,1)S(1)} %get-tuple-element.37.refs_0_, bf16[6,256,512]{2,1,0:T(8,128)(2,1)S(1)} %collective-permute-done.17.refs_1_.refs_3_.refs_4_, ...), custom_call_target="tpu_custom_call" | custom-call | flops 1073741824 | bytes 8388608 | tf_op jit(solution)/shard_map/tile_kernel/pallas_call | solution.py:347
  103.6 5.3 %collective-permute-done.25 = bf16[512,256]{1,0:T(8,128)(2,1)S(1)} collective-permute-done((bf16[512,256]{1,0:T(8,128)(2,1)S(1)}, bf16[512,256]{1,0:T(8,128)(2,1)S(1)}, u32[]{:S(2)}, u32[]{:S(2)}) %collective-permute-start.25) | collective-permute-done | bytes 262176 | tf_op jit(solution)/shard_map/ppermute | solution.py:115
  110.7 8.5 %collective-permute-done.18 = bf16[512,256]{1,0:T(8,128)(2,1)S(1)} collective-permute-done((bf16[512,256]{1,0:T(8,128)(2,1)S(1)}, bf16[512,256]{1,0:T(8,128)(2,1)S(1)}, u32[]{:S(2)}, u32[]{:S(2)}) %collective-permute-start.18) | collective-permute-done | bytes 262176 | tf_op jit(solution)/shard_map/ppermute | solution.py:115
  (59 shorter events, 24.3 us)
Async XLA Ops:
  5.2 9.5 %collective-permute-start = (bf16[224,512]{1,0:T(8,128)(2,1)S(1)}, bf16[224,512]{1,0:T(8,128)(2,1)S(1)}, u32[]{:S(2)}, u32[]{:S(2)}) collective-permute-start(bf16[224,512]{1,0:T(8,128)(2,1)S(1)} %get-tuple-element.31), channel_id=1, source_target_pairs={{0,4},{1,5},{2,6},{3,7},{4,0},{5,1},{6,2},{7,3},{8,12},{9,13},{10,... | collective-permute-start | bytes 688136 | tf_op jit(solution)/shard_map/y0/ppermute | solution.py:115
  10.1 9.5 %collective-permute-start.2 = (bf16[224,512]{1,0:T(8,128)(2,1)S(1)}, bf16[224,512]{1,0:T(8,128)(2,1)S(1)}, u32[]{:S(2)}, u32[]{:S(2)}) collective-permute-start(bf16[224,512]{1,0:T(8,128)(2,1)S(1)} %get-tuple-element.32), channel_id=1, source_target_pairs={{0,4},{1,5},{2,6},{3,7},{4,0},{5,1},{6,2},{7,3},{8,12},{9,13},{10,... | collective-permute-start | bytes 688136 | tf_op jit(solution)/shard_map/y1/ppermute | solution.py:115
  14.7 15.7 %collective-permute-start.4 = (bf16[448,512]{1,0:T(8,128)(2,1)S(1)}, bf16[448,512]{1,0:T(8,128)(2,1)S(1)}, u32[]{:S(2)}, u32[]{:S(2)}) collective-permute-start(bf16[448,512]{1,0:T(8,128)(2,1)S(1)} %get-tuple-element.34), channel_id=1, source_target_pairs={{0,4},{1,5},{2,6},{3,7},{4,0},{5,1},{6,2},{7,3},{8,12},{9,13},{10,... | collective-permute-start | bytes 1376264 | tf_op jit(solution)/shard_map/y2/ppermute | solution.py:115
  20.5 9.2 %collective-permute-start.3 = (bf16[256,512]{1,0:T(8,128)(2,1)S(1)}, bf16[256,512]{1,0:T(8,128)(2,1)S(1)}, u32[]{:S(2)}, u32[]{:S(2)}) collective-permute-start(bf16[256,512]{1,0:T(8,128)(2,1)S(1)} %merge_kernel.4.refs_12_.refs_9_), channel_id=1, source_target_pairs={{0,8},{1,9},{2,10},{3,11},{4,12},{5,13},{6,14},{7,15},{8,0},{9,1},... | collective-permute-start | bytes 786440 | tf_op jit(solution)/shard_map/a1/ppermute | solution.py:115
  22.7 9.4 %collective-permute-start.6 = (bf16[256,512]{1,0:T(8,128)(2,1)S(1)}, bf16[256,512]{1,0:T(8,128)(2,1)S(1)}, u32[]{:S(2)}, u32[]{:S(2)}) collective-permute-start(bf16[256,512]{1,0:T(8,128)(2,1)S(1)} %merge_kernel.3.refs_11_.refs_8_), channel_id=1, source_target_pairs={{8,16},{9,17},{10,18},{11,19},{12,20},{13,21},{14,22},{15,23},{16,... | collective-permute-start | bytes 786440 | tf_op jit(solution)/shard_map/b0/ppermute | solution.py:115
  23.4 9.5 %collective-permute-start.7 = (bf16[256,512]{1,0:T(8,128)(2,1)S(1)}, bf16[256,512]{1,0:T(8,128)(2,1)S(1)}, u32[]{:S(2)}, u32[]{:S(2)}) collective-permute-start(bf16[256,512]{1,0:T(8,128)(2,1)S(1)} %merge_kernel.4.refs_12_.refs_9_), channel_id=1, source_target_pairs={{8,16},{9,17},{10,18},{11,19},{12,20},{13,21},{14,22},{15,23},{16,... | collective-permute-start | bytes 786440 | tf_op jit(solution)/shard_map/b1/ppermute | solution.py:115
  26.6 16.0 %collective-permute-start.11 = (bf16[256,512]{1,0:T(8,128)(2,1)S(1)}, bf16[256,512]{1,0:T(8,128)(2,1)S(1)}, u32[]{:S(2)}, u32[]{:S(2)}) collective-permute-start(bf16[256,512]{1,0:T(8,128)(2,1)S(1)} %collective-permute-done.1.refs_0_), channel_id=1, source_target_pairs={{8,16},{9,17},{10,18},{11,19},{12,20},{13,21},{14,22},{15,23},{16,... | collective-permute-start | bytes 786440 | tf_op jit(solution)/shard_map/c0/ppermute | solution.py:115
  29.7 16.2 %collective-permute-start.15 = (bf16[256,512]{1,0:T(8,128)(2,1)S(1)}, bf16[256,512]{1,0:T(8,128)(2,1)S(1)}, u32[]{:S(2)}, u32[]{:S(2)}) collective-permute-start(bf16[256,512]{1,0:T(8,128)(2,1)S(1)} %collective-permute-done.3.refs_1_), channel_id=1, source_target_pairs={{8,16},{9,17},{10,18},{11,19},{12,20},{13,21},{14,22},{15,23},{16,... | collective-permute-start | bytes 786440 | tf_op jit(solution)/shard_map/c1/ppermute | solution.py:115
  31.4 20.1 %collective-permute-start.9 = (bf16[256,512]{1,0:T(8,128)(2,1)S(1)}, bf16[256,512]{1,0:T(8,128)(2,1)S(1)}, u32[]{:S(2)}, u32[]{:S(2)}) collective-permute-start(bf16[256,512]{1,0:T(8,128)(2,1)S(1)} %get-tuple-element.35.refs_13_.refs_10_), channel_id=1, source_target_pairs={{8,16},{9,17},{10,18},{11,19},{12,20},{13,21},{14,22},{15,23},{16,... | collective-permute-start | bytes 786440 | tf_op jit(solution)/shard_map/b2/ppermute | solution.py:115
  32.1 19.4 %collective-permute-start.10 = (bf16[256,512]{1,0:T(8,128)(2,1)S(1)}, bf16[256,512]{1,0:T(8,128)(2,1)S(1)}, u32[]{:S(2)}, u32[]{:S(2)}) collective-permute-start(bf16[256,512]{1,0:T(8,128)(2,1)S(1)} %get-tuple-element.36.refs_14_.refs_11_), channel_id=1, source_target_pairs={{8,16},{9,17},{10,18},{11,19},{12,20},{13,21},{14,22},{15,23},{16,... | collective-permute-start | bytes 786440 | tf_op jit(solution)/shard_map/b3/ppermute | solution.py:115
  32.8 27.5 %collective-permute-start.5 = (bf16[256,512]{1,0:T(8,128)(2,1)S(1)}, bf16[256,512]{1,0:T(8,128)(2,1)S(1)}, u32[]{:S(2)}, u32[]{:S(2)}) collective-permute-start(bf16[256,512]{1,0:T(8,128)(2,1)S(1)} %get-tuple-element.35.refs_13_.refs_10_), channel_id=1, source_target_pairs={{0,8},{1,9},{2,10},{3,11},{4,12},{5,13},{6,14},{7,15},{8,0},{9,1},... | collective-permute-start | bytes 786440 | tf_op jit(solution)/shard_map/a2/ppermute | solution.py:115
  42.6 21.1 %collective-permute-start.14 = (bf16[256,512]{1,0:T(8,128)(2,1)S(1)}, bf16[256,512]{1,0:T(8,128)(2,1)S(1)}, u32[]{:S(2)}, u32[]{:S(2)}) collective-permute-start(bf16[256,512]{1,0:T(8,128)(2,1)S(1)} %collective-permute-done.11.refs_6_), channel_id=1, source_target_pairs={{0,8},{1,9},{2,10},{3,11},{4,12},{5,13},{6,14},{7,15},{8,0},{9,1},... | collective-permute-start | bytes 786440 | tf_op jit(solution)/shard_map/e0/ppermute | solution.py:115
  45.9 17.8 %collective-permute-start.16 = (bf16[256,512]{1,0:T(8,128)(2,1)S(1)}, bf16[256,512]{1,0:T(8,128)(2,1)S(1)}, u32[]{:S(2)}, u32[]{:S(2)}) collective-permute-start(bf16[256,512]{1,0:T(8,128)(2,1)S(1)} %collective-permute-done.15.refs_4_), channel_id=1, source_target_pairs={{0,8},{1,9},{2,10},{3,11},{4,12},{5,13},{6,14},{7,15},{8,0},{9,1},... | collective-permute-start | bytes 786440 | tf_op jit(solution)/shard_map/e1/ppermute | solution.py:115
  51.6 15.5 %collective-permute-start.13 = (bf16[256,512]{1,0:T(8,128)(2,1)S(1)}, bf16[256,512]{1,0:T(8,128)(2,1)S(1)}, u32[]{:S(2)}, u32[]{:S(2)}) collective-permute-start(bf16[256,512]{1,0:T(8,128)(2,1)S(1)} %get-tuple-element.50), channel_id=1, source_target_pairs={{0,8},{1,9},{2,10},{3,11},{4,12},{5,13},{6,14},{7,15},{8,0},{9,1},... | collective-permute-start | bytes 786440 | tf_op jit(solution)/shard_map/d0/ppermute | solution.py:115
  61.0 8.9 %collective-permute-start.8 = (bf16[256,512]{1,0:T(8,128)(2,1)S(1)}, bf16[256,512]{1,0:T(8,128)(2,1)S(1)}, u32[]{:S(2)}, u32[]{:S(2)}) collective-permute-start(bf16[256,512]{1,0:T(8,128)(2,1)S(1)} %get-tuple-element.51), channel_id=1, source_target_pairs={{0,8},{1,9},{2,10},{3,11},{4,12},{5,13},{6,14},{7,15},{8,0},{9,1},... | collective-permute-start | bytes 786440 | tf_op jit(solution)/shard_map/a3/ppermute | solution.py:115
  70.2 20.8 %collective-permute-start.17 = (bf16[6,256,512]{2,1,0:T(8,128)(2,1)S(1)}, bf16[6,256,512]{2,1,0:T(8,128)(2,1)S(1)}, u32[]{:S(2)}, u32[]{:S(2)}) collective-permute-start(bf16[6,256,512]{2,1,0:T(8,128)(2,1)S(1)} %get-tuple-element.37.refs_0_), channel_id=1, source_target_pairs={{0,1},{1,0},{2,3},{3,2},{4,5},{5,4},{6,7},{7,6},{8,9},{9,8},{10,11... | collective-permute-start | bytes 4718600 | tf_op jit(solution)/shard_map/ppermute | solution.py:115
  71.0 11.7 %collective-permute-start.22 = (bf16[256,512]{1,0:T(8,128)(2,1)S(1)}, bf16[256,512]{1,0:T(8,128)(2,1)S(1)}, u32[]{:S(2)}, u32[]{:S(2)}) collective-permute-start(bf16[256,512]{1,0:T(8,128)(2,1)S(1)} %get-tuple-element.49), channel_id=1, source_target_pairs={{0,8},{1,9},{2,10},{3,11},{4,12},{5,13},{6,14},{7,15},{8,0},{9,1},... | collective-permute-start | bytes 786440 | tf_op jit(solution)/shard_map/d2/ppermute | solution.py:115
  74.9 13.9 %collective-permute-start.23 = (bf16[256,512]{1,0:T(8,128)(2,1)S(1)}, bf16[256,512]{1,0:T(8,128)(2,1)S(1)}, u32[]{:S(2)}, u32[]{:S(2)}) collective-permute-start(bf16[256,512]{1,0:T(8,128)(2,1)S(1)} %broadcast_select_fusion), channel_id=1, source_target_pairs={{0,8},{1,9},{2,10},{3,11},{4,12},{5,13},{6,14},{7,15},{8,0},{9,1},... | collective-permute-start | bytes 786440 | tf_op jit(solution)/shard_map/e2/ppermute | solution.py:115
  94.0 14.8 %collective-permute-start.25 = (bf16[512,256]{1,0:T(8,128)(2,1)S(1)}, bf16[512,256]{1,0:T(8,128)(2,1)S(1)}, u32[]{:S(2)}, u32[]{:S(2)}) collective-permute-start(bf16[512,256]{1,0:T(8,128)(2,1)S(1)} %get-tuple-element.46), channel_id=1, source_target_pairs={{0,4},{1,5},{2,6},{3,7},{4,0},{5,1},{6,2},{7,3},{8,12},{9,13},{10,... | collective-permute-start | bytes 786440 | tf_op jit(solution)/shard_map/ppermute | solution.py:115
  95.6 14.7 %collective-permute-start.26 = (bf16[512,256]{1,0:T(8,128)(2,1)S(1)}, bf16[512,256]{1,0:T(8,128)(2,1)S(1)}, u32[]{:S(2)}, u32[]{:S(2)}) collective-permute-start(bf16[512,256]{1,0:T(8,128)(2,1)S(1)} %get-tuple-element.47), channel_id=1, source_target_pairs={{0,6},{1,7},{2,4},{3,5},{4,2},{5,3},{6,0},{7,1},{8,14},{9,15},{10,... | collective-permute-start | bytes 786440 | tf_op jit(solution)/shard_map/ppermute | solution.py:115
  97.0 13.3 %collective-permute-start.27 = (bf16[512,256]{1,0:T(8,128)(2,1)S(1)}, bf16[512,256]{1,0:T(8,128)(2,1)S(1)}, u32[]{:S(2)}, u32[]{:S(2)}) collective-permute-start(bf16[512,256]{1,0:T(8,128)(2,1)S(1)} %get-tuple-element.48), channel_id=1, source_target_pairs={{0,2},{1,3},{2,0},{3,1},{4,6},{5,7},{6,4},{7,5},{8,10},{9,11},{10,... | collective-permute-start | bytes 786440 | tf_op jit(solution)/shard_map/ppermute | solution.py:115
  100.5 18.7 %collective-permute-start.18 = (bf16[512,256]{1,0:T(8,128)(2,1)S(1)}, bf16[512,256]{1,0:T(8,128)(2,1)S(1)}, u32[]{:S(2)}, u32[]{:S(2)}) collective-permute-start(bf16[512,256]{1,0:T(8,128)(2,1)S(1)} %get-tuple-element.40), channel_id=1, source_target_pairs={{0,4},{1,5},{2,6},{3,7},{4,0},{5,1},{6,2},{7,3},{8,12},{9,13},{10,... | collective-permute-start | bytes 786440 | tf_op jit(solution)/shard_map/ppermute | solution.py:115
  102.1 17.1 %collective-permute-start.19 = (bf16[512,256]{1,0:T(8,128)(2,1)S(1)}, bf16[512,256]{1,0:T(8,128)(2,1)S(1)}, u32[]{:S(2)}, u32[]{:S(2)}) collective-permute-start(bf16[512,256]{1,0:T(8,128)(2,1)S(1)} %get-tuple-element.41), channel_id=1, source_target_pairs={{0,6},{1,7},{2,4},{3,5},{4,2},{5,3},{6,0},{7,1},{8,14},{9,15},{10,... | collective-permute-start | bytes 786440 | tf_op jit(solution)/shard_map/ppermute | solution.py:115
  108.8 11.7 %collective-permute-start.20 = (bf16[512,256]{1,0:T(8,128)(2,1)S(1)}, bf16[512,256]{1,0:T(8,128)(2,1)S(1)}, u32[]{:S(2)}, u32[]{:S(2)}) collective-permute-start(bf16[512,256]{1,0:T(8,128)(2,1)S(1)} %get-tuple-element.42), channel_id=1, source_target_pairs={{0,2},{1,3},{2,0},{3,1},{4,6},{5,7},{6,4},{7,5},{8,10},{9,11},{10,... | collective-permute-start | bytes 786440 | tf_op jit(solution)/shard_map/ppermute | solution.py:115
  (9 other events, 29.8 us)

commit v2 on v1

--- a/solution.py
+++ b/solution.py
@@ -13,23 +13,25 @@
 ROUNDS = 4
 PAIR_ROWS = 128
 NZ, NY, NX, NC = 4, 2, 2, 2
+WINDOW = 9
 VMEM_LIMIT = 40 * 1024 * 1024
+FIRST_LIMIT = 62 * 1024 * 1024
 BOTH = ("panel", "feat")
-ORDER = ((2, 3, 1, 0), (0, 3, 2, 1), (3, 2, 1, 0), (0, 3, 1, 2))
+ORDER = ((2, 3, 0, 1), (3, 2, 0, 1), (3, 2, 1, 0), (0, 3, 1, 2))
 CHUNKS = ((0,), (1,), (2, 3))
 FOUND = (
-    {1: {0: "a0", 3: "a1", 2: "a2"}, 2: {3: "a3", 0: "d0", 2: "d2"}, 3: {0: "e0", 3: "e1", 2: "e2"}},
+    {1: {3: "a0", 2: "a1", 0: "a2"}, 2: {3: "a3", 2: "d0", 0: "d1"}, 3: {0: "e0", 3: "e1", 2: "e2"}},
     {
-        0: {2: "a0", 3: "a1", 1: "a2", 0: "a3"},
+        0: {2: "a0", 3: "a1", 0: "a2", 1: "a3"},
         2: {3: "b0", 2: "b1", 1: "b2", 0: "b3"},
         3: {0: "c0", 3: "c1", 1: "c2", 2: "c3"},
     },
     {
         3: {0: "a0", 3: "a1", 1: "a2", 2: "a3"},
-        1: {0: "b0", 3: "b1", 2: "b2", 1: "b3"},
-        0: {2: "c0", 3: "c1", 1: "c2", 0: "c3"},
+        1: {3: "b0", 2: "b1", 0: "b2", 1: "b3"},
+        0: {2: "c0", 3: "c1", 0: "c2", 1: "c3"},
     },
-    {2: {3: "a0", 2: "a1", 1: "a2"}, 1: {3: "a3", 2: "d0", 1: "d2"}, 0: {2: "e0", 3: "e1", 1: "e2"}},
+    {2: {3: "a0", 2: "a1", 1: "a2"}, 1: {3: "a3", 2: "d0", 1: "d1"}, 0: {2: "e0", 3: "e1", 1: "e2"}},
 )
 
 
@@ -136,7 +138,7 @@
 
 
 def z_middle(value):
-    return hop(value, lambda z, y, x, c: (3 - z, y, x, c) if z in (1, 2) else None)
+    return hop(value, lambda z, y, x, c: (3 - z, y, x, c) if z in (1, 2) else (z, y, x, 1 - c))
 
 
 def place():
@@ -144,7 +146,7 @@
     return panel // NY, panel % NY, feat // NC, feat % NC
 
 
-def call(kernel, out_shape, in_specs, out_specs, cost, scratch=()):
+def call(kernel, out_shape, in_specs, out_specs, cost, scratch=(), limit=VMEM_LIMIT):
     return pl.pallas_call(
         kernel,
         name=kernel.func.__name__,
@@ -152,7 +154,7 @@
         in_specs=in_specs,
         out_specs=out_specs,
         scratch_shapes=scratch,
-        compiler_params=pltpu.CompilerParams(vmem_limit_bytes=VMEM_LIMIT),
+        compiler_params=pltpu.CompilerParams(vmem_limit_bytes=limit),
         cost_estimate=pl.CostEstimate(flops=cost[0], bytes_accessed=cost[1], transcendentals=0),
     )
 
@@ -201,12 +203,36 @@
 
 
 def first_kernel(
-    slots, count_ref, assign_ref, center_ref, weight_ref, dosage_ref, slot_ref, counts_ref, rows_ref, away_ref
+    slots,
+    count_ref,
+    assign_hbm,
+    center_hbm,
+    weight_hbm,
+    dosage_hbm,
+    slot_ref,
+    counts_ref,
+    rows_ref,
+    away_ref,
+    assign_ref,
+    center_ref,
+    weight_ref,
+    dosage_ref,
+    sems,
 ):
-    capacity = dosage_ref.shape[0]
+    capacity, half = dosage_ref.shape
     _, y, _, _ = place()
     panels = capacity // slots
-    assign = assign_ref[...]
+    columns, features = columns_of_half(NY * half, 1 - y)
+    copies = [
+        pltpu.make_async_copy(assign_hbm, assign_ref, sems.at[0]),
+        pltpu.make_async_copy(dosage_hbm.at[:, columns], dosage_ref, sems.at[1]),
+        pltpu.make_async_copy(center_hbm.at[:, features], center_ref, sems.at[2]),
+        pltpu.make_async_copy(weight_hbm.at[:, features], weight_ref, sems.at[3]),
+    ]
+    for copy in copies:
+        copy.start()
+    copies[0].wait()
+    assign = assign_ref[...].reshape(1, capacity)
     lane = lax.broadcasted_iota(jnp.int32, (panels, capacity), 1)
     panel_id = lax.broadcasted_iota(jnp.int32, (panels, capacity), 0)
     live = lane < count_ref[0]
@@ -220,7 +246,10 @@
     rank = jnp.sum(jnp.where(member, running - 1, 0), axis=0, keepdims=True)
     slot = jnp.where(live[:1], assign * slots + rank, -1)
     slot_ref[...] = slot
-    rows_ref[...] = standard(dosage_ref, center_ref, weight_ref, 1 - y)
+    for copy in copies[1:]:
+        copy.wait()
+    rows = dosage_ref[...].astype(jnp.float32)
+    rows_ref[...] = ((rows - center_ref[...]) * weight_ref[...]).astype(jnp.bfloat16)
     at = 0
     for step in CHUNKS[0]:
         away_ref[pl.ds(at, 2 * slots), :] = picked(picks(slot, slots, step), rows_ref[...])
@@ -372,10 +401,18 @@
             bf16(capacity, half),
             bf16(chunk_rows[0], half),
         ),
-        [IN_SMEM] + [IN_VMEM] * 4,
+        [IN_SMEM] + [ANYWHERE] * 4,
         (IN_VMEM,) * 4,
         (2 * chunk_rows[0] * capacity * half, 3 * capacity * width),
-    )(row_counts, assignment.reshape(1, capacity), center, weight, dosage)
+        (
+            pltpu.VMEM((capacity,), jnp.int32),
+            pltpu.VMEM((1, half), jnp.float32),
+            pltpu.VMEM((1, half), jnp.float32),
+            pltpu.VMEM((capacity, half), jnp.bfloat16),
+            pltpu.SemaphoreType.DMA((4,)),
+        ),
+        FIRST_LIMIT,
+    )(row_counts, assignment, center, weight, dosage)
     with jax.named_scope("y0"):
         came = [to_y(away)]
     own, *later = call(
@@ -391,7 +428,26 @@
                 away, _ = lax.optimization_barrier((away, came[k - 1]))
             came.append(to_y(away))
     pieces = {}
+    z = lax.axis_index("panel") // NY
+
+    sent = {z_ends: [], z_middle: []}
+
+    def swap(move, name, value):
+        before = sent[move]
+        if len(before) >= WINDOW:
+            value, _ = lax.optimization_barrier((value, pieces[before[-WINDOW]]))
+        with jax.named_scope(name):
+            pieces[name] = move(value)
+        before.append(name)
+
+    ends = functools.partial(swap, z_ends)
+    middle = functools.partial(swap, z_middle)
+
     for chunk, other in zip(CHUNKS, came):
+        if pieces:
+            other, _ = lax.optimization_barrier((other, merged[-1]))
+        if len(chunk) == 2:
+            other, _, _ = lax.optimization_barrier((other, pieces["a0"], pieces["b0"]))
         merged = call(
             functools.partial(merge_kernel, slots, chunk),
             (bf16(group_rows, half),) * len(chunk),
@@ -401,33 +457,15 @@
         )(counts, own, other)
         for step, piece in zip(chunk, merged):
             pieces["o%d" % step] = piece
-
-    z = lax.axis_index("panel") // NY
-
-    def either(first, second, planes):
-        return jnp.where((z == planes[0]) | (z == planes[1]), pieces[first], pieces[second])
-
-    def ends(name, value):
-        with jax.named_scope(name):
-            pieces[name] = z_ends(value)
-
-    def middle(name, value):
-        with jax.named_scope(name):
-            pieces[name] = z_middle(value)
-
-    for k in range(NZ - 1):
-        ends("a%d" % k, pieces["o%d" % k])
-        middle("b%d" % k, pieces["o%d" % k])
-    pieces["f"] = either("b0", "b1", (0, 1))
-    ends("a3", either("o3", "f", (0, 3)))
-    middle("b3", pieces["o3"])
-    ends("d0", either("b3", "b2", (0, 1)))
+            if step < NZ - 1:
+                ends("a%d" % step, piece)
+            middle("b%d" % step, piece)
+
+    ends("a3", jnp.where((z == 0) | (z == 3), pieces["o3"], pieces["b0"]))
     for k in range(NZ):
         middle("c%d" % k, pieces["a%d" % k])
-    ends("e0", pieces["c0"])
-    ends("e1", pieces["c1"])
-    ends("d2", either("b1", "b3", (0, 1)))
-    ends("e2", either("c3", "c2", (0, 1)))
+    for name, passed in (("d0", "b1"), ("d1", "b3"), ("e0", "c0"), ("e1", "c1"), ("e2", "c3")):
+        ends(name, pieces[passed])
 
     def collect(whole, split):
         sent, kept = 4 * len(whole) + 2 * len(split), 2 * len(split)
@@ -450,6 +488,7 @@
     sent1, kept1 = collect((0,), (1,))
     far1 = to_core(sent1)
     first = plane_tiles((((1, 1), (1, 0)), ((0, 0), (1, 1))), sent1, far1, (kept1,), (far1,))
+    pieces["e2"], _ = lax.optimization_barrier((pieces["e2"], first[0]))
     sent2, kept2 = collect((), (2,))
     far2 = to_core(sent2)
     second = plane_tiles((((2, 1), (2, 0)), ((1, 0), (2, 1))), sent1, far1, (kept1, kept2), (far1, far2))

time: 123 us -> 105 us (0.85)
  starting transfers between devices: 64.8 us -> 48.6 us
  local copies, waits for them, and re-layouts: 4.17 us -> 2.4 us
  waiting for transfers between devices: 38.7 us -> 37.1 us
  Pallas kernels: 12 us -> 13.6 us
    ppermute x28, starting transfers between devices: 64.8 us -> 48.6 us  [hop(): return lax.ppermute(value, BOTH, pairs)]
    pallas_call x1, Pallas kernels: 0.94 us -> 2.6 us  [plane_shards(): call(functools.partial(first_kernel, slots), (jax.ShapeDtypeStruct((1, ca...]
    ppermute x28, waiting for transfers between devices: 38.7 us -> 37.1 us  [hop(): return lax.ppermute(value, BOTH, pairs)]
    unnamed x10 -> x12, local copies, waits for them, and re-layouts: 2.94 us -> 1.86 us
  transfers between devices with their start and end apart: 28 -> 28, of which waited for: 11 -> 13; matrix products, arithmetic and copies ran while one was open for 0% -> 0% of each run, Pallas kernels for 6% -> 10%
where the time goes in v2:
time: 105 us; the launch traced here: 104 us
  starting transfers between devices  48.6 us (46%)
  waiting for transfers between devices  37.1 us (35%)
  Pallas kernels  13.6 us (13%)
  local copies, waits for them, and re-layouts  2.4 us (2%)
  other arithmetic  1.76 us (2%)
    ppermute x28, starting transfers between devices, hop(): return lax.ppermute(value, BOTH, pairs)  48.6 us
    ppermute x28, waiting for transfers between devices, hop(): return lax.ppermute(value, BOTH, pairs)  37.1 us
    pallas_call x2, Pallas kernels, plane_tiles(): call(functools.partial(tile_kernel, tiles, len(kept)), (jax.ShapeDtypeStr...  5.97 us
    pallas_call x3, Pallas kernels, plane_shards(): call(functools.partial(merge_kernel, slots, chunk), (bf16(group_rows, hal...  2.8 us
    pallas_call x1, Pallas kernels, plane_shards(): call(functools.partial(first_kernel, slots), (jax.ShapeDtypeStruct((1, ca...  2.6 us
  transfers between devices with their start and end apart: 28, of which 13 were waited for; matrix products, arithmetic and copies ran while one was open for 0% of the time, Pallas kernels for 10%

profile of v2, /device:TPU:0, one launch (start us, length us, event | category | flops | bytes accessed | tf_op | source)
XLA Modules:
  0.0 104.4 jit_solution(3639835272053476462)
XLA Ops:
  0.8 2.6 %first_kernel.1 = (s32[1,896]{1,0:T(1,128)}, s32[8,128]{1,0:T(8,128)}, bf16[896,512]{1,0:T(8,128)(2,1)}, bf16[224,512]{1,0:T(8,128)(2,1)}) custom-call(s32[1]{0:T(128)S(6)} %copy.6.count_ref, s32[896]{0:T(1024)} %assign_hbm.1, f32[1,4096]{1,0:T(1,128)} %bitcast.2, f32[1,4096]{1,0:T(1,128)} %bitcast.4, bf16[896,1024]{1,0:T(8,128)(2,1)} %dosage_ref.1), custom_call_target="tpu_custom_call" | custom-call | flops 205520896 | bytes 2752512 | tf_op jit(solution)/shard_map/first_kernel/pallas_call | solution.py:396
  3.4 3.0 %collective-permute-start = (bf16[224,512]{1,0:T(8,128)(2,1)}, bf16[224,512]{1,0:T(8,128)(2,1)S(1)}, u32[]{:S(2)}, u32[]{:S(2)}) collective-permute-start(bf16[224,512]{1,0:T(8,128)(2,1)} %get-tuple-element.35), channel_id=1, source_target_pairs={{0,4},{1,5},{2,6},{3,7},{4,0},{5,1},{6,2},{7,3},{8,12},{9,13},{10,... | collective-permute-start | bytes 688136 | tf_op jit(solution)/shard_map/y0/ppermute | solution.py:117
  8.3 1.9 %rest_kernel.1 = (bf16[896,512]{1,0:T(8,128)(2,1)S(1)}, bf16[224,512]{1,0:T(8,128)(2,1)S(1)}, bf16[448,512]{1,0:T(8,128)(2,1)}) custom-call(s32[1,896]{1,0:T(1,128)S(1)} %copy-done.5, bf16[896,512]{1,0:T(8,128)(2,1)S(1)} %copy-done.4, f32[1,4096]{1,0:T(1,128)S(1)} %bitcast.3, f32[1,4096]{1,0:T(1,128)S(1)} %bitcast.5, bf16[896,1024]{1,0:T(8,128)(2,1)S(1)} %copy-done), custom_call_target="tpu_custom_call" | custom-call | flops 1644167168 | bytes 2752512 | tf_op jit(solution)/shard_map/rest_kernel/pallas_call | solution.py:418
  10.3 2.5 %collective-permute-done.other_ref = bf16[224,512]{1,0:T(8,128)(2,1)S(1)} collective-permute-done((bf16[224,512]{1,0:T(8,128)(2,1)}, bf16[224,512]{1,0:T(8,128)(2,1)S(1)}, u32[]{:S(2)}, u32[]{:S(2)}) %collective-permute-start) | collective-permute-done | bytes 229408 | tf_op jit(solution)/shard_map/y0/ppermute | solution.py:117
  12.8 2.4 %collective-permute-start.4 = (bf16[448,512]{1,0:T(8,128)(2,1)}, bf16[448,512]{1,0:T(8,128)(2,1)S(1)}, u32[]{:S(2)}, u32[]{:S(2)}) collective-permute-start(bf16[448,512]{1,0:T(8,128)(2,1)} %get-tuple-element.39), channel_id=1, source_target_pairs={{0,4},{1,5},{2,6},{3,7},{4,0},{5,1},{6,2},{7,3},{8,12},{9,13},{10,... | collective-permute-start | bytes 1376264 | tf_op jit(solution)/shard_map/y2/ppermute | solution.py:117
  16.0 2.7 %collective-permute-done.2.other_ref = bf16[224,512]{1,0:T(8,128)(2,1)S(1)} collective-permute-done((bf16[224,512]{1,0:T(8,128)(2,1)S(1)}, bf16[224,512]{1,0:T(8,128)(2,1)S(1)}, u32[]{:S(2)}, u32[]{:S(2)}) %collective-permute-start.2) | collective-permute-done | bytes 229408 | tf_op jit(solution)/shard_map/y1/ppermute | solution.py:117
  19.7 1.6 %collective-permute-start.3 = (bf16[256,512]{1,0:T(8,128)(2,1)S(1)}, bf16[256,512]{1,0:T(8,128)(2,1)S(1)}, u32[]{:S(2)}, u32[]{:S(2)}) collective-permute-start(bf16[256,512]{1,0:T(8,128)(2,1)S(1)} %merge_kernel.4.refs_14_), channel_id=1, source_target_pairs={{0,8},{1,9},{2,10},{3,11},{4,12},{5,13},{6,14},{7,15},{8,0},{9,1},... | collective-permute-start | bytes 786440 | tf_op jit(solution)/shard_map/a1/ppermute | solution.py:117
  21.3 3.2 %collective-permute-start.1 = (bf16[256,512]{1,0:T(8,128)(2,1)S(1)}, bf16[256,512]{1,0:T(8,128)(2,1)S(1)}, u32[]{:S(2)}, u32[]{:S(2)}) collective-permute-start(bf16[256,512]{1,0:T(8,128)(2,1)S(1)} %merge_kernel.3.refs_10_), channel_id=1, source_target_pairs={{0,8},{1,9},{2,10},{3,11},{4,12},{5,13},{6,14},{7,15},{8,0},{9,1},... | collective-permute-start | bytes 786440 | tf_op jit(solution)/shard_map/a0/ppermute | solution.py:117
  24.5 3.4 %collective-permute-done.3.refs_1_ = bf16[256,512]{1,0:T(8,128)(2,1)S(1)} collective-permute-done((bf16[256,512]{1,0:T(8,128)(2,1)S(1)}, bf16[256,512]{1,0:T(8,128)(2,1)S(1)}, u32[]{:S(2)}, u32[]{:S(2)}) %collective-permute-start.3) | collective-permute-done | bytes 262176 | tf_op jit(solution)/shard_map/a1/ppermute | solution.py:117
  27.8 4.1 %collective-permute-start.14 = (bf16[256,512]{1,0:T(8,128)(2,1)S(1)}, bf16[256,512]{1,0:T(8,128)(2,1)S(1)}, u32[]{:S(2)}, u32[]{:S(2)}) collective-permute-start(bf16[256,512]{1,0:T(8,128)(2,1)S(1)} %collective-permute-done.8.refs_4_), channel_id=1, source_target_pairs={{0,8},{1,9},{2,10},{3,11},{4,12},{5,13},{6,14},{7,15},{8,0},{9,1},... | collective-permute-start | bytes 786440 | tf_op jit(solution)/shard_map/d0/ppermute | solution.py:117
  33.6 4.7 %collective-permute-start.7 = (bf16[256,512]{1,0:T(8,128)(2,1)S(1)}, bf16[256,512]{1,0:T(8,128)(2,1)S(1)}, u32[]{:S(2)}, u32[]{:S(2)}) collective-permute-start(bf16[256,512]{1,0:T(8,128)(2,1)S(1)} %broadcast_select_fusion), channel_id=1, source_target_pairs={{0,8},{1,9},{2,10},{3,11},{4,12},{5,13},{6,14},{7,15},{8,0},{9,1},... | collective-permute-start | bytes 786440 | tf_op jit(solution)/shard_map/a3/ppermute | solution.py:117
  38.8 9.5 %collective-permute-start.18 = (bf16[256,512]{1,0:T(8,128)(2,1)S(1)}, bf16[256,512]{1,0:T(8,128)(2,1)S(1)}, u32[]{:S(2)}, u32[]{:S(2)}) collective-permute-start(bf16[256,512]{1,0:T(8,128)(2,1)S(1)} %collective-permute-done.17.refs_5_), channel_id=1, source_target_pairs={{0,8},{1,9},{2,10},{3,11},{4,12},{5,13},{6,14},{7,15},{8,0},{9,1},... | collective-permute-start | bytes 786440 | tf_op jit(solution)/shard_map/e1/ppermute | solution.py:117
  48.4 2.7 %collective-permute-done.6.refs_2_ = bf16[256,512]{1,0:T(8,128)(2,1)S(1)} collective-permute-done((bf16[256,512]{1,0:T(8,128)(2,1)S(1)}, bf16[256,512]{1,0:T(8,128)(2,1)S(1)}, u32[]{:S(2)}, u32[]{:S(2)}) %collective-permute-start.6) | collective-permute-done | bytes 262176 | tf_op jit(solution)/shard_map/a2/ppermute | solution.py:117
  51.6 8.0 %collective-permute-start.15 = (bf16[256,512]{1,0:T(8,128)(2,1)S(1)}, bf16[256,512]{1,0:T(8,128)(2,1)S(1)}, u32[]{:S(2)}, u32[]{:S(2)}) collective-permute-start(bf16[256,512]{1,0:T(8,128)(2,1)S(1)} %collective-permute-done.10.refs_6_), channel_id=1, source_target_pairs={{0,8},{1,9},{2,10},{3,11},{4,12},{5,13},{6,14},{7,15},{8,0},{9,1},... | collective-permute-start | bytes 786440 | tf_op jit(solution)/shard_map/d1/ppermute | solution.py:117
  59.6 2.7 %collective-permute-done.16.refs_12_ = bf16[256,512]{1,0:T(8,128)(2,1)S(1)} collective-permute-done((bf16[256,512]{1,0:T(8,128)(2,1)S(1)}, bf16[256,512]{1,0:T(8,128)(2,1)S(1)}, u32[]{:S(2)}, u32[]{:S(2)}) %collective-permute-start.16) | collective-permute-done | bytes 262176 | tf_op jit(solution)/shard_map/e0/ppermute | solution.py:117
  62.3 3.1 %collective-permute-done.15.refs_11_.refs_8_ = bf16[256,512]{1,0:T(8,128)(2,1)S(1)} collective-permute-done((bf16[256,512]{1,0:T(8,128)(2,1)S(1)}, bf16[256,512]{1,0:T(8,128)(2,1)S(1)}, u32[]{:S(2)}, u32[]{:S(2)}) %collective-permute-start.15) | collective-permute-done | bytes 262176 | tf_op jit(solution)/shard_map/d1/ppermute | solution.py:117
  65.8 2.8 %collective-permute-start.23 = (bf16[256,512]{1,0:T(8,128)(2,1)S(1)}, bf16[256,512]{1,0:T(8,128)(2,1)S(1)}, u32[]{:S(2)}, u32[]{:S(2)}) collective-permute-start(bf16[256,512]{1,0:T(8,128)(2,1)S(1)} %collective-permute-done.13.refs_9_), channel_id=1, source_target_pairs={{0,8},{1,9},{2,10},{3,11},{4,12},{5,13},{6,14},{7,15},{8,0},{9,1},... | collective-permute-start | bytes 786440 | tf_op jit(solution)/shard_map/e2/ppermute | solution.py:117
  69.2 3.0 %tile_kernel.2 = (f32[512,256]{1,0:T(8,128)S(1)}, bf16[512,256]{1,0:T(8,128)(2,1)S(1)}, bf16[512,256]{1,0:T(8,128)(2,1)S(1)}, bf16[512,256]{1,0:T(8,128)(2,1)S(1)}) custom-call(bf16[6,256,512]{2,1,0:T(8,128)(2,1)S(1)} %get-tuple-element.44.refs_0_, bf16[6,256,512]{2,1,0:T(8,128)(2,1)S(1)} %collective-permute-done.19.refs_1_.refs_3_.refs_4_, ...), custom_call_target="tpu_custom_call" | custom-call | flops 1073741824 | bytes 8388608 | tf_op jit(solution)/shard_map/tile_kernel/pallas_call | solution.py:376
  72.2 3.3 %collective-permute-done.23.refs_9_ = bf16[256,512]{1,0:T(8,128)(2,1)S(1)} collective-permute-done((bf16[256,512]{1,0:T(8,128)(2,1)S(1)}, bf16[256,512]{1,0:T(8,128)(2,1)S(1)}, u32[]{:S(2)}, u32[]{:S(2)}) %collective-permute-start.23) | collective-permute-done | bytes 262176 | tf_op jit(solution)/shard_map/e2/ppermute | solution.py:117
  76.9 1.8 %collective-permute-start.21 = (bf16[512,256]{1,0:T(8,128)(2,1)S(1)}, bf16[512,256]{1,0:T(8,128)(2,1)S(1)}, u32[]{:S(2)}, u32[]{:S(2)}) collective-permute-start(bf16[512,256]{1,0:T(8,128)(2,1)S(1)} %get-tuple-element.48), channel_id=1, source_target_pairs={{0,6},{1,7},{2,4},{3,5},{4,2},{5,3},{6,0},{7,1},{8,14},{9,15},{10,... | collective-permute-start | bytes 786440 | tf_op jit(solution)/shard_map/ppermute | solution.py:117
  79.2 3.0 %tile_kernel.3 = (f32[512,256]{1,0:T(8,128)S(1)}, bf16[512,256]{1,0:T(8,128)(2,1)S(1)}, bf16[512,256]{1,0:T(8,128)(2,1)S(1)}, bf16[512,256]{1,0:T(8,128)(2,1)S(1)}) custom-call(bf16[6,256,512]{2,1,0:T(8,128)(2,1)S(1)} %get-tuple-element.44.refs_0_, bf16[6,256,512]{2,1,0:T(8,128)(2,1)S(1)} %collective-permute-done.19.refs_1_.refs_3_.refs_4_, ...), custom_call_target="tpu_custom_call" | custom-call | flops 1073741824 | bytes 8388608 | tf_op jit(solution)/shard_map/tile_kernel/pallas_call | solution.py:376
  83.4 1.8 %collective-permute-start.26 = (bf16[512,256]{1,0:T(8,128)(2,1)S(1)}, bf16[512,256]{1,0:T(8,128)(2,1)S(1)}, u32[]{:S(2)}, u32[]{:S(2)}) collective-permute-start(bf16[512,256]{1,0:T(8,128)(2,1)S(1)} %get-tuple-element.55), channel_id=1, source_target_pairs={{0,6},{1,7},{2,4},{3,5},{4,2},{5,3},{6,0},{7,1},{8,14},{9,15},{10,... | collective-permute-start | bytes 786440 | tf_op jit(solution)/shard_map/ppermute | solution.py:117
  85.2 5.2 %collective-permute-done.20 = bf16[512,256]{1,0:T(8,128)(2,1)S(1)} collective-permute-done((bf16[512,256]{1,0:T(8,128)(2,1)S(1)}, bf16[512,256]{1,0:T(8,128)(2,1)S(1)}, u32[]{:S(2)}, u32[]{:S(2)}) %collective-permute-start.20) | collective-permute-done | bytes 262176 | tf_op jit(solution)/shard_map/ppermute | solution.py:117
  92.4 8.8 %collective-permute-done.25 = bf16[512,256]{1,0:T(8,128)(2,1)S(1)} collective-permute-done((bf16[512,256]{1,0:T(8,128)(2,1)S(1)}, bf16[512,256]{1,0:T(8,128)(2,1)S(1)}, u32[]{:S(2)}, u32[]{:S(2)}) %collective-permute-start.25) | collective-permute-done | bytes 262176 | tf_op jit(solution)/shard_map/ppermute | solution.py:117
  (59 shorter events, 15.8 us)
Async XLA Ops:
  3.4 9.4 %collective-permute-start = (bf16[224,512]{1,0:T(8,128)(2,1)}, bf16[224,512]{1,0:T(8,128)(2,1)S(1)}, u32[]{:S(2)}, u32[]{:S(2)}) collective-permute-start(bf16[224,512]{1,0:T(8,128)(2,1)} %get-tuple-element.35), channel_id=1, source_target_pairs={{0,4},{1,5},{2,6},{3,7},{4,0},{5,1},{6,2},{7,3},{8,12},{9,13},{10,... | collective-permute-start | bytes 688136 | tf_op jit(solution)/shard_map/y0/ppermute | solution.py:117
  10.2 8.6 %collective-permute-start.2 = (bf16[224,512]{1,0:T(8,128)(2,1)S(1)}, bf16[224,512]{1,0:T(8,128)(2,1)S(1)}, u32[]{:S(2)}, u32[]{:S(2)}) collective-permute-start(bf16[224,512]{1,0:T(8,128)(2,1)S(1)} %get-tuple-element.36), channel_id=1, source_target_pairs={{0,4},{1,5},{2,6},{3,7},{4,0},{5,1},{6,2},{7,3},{8,12},{9,13},{10,... | collective-permute-start | bytes 688136 | tf_op jit(solution)/shard_map/y1/ppermute | solution.py:117
  12.8 19.7 %collective-permute-start.4 = (bf16[448,512]{1,0:T(8,128)(2,1)}, bf16[448,512]{1,0:T(8,128)(2,1)S(1)}, u32[]{:S(2)}, u32[]{:S(2)}) collective-permute-start(bf16[448,512]{1,0:T(8,128)(2,1)} %get-tuple-element.39), channel_id=1, source_target_pairs={{0,4},{1,5},{2,6},{3,7},{4,0},{5,1},{6,2},{7,3},{8,12},{9,13},{10,... | collective-permute-start | bytes 1376264 | tf_op jit(solution)/shard_map/y2/ppermute | solution.py:117
  19.7 8.2 %collective-permute-start.3 = (bf16[256,512]{1,0:T(8,128)(2,1)S(1)}, bf16[256,512]{1,0:T(8,128)(2,1)S(1)}, u32[]{:S(2)}, u32[]{:S(2)}) collective-permute-start(bf16[256,512]{1,0:T(8,128)(2,1)S(1)} %merge_kernel.4.refs_14_), channel_id=1, source_target_pairs={{0,8},{1,9},{2,10},{3,11},{4,12},{5,13},{6,14},{7,15},{8,0},{9,1},... | collective-permute-start | bytes 786440 | tf_op jit(solution)/shard_map/a1/ppermute | solution.py:117
  21.3 11.2 %collective-permute-start.1 = (bf16[256,512]{1,0:T(8,128)(2,1)S(1)}, bf16[256,512]{1,0:T(8,128)(2,1)S(1)}, u32[]{:S(2)}, u32[]{:S(2)}) collective-permute-start(bf16[256,512]{1,0:T(8,128)(2,1)S(1)} %merge_kernel.3.refs_10_), channel_id=1, source_target_pairs={{0,8},{1,9},{2,10},{3,11},{4,12},{5,13},{6,14},{7,15},{8,0},{9,1},... | collective-permute-start | bytes 786440 | tf_op jit(solution)/shard_map/a0/ppermute | solution.py:117
  24.5 8.0 %collective-permute-start.5 = (bf16[256,512]{1,0:T(8,128)(2,1)S(1)}, bf16[256,512]{1,0:T(8,128)(2,1)S(1)}, u32[]{:S(2)}, u32[]{:S(2)}) collective-permute-start(bf16[256,512]{1,0:T(8,128)(2,1)S(1)} %merge_kernel.3.refs_10_), channel_id=1, source_target_pairs={{0,1},{1,0},{2,3},{3,2},{4,5},{5,4},{6,7},{7,6},{8,16},{9,17},{10,... | collective-permute-start | bytes 786440 | tf_op jit(solution)/shard_map/b0/ppermute | solution.py:117
  27.8 10.5 %collective-permute-start.17 = (bf16[256,512]{1,0:T(8,128)(2,1)S(1)}, bf16[256,512]{1,0:T(8,128)(2,1)S(1)}, u32[]{:S(2)}, u32[]{:S(2)}) collective-permute-start(bf16[256,512]{1,0:T(8,128)(2,1)S(1)} %collective-permute-done.3.refs_1_), channel_id=1, source_target_pairs={{0,1},{1,0},{2,3},{3,2},{4,5},{5,4},{6,7},{7,6},{8,16},{9,17},{10,... | collective-permute-start | bytes 786440 | tf_op jit(solution)/shard_map/c1/ppermute | solution.py:117
  27.8 10.5 %collective-permute-start.14 = (bf16[256,512]{1,0:T(8,128)(2,1)S(1)}, bf16[256,512]{1,0:T(8,128)(2,1)S(1)}, u32[]{:S(2)}, u32[]{:S(2)}) collective-permute-start(bf16[256,512]{1,0:T(8,128)(2,1)S(1)} %collective-permute-done.8.refs_4_), channel_id=1, source_target_pairs={{0,8},{1,9},{2,10},{3,11},{4,12},{5,13},{6,14},{7,15},{8,0},{9,1},... | collective-permute-start | bytes 786440 | tf_op jit(solution)/shard_map/d0/ppermute | solution.py:117
  33.6 14.8 %collective-permute-start.7 = (bf16[256,512]{1,0:T(8,128)(2,1)S(1)}, bf16[256,512]{1,0:T(8,128)(2,1)S(1)}, u32[]{:S(2)}, u32[]{:S(2)}) collective-permute-start(bf16[256,512]{1,0:T(8,128)(2,1)S(1)} %broadcast_select_fusion), channel_id=1, source_target_pairs={{0,8},{1,9},{2,10},{3,11},{4,12},{5,13},{6,14},{7,15},{8,0},{9,1},... | collective-permute-start | bytes 786440 | tf_op jit(solution)/shard_map/a3/ppermute | solution.py:117
  38.2 12.8 %collective-permute-start.6 = (bf16[256,512]{1,0:T(8,128)(2,1)S(1)}, bf16[256,512]{1,0:T(8,128)(2,1)S(1)}, u32[]{:S(2)}, u32[]{:S(2)}) collective-permute-start(bf16[256,512]{1,0:T(8,128)(2,1)S(1)} %get-tuple-element.42.refs_15_.refs_11_), channel_id=1, source_target_pairs={{0,8},{1,9},{2,10},{3,11},{4,12},{5,13},{6,14},{7,15},{8,0},{9,1},... | collective-permute-start | bytes 786440 | tf_op jit(solution)/shard_map/a2/ppermute | solution.py:117
  38.3 12.8 %collective-permute-start.10 = (bf16[256,512]{1,0:T(8,128)(2,1)S(1)}, bf16[256,512]{1,0:T(8,128)(2,1)S(1)}, u32[]{:S(2)}, u32[]{:S(2)}) collective-permute-start(bf16[256,512]{1,0:T(8,128)(2,1)S(1)} %get-tuple-element.43.refs_16_.refs_12_), channel_id=1, source_target_pairs={{0,1},{1,0},{2,3},{3,2},{4,5},{5,4},{6,7},{7,6},{8,16},{9,17},{10,... | collective-permute-start | bytes 786440 | tf_op jit(solution)/shard_map/b3/ppermute | solution.py:117
  38.3 13.3 %collective-permute-start.9 = (bf16[256,512]{1,0:T(8,128)(2,1)S(1)}, bf16[256,512]{1,0:T(8,128)(2,1)S(1)}, u32[]{:S(2)}, u32[]{:S(2)}) collective-permute-start(bf16[256,512]{1,0:T(8,128)(2,1)S(1)} %get-tuple-element.42.refs_15_.refs_11_), channel_id=1, source_target_pairs={{0,1},{1,0},{2,3},{3,2},{4,5},{5,4},{6,7},{7,6},{8,16},{9,17},{10,... | collective-permute-start | bytes 786440 | tf_op jit(solution)/shard_map/b2/ppermute | solution.py:117
  38.8 20.7 %collective-permute-start.18 = (bf16[256,512]{1,0:T(8,128)(2,1)S(1)}, bf16[256,512]{1,0:T(8,128)(2,1)S(1)}, u32[]{:S(2)}, u32[]{:S(2)}) collective-permute-start(bf16[256,512]{1,0:T(8,128)(2,1)S(1)} %collective-permute-done.17.refs_5_), channel_id=1, source_target_pairs={{0,8},{1,9},{2,10},{3,11},{4,12},{5,13},{6,14},{7,15},{8,0},{9,1},... | collective-permute-start | bytes 786440 | tf_op jit(solution)/shard_map/e1/ppermute | solution.py:117
  48.3 14.0 %collective-permute-start.16 = (bf16[256,512]{1,0:T(8,128)(2,1)S(1)}, bf16[256,512]{1,0:T(8,128)(2,1)S(1)}, u32[]{:S(2)}, u32[]{:S(2)}) collective-permute-start(bf16[256,512]{1,0:T(8,128)(2,1)S(1)} %collective-permute-done.11.refs_7_), channel_id=1, source_target_pairs={{0,8},{1,9},{2,10},{3,11},{4,12},{5,13},{6,14},{7,15},{8,0},{9,1},... | collective-permute-start | bytes 786440 | tf_op jit(solution)/shard_map/e0/ppermute | solution.py:117
  51.1 11.2 %collective-permute-start.13 = (bf16[256,512]{1,0:T(8,128)(2,1)S(1)}, bf16[256,512]{1,0:T(8,128)(2,1)S(1)}, u32[]{:S(2)}, u32[]{:S(2)}) collective-permute-start(bf16[256,512]{1,0:T(8,128)(2,1)S(1)} %collective-permute-done.7.refs_3_), channel_id=1, source_target_pairs={{0,1},{1,0},{2,3},{3,2},{4,5},{5,4},{6,7},{7,6},{8,16},{9,17},{10,... | collective-permute-start | bytes 786440 | tf_op jit(solution)/shard_map/c3/ppermute | solution.py:117
  51.1 11.2 %collective-permute-start.12 = (bf16[256,512]{1,0:T(8,128)(2,1)S(1)}, bf16[256,512]{1,0:T(8,128)(2,1)S(1)}, u32[]{:S(2)}, u32[]{:S(2)}) collective-permute-start(bf16[256,512]{1,0:T(8,128)(2,1)S(1)} %collective-permute-done.6.refs_2_), channel_id=1, source_target_pairs={{0,1},{1,0},{2,3},{3,2},{4,5},{5,4},{6,7},{7,6},{8,16},{9,17},{10,... | collective-permute-start | bytes 786440 | tf_op jit(solution)/shard_map/c2/ppermute | solution.py:117
  51.6 13.8 %collective-permute-start.15 = (bf16[256,512]{1,0:T(8,128)(2,1)S(1)}, bf16[256,512]{1,0:T(8,128)(2,1)S(1)}, u32[]{:S(2)}, u32[]{:S(2)}) collective-permute-start(bf16[256,512]{1,0:T(8,128)(2,1)S(1)} %collective-permute-done.10.refs_6_), channel_id=1, source_target_pairs={{0,8},{1,9},{2,10},{3,11},{4,12},{5,13},{6,14},{7,15},{8,0},{9,1},... | collective-permute-start | bytes 786440 | tf_op jit(solution)/shard_map/d1/ppermute | solution.py:117
  65.8 9.7 %collective-permute-start.23 = (bf16[256,512]{1,0:T(8,128)(2,1)S(1)}, bf16[256,512]{1,0:T(8,128)(2,1)S(1)}, u32[]{:S(2)}, u32[]{:S(2)}) collective-permute-start(bf16[256,512]{1,0:T(8,128)(2,1)S(1)} %collective-permute-done.13.refs_9_), channel_id=1, source_target_pairs={{0,8},{1,9},{2,10},{3,11},{4,12},{5,13},{6,14},{7,15},{8,0},{9,1},... | collective-permute-start | bytes 786440 | tf_op jit(solution)/shard_map/e2/ppermute | solution.py:117
  75.7 14.8 %collective-permute-start.20 = (bf16[512,256]{1,0:T(8,128)(2,1)S(1)}, bf16[512,256]{1,0:T(8,128)(2,1)S(1)}, u32[]{:S(2)}, u32[]{:S(2)}) collective-permute-start(bf16[512,256]{1,0:T(8,128)(2,1)S(1)} %get-tuple-element.47), channel_id=1, source_target_pairs={{0,4},{1,5},{2,6},{3,7},{4,0},{5,1},{6,2},{7,3},{8,12},{9,13},{10,... | collective-permute-start | bytes 786440 | tf_op jit(solution)/shard_map/ppermute | solution.py:117
  76.9 15.1 %collective-permute-start.21 = (bf16[512,256]{1,0:T(8,128)(2,1)S(1)}, bf16[512,256]{1,0:T(8,128)(2,1)S(1)}, u32[]{:S(2)}, u32[]{:S(2)}) collective-permute-start(bf16[512,256]{1,0:T(8,128)(2,1)S(1)} %get-tuple-element.48), channel_id=1, source_target_pairs={{0,6},{1,7},{2,4},{3,5},{4,2},{5,3},{6,0},{7,1},{8,14},{9,15},{10,... | collective-permute-start | bytes 786440 | tf_op jit(solution)/shard_map/ppermute | solution.py:117
  78.7 13.3 %collective-permute-start.22 = (bf16[512,256]{1,0:T(8,128)(2,1)S(1)}, bf16[512,256]{1,0:T(8,128)(2,1)S(1)}, u32[]{:S(2)}, u32[]{:S(2)}) collective-permute-start(bf16[512,256]{1,0:T(8,128)(2,1)S(1)} %get-tuple-element.49), channel_id=1, source_target_pairs={{0,2},{1,3},{2,0},{3,1},{4,6},{5,7},{6,4},{7,5},{8,10},{9,11},{10,... | collective-permute-start | bytes 786440 | tf_op jit(solution)/shard_map/ppermute | solution.py:117
  82.2 19.0 %collective-permute-start.25 = (bf16[512,256]{1,0:T(8,128)(2,1)S(1)}, bf16[512,256]{1,0:T(8,128)(2,1)S(1)}, u32[]{:S(2)}, u32[]{:S(2)}) collective-permute-start(bf16[512,256]{1,0:T(8,128)(2,1)S(1)} %get-tuple-element.54), channel_id=1, source_target_pairs={{0,4},{1,5},{2,6},{3,7},{4,0},{5,1},{6,2},{7,3},{8,12},{9,13},{10,... | collective-permute-start | bytes 786440 | tf_op jit(solution)/shard_map/ppermute | solution.py:117
  83.4 17.8 %collective-permute-start.26 = (bf16[512,256]{1,0:T(8,128)(2,1)S(1)}, bf16[512,256]{1,0:T(8,128)(2,1)S(1)}, u32[]{:S(2)}, u32[]{:S(2)}) collective-permute-start(bf16[512,256]{1,0:T(8,128)(2,1)S(1)} %get-tuple-element.55), channel_id=1, source_target_pairs={{0,6},{1,7},{2,4},{3,5},{4,2},{5,3},{6,0},{7,1},{8,14},{9,15},{10,... | collective-permute-start | bytes 786440 | tf_op jit(solution)/shard_map/ppermute | solution.py:117
  90.5 12.1 %collective-permute-start.27 = (bf16[512,256]{1,0:T(8,128)(2,1)S(1)}, bf16[512,256]{1,0:T(8,128)(2,1)S(1)}, u32[]{:S(2)}, u32[]{:S(2)}) collective-permute-start(bf16[512,256]{1,0:T(8,128)(2,1)S(1)} %get-tuple-element.56), channel_id=1, source_target_pairs={{0,2},{1,3},{2,0},{3,1},{4,6},{5,7},{6,4},{7,5},{8,10},{9,11},{10,... | collective-permute-start | bytes 786440 | tf_op jit(solution)/shard_map/ppermute | solution.py:117
  (10 other events, 48.0 us)

commit v3 on v2

--- a/solution.py
+++ b/solution.py
@@ -18,6 +18,7 @@
 FIRST_LIMIT = 62 * 1024 * 1024
 BOTH = ("panel", "feat")
 ORDER = ((2, 3, 0, 1), (3, 2, 0, 1), (3, 2, 1, 0), (0, 3, 1, 2))
+LAST = "e2"
 CHUNKS = ((0,), (1,), (2, 3))
 FOUND = (
     {1: {3: "a0", 2: "a1", 0: "a2"}, 2: {3: "a3", 2: "d0", 0: "d1"}, 3: {0: "e0", 3: "e1", 2: "e2"}},
@@ -135,6 +136,17 @@
 
 def z_ends(value):
     return hop(value, lambda z, y, x, c: (z ^ 1, y, x, c))
+
+
+def z_last(value, far):
+    def move(z, y, x, c):
+        to = 1 - c if far else c
+        receiver = 1 if z in (0, 1) else 0
+        if (c if z in (0, 3) else to) == receiver:
+            return z ^ 1, y, x, to
+        return z, y, 1 - x, c
+
+    return hop(value, move)
 
 
 def z_middle(value):
@@ -306,13 +318,15 @@
                 for r in whole + split:
                     g = (zz - r) % NZ
                     for s in range(NZ):
-                        source = pieces["o%d" % ORDER[zz].index(g) if s == zz else FOUND[zz][s][g]]
+                        name = "o%d" % ORDER[zz].index(g) if s == zz else FOUND[zz][s][g]
                         if r in split and s % NC == cc:
-                            copies.append((source, keep_ref.at[kept]))
+                            target = keep_ref.at[kept]
                             kept += 1
                         else:
-                            copies.append((source, send_ref.at[sent]))
+                            target = send_ref.at[sent]
                             sent += 1
+                        if name != LAST:
+                            copies.append((pieces[name], target))
                 started = []
                 for i, (source, target) in enumerate(copies):
                     copy = pltpu.make_async_copy(source, target, sems.at[i])
@@ -322,14 +336,26 @@
                     copy.wait()
 
 
-def tile_kernel(tiles, n_kept, *refs):
-    own_ref, own_far_ref = refs[:2]
-    kept_refs = refs[2 : 2 + n_kept]
-    far_refs = refs[2 + n_kept : 2 + 2 * n_kept]
-    mine_ref, x_ref, y_ref, d_ref = refs[2 + 2 * n_kept :]
-    _, y, x, c = place()
-    depth = own_ref.shape[2]
+def tile_kernel(tiles, sent_ref, far_ref, kept_ref, *refs):
+    mine_ref, x_ref, y_ref, d_ref = refs[2:6] if len(refs) > 4 else refs
+    z, y, x, c = place()
+    depth = sent_ref.shape[2]
     nt = (((1,), (1,)), ((), ()))
+    if len(refs) > 4:
+        last_ref, last_far_ref = refs[:2]
+        near2_ref, far2_ref = refs[6:]
+        for part in range(2):
+            here = ((z == 0) & (c == 1)) if part == 1 else ((z == 3) & (c == 0))
+
+            @pl.when(here)
+            def _(part=part):
+                near2_ref[part] = last_ref[...]
+                far2_ref[part] = last_far_ref[...]
+
+            @pl.when(jnp.logical_not(here))
+            def _(part=part):
+                near2_ref[part] = kept_ref[2 + part]
+                far2_ref[part] = far_ref[NZ + 2 + part]
 
     def rows_of(ref, p):
         return ref[0:NZ, pl.ds(p * PAIR_ROWS, PAIR_ROWS), :].reshape(P_SIZE, depth)
@@ -337,50 +363,39 @@
     def columns_of(distance, q, part, near):
         rows = pl.ds(q * PAIR_ROWS, PAIR_ROWS)
         if distance == 0:
-            return (own_ref if near else own_far_ref)[2 * part + c, rows, :]
-        if near:
-            return kept_refs[distance - 1][part, rows, :]
-        ref = far_refs[distance - 1]
-        first = ref.shape[0] - 2
-        return ref[first + part, rows, :]
+            return (sent_ref if near else far_ref)[2 * part + c, rows, :]
+        if distance == 1:
+            return kept_ref[part, rows, :] if near else far_ref[NZ + part, rows, :]
+        return (near2_ref if near else far2_ref)[part, rows, :]
 
     for p in range(2):
-        left, left_far = rows_of(own_ref, p), rows_of(own_far_ref, p)
-        for part in range(2):
-            near = jnp.concatenate([columns_of(d, q, part, True) for d, q in tiles[p]], axis=0)
-            far = jnp.concatenate([columns_of(d, q, part, False) for d, q in tiles[p]], axis=0)
-            total = lax.dot_general(left, near, nt, preferred_element_type=jnp.float32) + lax.dot_general(
-                left_far, far, nt, preferred_element_type=jnp.float32
-            )
-
-            @pl.when((y == p) & (x == part))
-            def _(total=total):
-                mine_ref[...] = total
-
-            @pl.when((y == p) & (x != part))
-            def _(total=total):
-                x_ref[...] = total.astype(jnp.bfloat16)
-
-            @pl.when((y != p) & (x == part))
-            def _(total=total):
-                y_ref[...] = total.astype(jnp.bfloat16)
-
-            @pl.when((y != p) & (x != part))
-            def _(total=total):
-                d_ref[...] = total.astype(jnp.bfloat16)
-
-
-def plane_tiles(tiles, own, own_far, kept, far):
+        for mine in (True, False):
+
+            @pl.when((y == p) if mine else (y != p))
+            def _(p=p, mine=mine):
+                left, left_far = rows_of(sent_ref, p), rows_of(far_ref, p)
+                for part, out_ref in ((x, mine_ref if mine else y_ref), (1 - x, x_ref if mine else d_ref)):
+                    near = jnp.concatenate([columns_of(d, q, part, True) for d, q in tiles[p]], axis=0)
+                    far = jnp.concatenate([columns_of(d, q, part, False) for d, q in tiles[p]], axis=0)
+                    total = lax.dot_general(left, near, nt, preferred_element_type=jnp.float32) + lax.dot_general(
+                        left_far, far, nt, preferred_element_type=jnp.float32
+                    )
+                    out_ref[...] = total.astype(out_ref.dtype)
+
+
+def plane_tiles(tiles, sent, far, kept, *last):
     columns = len(tiles[0]) * PAIR_ROWS
     part = bf16(P_SIZE, columns)
+    room = (2, *sent.shape[1:])
     mine, x_part, y_part, d_part = call(
-        functools.partial(tile_kernel, tiles, len(kept)),
+        functools.partial(tile_kernel, tiles),
         (jax.ShapeDtypeStruct((P_SIZE, columns), jnp.float32), part, part, part),
-        [IN_VMEM] * (2 + 2 * len(kept)),
+        [IN_VMEM] * (3 + len(last)),
         (IN_VMEM,) * 4,
-        (2 * 4 * P_SIZE * columns * 2 * own.shape[2], 8 * 1024 * 1024),
-    )(own, own_far, *kept, *far)
-    return mine, to_y(y_part), to_diagonal(d_part), to_x(x_part)
+        (2 * 4 * P_SIZE * columns * 2 * sent.shape[2], 8 * 1024 * 1024),
+        (pltpu.VMEM(room, jnp.bfloat16),) * 2 if last else (),
+    )(sent, far, kept, *last)
+    return mine, y_part, d_part, x_part
 
 
 def plane_shards(dosage, row_counts, assignment, center, weight):
@@ -430,10 +445,10 @@
     pieces = {}
     z = lax.axis_index("panel") // NY
 
-    sent = {z_ends: [], z_middle: []}
+    queues = {z_ends: [], z_middle: []}
 
     def swap(move, name, value):
-        before = sent[move]
+        before = queues[move]
         if len(before) >= WINDOW:
             value, _ = lax.optimization_barrier((value, pieces[before[-WINDOW]]))
         with jax.named_scope(name):
@@ -462,36 +477,39 @@
             middle("b%d" % step, piece)
 
     ends("a3", jnp.where((z == 0) | (z == 3), pieces["o3"], pieces["b0"]))
+    pieces["a1"], pieces["b1"], _, _ = lax.optimization_barrier((pieces["a1"], pieces["b1"], pieces["a0"], pieces["b0"]))
     for k in range(NZ):
         middle("c%d" % k, pieces["a%d" % k])
-    for name, passed in (("d0", "b1"), ("d1", "b3"), ("e0", "c0"), ("e1", "c1"), ("e2", "c3")):
+    for name, passed in (("d0", "b1"), ("d1", "b3"), ("e0", "c0"), ("e1", "c1")):
         ends(name, pieces[passed])
-
-    def collect(whole, split):
-        sent, kept = 4 * len(whole) + 2 * len(split), 2 * len(split)
-        names = set()
-        for z in range(NZ):
-            for r in whole + split:
-                g = (z - r) % NZ
-                names.add("o%d" % ORDER[z].index(g))
-                names.update(FOUND[z][s][g] for s in range(NZ) if s != z)
-        names = sorted(names)
-        return call(
-            functools.partial(collect_kernel, names, whole, split),
-            (bf16(sent, group_rows, half), bf16(kept, group_rows, half)),
-            [ANYWHERE] * len(names),
-            (ANYWHERE, ANYWHERE),
-            (0, 4 * (sent + kept) * group_rows * half),
-            (pltpu.SemaphoreType.DMA((sent + kept,)),),
-        )(*[pieces[name] for name in names])
-
-    sent1, kept1 = collect((0,), (1,))
-    far1 = to_core(sent1)
-    first = plane_tiles((((1, 1), (1, 0)), ((0, 0), (1, 1))), sent1, far1, (kept1,), (far1,))
-    pieces["e2"], _ = lax.optimization_barrier((pieces["e2"], first[0]))
-    sent2, kept2 = collect((), (2,))
-    far2 = to_core(sent2)
-    second = plane_tiles((((2, 1), (2, 0)), ((1, 0), (2, 1))), sent1, far1, (kept1, kept2), (far1, far2))
+    with jax.named_scope("last"):
+        last = z_last(pieces["c3"], False), z_last(pieces["c3"], True)
+
+    names = set()
+    for plane in range(NZ):
+        for r in range(3):
+            g = (plane - r) % NZ
+            names.add("o%d" % ORDER[plane].index(g))
+            names.update(FOUND[plane][s][g] for s in range(NZ) if s != plane)
+    names = sorted(names - {LAST})
+    sent, kept = call(
+        functools.partial(collect_kernel, names, (0,), (1, 2)),
+        (bf16(2 * NZ, group_rows, half), bf16(NZ, group_rows, half)),
+        [ANYWHERE] * len(names),
+        (ANYWHERE, ANYWHERE),
+        (0, 4 * 3 * NZ * group_rows * half),
+        (pltpu.SemaphoreType.DMA((3 * NZ,)),),
+    )(*[pieces[name] for name in names])
+    far = to_core(sent)
+    first = plane_tiles((((1, 1), (1, 0)), ((0, 0), (1, 1))), sent, far, kept)
+    second = plane_tiles((((2, 1), (2, 0)), ((1, 0), (2, 1))), sent, far, kept, *last)
+
+    def exchanged(mine, y_part, d_part, x_part):
+        return mine, to_y(y_part), to_diagonal(d_part), to_x(x_part)
+
+    first = exchanged(*first)
+    x_part, _ = lax.optimization_barrier((second[3], first[3]))
+    second = exchanged(*second[:3], x_part)
 
     def total(parts):
         mine, *others = parts

time: 105 us -> 101 us (0.962)
  starting transfers between devices: 48.6 us -> 39.6 us
  waiting for transfers between devices: 37.1 us -> 42.7 us
  Pallas kernels: 13.6 us -> 10.6 us
  local copies, waits for them, and re-layouts: 2.4 us -> 5.33 us
    ppermute x28, starting transfers between devices: 48.6 us -> 39.6 us  [hop(): return lax.ppermute(value, BOTH, pairs)]
    ppermute x28, waiting for transfers between devices: 37.1 us -> 42.7 us  [hop(): return lax.ppermute(value, BOTH, pairs)]
    pallas_call x4 -> x3, Pallas kernels: 6.38 us -> 3.4 us  [the longest x2 3.04 us: plane_tiles(): call(functools.partial(tile_kernel, tiles), (jax.ShapeDtypeStruct((P_SIZE...]
    unnamed x12, local copies, waits for them, and re-layouts: 1.86 us -> 4.79 us
  transfers between devices with their start and end apart: 28 -> 28, of which waited for: 13 -> 11; matrix products, arithmetic and copies ran while one was open for 0% -> 0% of each run, Pallas kernels for 10% -> 8%
where the time goes in v3:
time: 101 us
  waiting for transfers between devices  42.7 us (42%)
  starting transfers between devices  39.6 us (39%)
  Pallas kernels  10.6 us (10%)
  local copies, waits for them, and re-layouts  5.33 us (5%)
  other arithmetic  1.76 us (2%)
    ppermute x28, waiting for transfers between devices, hop(): return lax.ppermute(value, BOTH, pairs)  42.7 us
    ppermute x28, starting transfers between devices, hop(): return lax.ppermute(value, BOTH, pairs)  39.6 us
    unnamed x12, local copies, waits for them, and re-layouts  4.79 us
    pallas_call x2, Pallas kernels, plane_tiles(): call(functools.partial(tile_kernel, tiles), (jax.ShapeDtypeStruct((P_SIZE...  3.04 us
    pallas_call x3, Pallas kernels, plane_shards(): call(functools.partial(merge_kernel, slots, chunk), (bf16(group_rows, hal...  2.8 us
    pallas_call x1, Pallas kernels, plane_shards(): call(functools.partial(first_kernel, slots), (jax.ShapeDtypeStruct((1, ca...  2.59 us
  transfers between devices with their start and end apart: 28, of which 11 were waited for; matrix products, arithmetic and copies ran while one was open for 0% of the time, Pallas kernels for 8%

profile of v3, /device:TPU:0, one launch (start us, length us, event | category | flops | bytes accessed | tf_op | source)
XLA Modules:
  0.0 100.9 jit_solution(5558999775767994140)
XLA Ops:
  0.7 2.6 %first_kernel.1 = (s32[1,896]{1,0:T(1,128)}, s32[8,128]{1,0:T(8,128)}, bf16[896,512]{1,0:T(8,128)(2,1)}, bf16[224,512]{1,0:T(8,128)(2,1)}) custom-call(s32[1]{0:T(128)S(6)} %copy.6.count_ref, s32[896]{0:T(1024)} %assign_hbm.1, f32[1,4096]{1,0:T(1,128)} %bitcast.2, f32[1,4096]{1,0:T(1,128)} %bitcast.4, bf16[896,1024]{1,0:T(8,128)(2,1)} %dosage_ref.1), custom_call_target="tpu_custom_call" | custom-call | flops 205520896 | bytes 2752512 | tf_op jit(solution)/shard_map/first_kernel/pallas_call | solution.py:411
  3.2 3.0 %collective-permute-start = (bf16[224,512]{1,0:T(8,128)(2,1)}, bf16[224,512]{1,0:T(8,128)(2,1)S(1)}, u32[]{:S(2)}, u32[]{:S(2)}) collective-permute-start(bf16[224,512]{1,0:T(8,128)(2,1)} %get-tuple-element.35), channel_id=1, source_target_pairs={{0,4},{1,5},{2,6},{3,7},{4,0},{5,1},{6,2},{7,3},{8,12},{9,13},{10,... | collective-permute-start | bytes 688136 | tf_op jit(solution)/shard_map/y0/ppermute | solution.py:118
  11.1 1.9 %rest_kernel.1 = (bf16[896,512]{1,0:T(8,128)(2,1)S(1)}, bf16[224,512]{1,0:T(8,128)(2,1)S(1)}, bf16[448,512]{1,0:T(8,128)(2,1)}) custom-call(s32[1,896]{1,0:T(1,128)S(1)} %copy-done.5, bf16[896,512]{1,0:T(8,128)(2,1)S(1)} %copy-done.4, f32[1,4096]{1,0:T(1,128)S(1)} %bitcast.3, f32[1,4096]{1,0:T(1,128)S(1)} %bitcast.5, bf16[896,1024]{1,0:T(8,128)(2,1)S(1)} %copy-done), custom_call_target="tpu_custom_call" | custom-call | flops 1644167168 | bytes 2752512 | tf_op jit(solution)/shard_map/rest_kernel/pallas_call | solution.py:433
  13.0 2.0 %collective-permute-start.6 = (bf16[448,512]{1,0:T(8,128)(2,1)}, bf16[448,512]{1,0:T(8,128)(2,1)S(1)}, u32[]{:S(2)}, u32[]{:S(2)}) collective-permute-start(bf16[448,512]{1,0:T(8,128)(2,1)} %get-tuple-element.40), channel_id=1, source_target_pairs={{0,4},{1,5},{2,6},{3,7},{4,0},{5,1},{6,2},{7,3},{8,12},{9,13},{10,... | collective-permute-start | bytes 1376264 | tf_op jit(solution)/shard_map/y2/ppermute | solution.py:118
  15.9 1.6 %collective-permute-start.1 = (bf16[256,512]{1,0:T(8,128)(2,1)S(1)}, bf16[256,512]{1,0:T(8,128)(2,1)S(1)}, u32[]{:S(2)}, u32[]{:S(2)}) collective-permute-start(bf16[256,512]{1,0:T(8,128)(2,1)S(1)} %merge_kernel.3.refs_16_), channel_id=1, source_target_pairs={{0,8},{1,9},{2,10},{3,11},{4,12},{5,13},{6,14},{7,15},{8,0},{9,1},... | collective-permute-start | bytes 786440 | tf_op jit(solution)/shard_map/a0/ppermute | solution.py:118
  17.6 4.0 %collective-permute-done.2.other_ref = bf16[224,512]{1,0:T(8,128)(2,1)S(1)} collective-permute-done((bf16[224,512]{1,0:T(8,128)(2,1)S(1)}, bf16[224,512]{1,0:T(8,128)(2,1)S(1)}, u32[]{:S(2)}, u32[]{:S(2)}) %collective-permute-start.2) | collective-permute-done | bytes 229408 | tf_op jit(solution)/shard_map/y1/ppermute | solution.py:118
  22.4 1.6 %collective-permute-start.3 = (bf16[256,512]{1,0:T(8,128)(2,1)S(1)}, bf16[256,512]{1,0:T(8,128)(2,1)S(1)}, u32[]{:S(2)}, u32[]{:S(2)}) collective-permute-start(bf16[256,512]{1,0:T(8,128)(2,1)S(1)} %merge_kernel.4.refs_17_), channel_id=1, source_target_pairs={{0,8},{1,9},{2,10},{3,11},{4,12},{5,13},{6,14},{7,15},{8,0},{9,1},... | collective-permute-start | bytes 786440 | tf_op jit(solution)/shard_map/a1/ppermute | solution.py:118
  24.1 4.8 %collective-permute-done.3.refs_1_ = bf16[256,512]{1,0:T(8,128)(2,1)S(1)} collective-permute-done((bf16[256,512]{1,0:T(8,128)(2,1)S(1)}, bf16[256,512]{1,0:T(8,128)(2,1)S(1)}, u32[]{:S(2)}, u32[]{:S(2)}) %collective-permute-start.3) | collective-permute-done | bytes 262176 | tf_op jit(solution)/shard_map/a1/ppermute | solution.py:118
  28.9 5.1 %collective-permute-start.15 = (bf16[256,512]{1,0:T(8,128)(2,1)S(1)}, bf16[256,512]{1,0:T(8,128)(2,1)S(1)}, u32[]{:S(2)}, u32[]{:S(2)}) collective-permute-start(bf16[256,512]{1,0:T(8,128)(2,1)S(1)} %collective-permute-done.4.refs_5_), channel_id=1, source_target_pairs={{0,8},{1,9},{2,10},{3,11},{4,12},{5,13},{6,14},{7,15},{8,0},{9,1},... | collective-permute-start | bytes 786440 | tf_op jit(solution)/shard_map/d0/ppermute | solution.py:118
  35.1 2.0 %collective-permute-start.7 = (bf16[256,512]{1,0:T(8,128)(2,1)S(1)}, bf16[256,512]{1,0:T(8,128)(2,1)S(1)}, u32[]{:S(2)}, u32[]{:S(2)}) collective-permute-start(bf16[256,512]{1,0:T(8,128)(2,1)S(1)} %get-tuple-element.43.refs_18_), channel_id=1, source_target_pairs={{0,8},{1,9},{2,10},{3,11},{4,12},{5,13},{6,14},{7,15},{8,0},{9,1},... | collective-permute-start | bytes 786440 | tf_op jit(solution)/shard_map/a2/ppermute | solution.py:118
  37.1 2.6 %collective-permute-done.15.refs_12_ = bf16[256,512]{1,0:T(8,128)(2,1)S(1)} collective-permute-done((bf16[256,512]{1,0:T(8,128)(2,1)S(1)}, bf16[256,512]{1,0:T(8,128)(2,1)S(1)}, u32[]{:S(2)}, u32[]{:S(2)}) %collective-permute-start.15) | collective-permute-done | bytes 262176 | tf_op jit(solution)/shard_map/d0/ppermute | solution.py:118
  39.7 6.6 %collective-permute-start.18 = (bf16[256,512]{1,0:T(8,128)(2,1)S(1)}, bf16[256,512]{1,0:T(8,128)(2,1)S(1)}, u32[]{:S(2)}, u32[]{:S(2)}) collective-permute-start(bf16[256,512]{1,0:T(8,128)(2,1)S(1)} %collective-permute-done.12.refs_9_), channel_id=1, source_target_pairs={{0,8},{1,9},{2,10},{3,11},{4,12},{5,13},{6,14},{7,15},{8,0},{9,1},... | collective-permute-start | bytes 786440 | tf_op jit(solution)/shard_map/e1/ppermute | solution.py:118
  47.8 3.1 %collective-permute-done.7.refs_2_ = bf16[256,512]{1,0:T(8,128)(2,1)S(1)} collective-permute-done((bf16[256,512]{1,0:T(8,128)(2,1)S(1)}, bf16[256,512]{1,0:T(8,128)(2,1)S(1)}, u32[]{:S(2)}, u32[]{:S(2)}) %collective-permute-start.7) | collective-permute-done | bytes 262176 | tf_op jit(solution)/shard_map/a2/ppermute | solution.py:118
  51.4 5.2 %collective-permute-start.16 = (bf16[256,512]{1,0:T(8,128)(2,1)S(1)}, bf16[256,512]{1,0:T(8,128)(2,1)S(1)}, u32[]{:S(2)}, u32[]{:S(2)}) collective-permute-start(bf16[256,512]{1,0:T(8,128)(2,1)S(1)} %collective-permute-done.10.refs_7_), channel_id=1, source_target_pairs={{0,8},{1,9},{2,10},{3,11},{4,12},{5,13},{6,14},{7,15},{8,0},{9,1},... | collective-permute-start | bytes 786440 | tf_op jit(solution)/shard_map/d1/ppermute | solution.py:118
  56.6 5.5 %collective-permute-done.17.refs_14_ = bf16[256,512]{1,0:T(8,128)(2,1)S(1)} collective-permute-done((bf16[256,512]{1,0:T(8,128)(2,1)S(1)}, bf16[256,512]{1,0:T(8,128)(2,1)S(1)}, u32[]{:S(2)}, u32[]{:S(2)}) %collective-permute-start.17) | collective-permute-done | bytes 262176 | tf_op jit(solution)/shard_map/e0/ppermute | solution.py:118
  62.2 4.2 %collective-permute-done.16.refs_13_ = bf16[256,512]{1,0:T(8,128)(2,1)S(1)} collective-permute-done((bf16[256,512]{1,0:T(8,128)(2,1)S(1)}, bf16[256,512]{1,0:T(8,128)(2,1)S(1)}, u32[]{:S(2)}, u32[]{:S(2)}) %collective-permute-start.16) | collective-permute-done | bytes 262176 | tf_op jit(solution)/shard_map/d1/ppermute | solution.py:118
  66.8 1.6 %collective-permute-start.23 = (bf16[256,512]{1,0:T(8,128)(2,1)S(1)}, bf16[256,512]{1,0:T(8,128)(2,1)S(1)}, u32[]{:S(2)}, u32[]{:S(2)}) collective-permute-start(bf16[256,512]{1,0:T(8,128)(2,1)S(1)} %collective-permute-done.14.refs_11_), channel_id=1, source_target_pairs={{0,2},{1,9},{2,0},{3,11},{4,6},{5,13},{6,4},{7,15},{8,10},{9,1},{1... | collective-permute-start | bytes 786440 | tf_op jit(solution)/shard_map/last/ppermute | solution.py:118
  68.9 2.1 %collective-permute-done.19.far_ref = bf16[8,256,512]{2,1,0:T(8,128)(2,1)S(1)} collective-permute-done((bf16[8,256,512]{2,1,0:T(8,128)(2,1)S(1)}, bf16[8,256,512]{2,1,0:T(8,128)(2,1)S(1)}, u32[]{:S(2)}, u32[]{:S(2)}) %collective-permute-start.19) | collective-permute-done | bytes 2097184 | tf_op jit(solution)/shard_map/ppermute | solution.py:118
  72.5 1.6 %collective-permute-start.22 = (bf16[512,256]{1,0:T(8,128)(2,1)S(1)}, bf16[512,256]{1,0:T(8,128)(2,1)S(1)}, u32[]{:S(2)}, u32[]{:S(2)}) collective-permute-start(bf16[512,256]{1,0:T(8,128)(2,1)S(1)} %get-tuple-element.51), channel_id=1, source_target_pairs={{0,2},{1,3},{2,0},{3,1},{4,6},{5,7},{6,4},{7,5},{8,10},{9,11},{10,... | collective-permute-start | bytes 786440 | tf_op jit(solution)/shard_map/ppermute | solution.py:118
  76.8 1.6 %tile_kernel.3 = (f32[512,256]{1,0:T(8,128)S(1)}, bf16[512,256]{1,0:T(8,128)(2,1)S(1)}, bf16[512,256]{1,0:T(8,128)(2,1)S(1)}, bf16[512,256]{1,0:T(8,128)(2,1)S(1)}) custom-call(bf16[8,256,512]{2,1,0:T(8,128)(2,1)S(1)} %get-tuple-element.46.sent_ref, bf16[8,256,512]{2,1,0:T(8,128)(2,1)S(1)} %collective-permute-done.19.far_ref, ...), custom_call_target="tpu_custom_call" | custom-call | flops 1073741824 | bytes 8388608 | tf_op jit(solution)/shard_map/tile_kernel/pallas_call | solution.py:390
  79.0 2.4 %collective-permute-start.26 = (bf16[512,256]{1,0:T(8,128)(2,1)S(1)}, bf16[512,256]{1,0:T(8,128)(2,1)S(1)}, u32[]{:S(2)}, u32[]{:S(2)}) collective-permute-start(bf16[512,256]{1,0:T(8,128)(2,1)S(1)} %get-tuple-element.54), channel_id=1, source_target_pairs={{0,6},{1,7},{2,4},{3,5},{4,2},{5,3},{6,0},{7,1},{8,14},{9,15},{10,... | collective-permute-start | bytes 786440 | tf_op jit(solution)/shard_map/ppermute | solution.py:118
  83.9 10.5 %collective-permute-done.20 = bf16[512,256]{1,0:T(8,128)(2,1)S(1)} collective-permute-done((bf16[512,256]{1,0:T(8,128)(2,1)S(1)}, bf16[512,256]{1,0:T(8,128)(2,1)S(1)}, u32[]{:S(2)}, u32[]{:S(2)}) %collective-permute-start.20) | collective-permute-done | bytes 262176 | tf_op jit(solution)/shard_map/ppermute | solution.py:118
  94.9 4.1 %collective-permute-done.25 = bf16[512,256]{1,0:T(8,128)(2,1)S(1)} collective-permute-done((bf16[512,256]{1,0:T(8,128)(2,1)S(1)}, bf16[512,256]{1,0:T(8,128)(2,1)S(1)}, u32[]{:S(2)}, u32[]{:S(2)}) %collective-permute-start.25) | collective-permute-done | bytes 262176 | tf_op jit(solution)/shard_map/ppermute | solution.py:118
  99.3 1.5 %maximum_multiply_fusion = f32[512,4,128]{2,1,0:T(4,128)} fusion(f32[512,2,128]{2,1,0:T(2,128)S(1)} %reshape.15, f32[512,2,128]{2,1,0:T(2,128)S(1)} %reshape.14), kind=kLoop, calls=%fused_computation | loop fusion | flops 524288 | bytes 2097152 | tf_op jit(solution)/shard_map/mul | solution.py:520
  (58 shorter events, 19.0 us)
Async XLA Ops:
  3.2 9.8 %collective-permute-start = (bf16[224,512]{1,0:T(8,128)(2,1)}, bf16[224,512]{1,0:T(8,128)(2,1)S(1)}, u32[]{:S(2)}, u32[]{:S(2)}) collective-permute-start(bf16[224,512]{1,0:T(8,128)(2,1)} %get-tuple-element.35), channel_id=1, source_target_pairs={{0,4},{1,5},{2,6},{3,7},{4,0},{5,1},{6,2},{7,3},{8,12},{9,13},{10,... | collective-permute-start | bytes 688136 | tf_op jit(solution)/shard_map/y0/ppermute | solution.py:118
  12.9 8.6 %collective-permute-start.2 = (bf16[224,512]{1,0:T(8,128)(2,1)S(1)}, bf16[224,512]{1,0:T(8,128)(2,1)S(1)}, u32[]{:S(2)}, u32[]{:S(2)}) collective-permute-start(bf16[224,512]{1,0:T(8,128)(2,1)S(1)} %get-tuple-element.36), channel_id=1, source_target_pairs={{0,4},{1,5},{2,6},{3,7},{4,0},{5,1},{6,2},{7,3},{8,12},{9,13},{10,... | collective-permute-start | bytes 688136 | tf_op jit(solution)/shard_map/y1/ppermute | solution.py:118
  13.0 20.9 %collective-permute-start.6 = (bf16[448,512]{1,0:T(8,128)(2,1)}, bf16[448,512]{1,0:T(8,128)(2,1)S(1)}, u32[]{:S(2)}, u32[]{:S(2)}) collective-permute-start(bf16[448,512]{1,0:T(8,128)(2,1)} %get-tuple-element.40), channel_id=1, source_target_pairs={{0,4},{1,5},{2,6},{3,7},{4,0},{5,1},{6,2},{7,3},{8,12},{9,13},{10,... | collective-permute-start | bytes 1376264 | tf_op jit(solution)/shard_map/y2/ppermute | solution.py:118
  15.9 8.2 %collective-permute-start.1 = (bf16[256,512]{1,0:T(8,128)(2,1)S(1)}, bf16[256,512]{1,0:T(8,128)(2,1)S(1)}, u32[]{:S(2)}, u32[]{:S(2)}) collective-permute-start(bf16[256,512]{1,0:T(8,128)(2,1)S(1)} %merge_kernel.3.refs_16_), channel_id=1, source_target_pairs={{0,8},{1,9},{2,10},{3,11},{4,12},{5,13},{6,14},{7,15},{8,0},{9,1},... | collective-permute-start | bytes 786440 | tf_op jit(solution)/shard_map/a0/ppermute | solution.py:118
  17.6 6.5 %collective-permute-start.5 = (bf16[256,512]{1,0:T(8,128)(2,1)S(1)}, bf16[256,512]{1,0:T(8,128)(2,1)S(1)}, u32[]{:S(2)}, u32[]{:S(2)}) collective-permute-start(bf16[256,512]{1,0:T(8,128)(2,1)S(1)} %merge_kernel.3.refs_16_), channel_id=1, source_target_pairs={{0,1},{1,0},{2,3},{3,2},{4,5},{5,4},{6,7},{7,6},{8,16},{9,17},{10,... | collective-permute-start | bytes 786440 | tf_op jit(solution)/shard_map/b0/ppermute | solution.py:118
  28.9 8.3 %collective-permute-start.12 = (bf16[256,512]{1,0:T(8,128)(2,1)S(1)}, bf16[256,512]{1,0:T(8,128)(2,1)S(1)}, u32[]{:S(2)}, u32[]{:S(2)}) collective-permute-start(bf16[256,512]{1,0:T(8,128)(2,1)S(1)} %collective-permute-done.3.refs_1_), channel_id=1, source_target_pairs={{0,1},{1,0},{2,3},{3,2},{4,5},{5,4},{6,7},{7,6},{8,16},{9,17},{10,... | collective-permute-start | bytes 786440 | tf_op jit(solution)/shard_map/c1/ppermute | solution.py:118
  28.9 10.8 %collective-permute-start.15 = (bf16[256,512]{1,0:T(8,128)(2,1)S(1)}, bf16[256,512]{1,0:T(8,128)(2,1)S(1)}, u32[]{:S(2)}, u32[]{:S(2)}) collective-permute-start(bf16[256,512]{1,0:T(8,128)(2,1)S(1)} %collective-permute-done.4.refs_5_), channel_id=1, source_target_pairs={{0,8},{1,9},{2,10},{3,11},{4,12},{5,13},{6,14},{7,15},{8,0},{9,1},... | collective-permute-start | bytes 786440 | tf_op jit(solution)/shard_map/d0/ppermute | solution.py:118
  35.0 11.2 %collective-permute-start.8 = (bf16[256,512]{1,0:T(8,128)(2,1)S(1)}, bf16[256,512]{1,0:T(8,128)(2,1)S(1)}, u32[]{:S(2)}, u32[]{:S(2)}) collective-permute-start(bf16[256,512]{1,0:T(8,128)(2,1)S(1)} %broadcast_select_fusion), channel_id=1, source_target_pairs={{0,8},{1,9},{2,10},{3,11},{4,12},{5,13},{6,14},{7,15},{8,0},{9,1},... | collective-permute-start | bytes 786440 | tf_op jit(solution)/shard_map/a3/ppermute | solution.py:118
  35.1 15.8 %collective-permute-start.7 = (bf16[256,512]{1,0:T(8,128)(2,1)S(1)}, bf16[256,512]{1,0:T(8,128)(2,1)S(1)}, u32[]{:S(2)}, u32[]{:S(2)}) collective-permute-start(bf16[256,512]{1,0:T(8,128)(2,1)S(1)} %get-tuple-element.43.refs_18_), channel_id=1, source_target_pairs={{0,8},{1,9},{2,10},{3,11},{4,12},{5,13},{6,14},{7,15},{8,0},{9,1},... | collective-permute-start | bytes 786440 | tf_op jit(solution)/shard_map/a2/ppermute | solution.py:118
  37.1 13.8 %collective-permute-start.10 = (bf16[256,512]{1,0:T(8,128)(2,1)S(1)}, bf16[256,512]{1,0:T(8,128)(2,1)S(1)}, u32[]{:S(2)}, u32[]{:S(2)}) collective-permute-start(bf16[256,512]{1,0:T(8,128)(2,1)S(1)} %get-tuple-element.44.refs_19_), channel_id=1, source_target_pairs={{0,1},{1,0},{2,3},{3,2},{4,5},{5,4},{6,7},{7,6},{8,16},{9,17},{10,... | collective-permute-start | bytes 786440 | tf_op jit(solution)/shard_map/b3/ppermute | solution.py:118
  39.7 11.8 %collective-permute-start.9 = (bf16[256,512]{1,0:T(8,128)(2,1)S(1)}, bf16[256,512]{1,0:T(8,128)(2,1)S(1)}, u32[]{:S(2)}, u32[]{:S(2)}) collective-permute-start(bf16[256,512]{1,0:T(8,128)(2,1)S(1)} %get-tuple-element.43.refs_18_), channel_id=1, source_target_pairs={{0,1},{1,0},{2,3},{3,2},{4,5},{5,4},{6,7},{7,6},{8,16},{9,17},{10,... | collective-permute-start | bytes 786440 | tf_op jit(solution)/shard_map/b2/ppermute | solution.py:118
  39.7 16.9 %collective-permute-start.18 = (bf16[256,512]{1,0:T(8,128)(2,1)S(1)}, bf16[256,512]{1,0:T(8,128)(2,1)S(1)}, u32[]{:S(2)}, u32[]{:S(2)}) collective-permute-start(bf16[256,512]{1,0:T(8,128)(2,1)S(1)} %collective-permute-done.12.refs_9_), channel_id=1, source_target_pairs={{0,8},{1,9},{2,10},{3,11},{4,12},{5,13},{6,14},{7,15},{8,0},{9,1},... | collective-permute-start | bytes 786440 | tf_op jit(solution)/shard_map/e1/ppermute | solution.py:118
  46.3 15.9 %collective-permute-start.17 = (bf16[256,512]{1,0:T(8,128)(2,1)S(1)}, bf16[256,512]{1,0:T(8,128)(2,1)S(1)}, u32[]{:S(2)}, u32[]{:S(2)}) collective-permute-start(bf16[256,512]{1,0:T(8,128)(2,1)S(1)} %collective-permute-done.11.refs_8_), channel_id=1, source_target_pairs={{0,8},{1,9},{2,10},{3,11},{4,12},{5,13},{6,14},{7,15},{8,0},{9,1},... | collective-permute-start | bytes 786440 | tf_op jit(solution)/shard_map/e0/ppermute | solution.py:118
  50.9 11.2 %collective-permute-start.14 = (bf16[256,512]{1,0:T(8,128)(2,1)S(1)}, bf16[256,512]{1,0:T(8,128)(2,1)S(1)}, u32[]{:S(2)}, u32[]{:S(2)}) collective-permute-start(bf16[256,512]{1,0:T(8,128)(2,1)S(1)} %collective-permute-done.8.refs_3_), channel_id=1, source_target_pairs={{0,1},{1,0},{2,3},{3,2},{4,5},{5,4},{6,7},{7,6},{8,16},{9,17},{10,... | collective-permute-start | bytes 786440 | tf_op jit(solution)/shard_map/c3/ppermute | solution.py:118
  50.9 11.2 %collective-permute-start.13 = (bf16[256,512]{1,0:T(8,128)(2,1)S(1)}, bf16[256,512]{1,0:T(8,128)(2,1)S(1)}, u32[]{:S(2)}, u32[]{:S(2)}) collective-permute-start(bf16[256,512]{1,0:T(8,128)(2,1)S(1)} %collective-permute-done.7.refs_2_), channel_id=1, source_target_pairs={{0,1},{1,0},{2,3},{3,2},{4,5},{5,4},{6,7},{7,6},{8,16},{9,17},{10,... | collective-permute-start | bytes 786440 | tf_op jit(solution)/shard_map/c2/ppermute | solution.py:118
  51.4 14.9 %collective-permute-start.16 = (bf16[256,512]{1,0:T(8,128)(2,1)S(1)}, bf16[256,512]{1,0:T(8,128)(2,1)S(1)}, u32[]{:S(2)}, u32[]{:S(2)}) collective-permute-start(bf16[256,512]{1,0:T(8,128)(2,1)S(1)} %collective-permute-done.10.refs_7_), channel_id=1, source_target_pairs={{0,8},{1,9},{2,10},{3,11},{4,12},{5,13},{6,14},{7,15},{8,0},{9,1},... | collective-permute-start | bytes 786440 | tf_op jit(solution)/shard_map/d1/ppermute | solution.py:118
  66.8 9.2 %collective-permute-start.23 = (bf16[256,512]{1,0:T(8,128)(2,1)S(1)}, bf16[256,512]{1,0:T(8,128)(2,1)S(1)}, u32[]{:S(2)}, u32[]{:S(2)}) collective-permute-start(bf16[256,512]{1,0:T(8,128)(2,1)S(1)} %collective-permute-done.14.refs_11_), channel_id=1, source_target_pairs={{0,2},{1,9},{2,0},{3,11},{4,6},{5,13},{6,4},{7,15},{8,10},{9,1},{1... | collective-permute-start | bytes 786440 | tf_op jit(solution)/shard_map/last/ppermute | solution.py:118
  68.4 8.4 %collective-permute-start.24 = (bf16[256,512]{1,0:T(8,128)(2,1)S(1)}, bf16[256,512]{1,0:T(8,128)(2,1)S(1)}, u32[]{:S(2)}, u32[]{:S(2)}) collective-permute-start(bf16[256,512]{1,0:T(8,128)(2,1)S(1)} %collective-permute-done.14.refs_11_), channel_id=1, source_target_pairs={{0,2},{1,8},{2,0},{3,10},{4,6},{5,12},{6,4},{7,14},{8,1},{9,11},{1... | collective-permute-start | bytes 786440 | tf_op jit(solution)/shard_map/last/ppermute | solution.py:118
  72.5 10.0 %collective-permute-start.22 = (bf16[512,256]{1,0:T(8,128)(2,1)S(1)}, bf16[512,256]{1,0:T(8,128)(2,1)S(1)}, u32[]{:S(2)}, u32[]{:S(2)}) collective-permute-start(bf16[512,256]{1,0:T(8,128)(2,1)S(1)} %get-tuple-element.51), channel_id=1, source_target_pairs={{0,2},{1,3},{2,0},{3,1},{4,6},{5,7},{6,4},{7,5},{8,10},{9,11},{10,... | collective-permute-start | bytes 786440 | tf_op jit(solution)/shard_map/ppermute | solution.py:118
  74.0 20.4 %collective-permute-start.20 = (bf16[512,256]{1,0:T(8,128)(2,1)S(1)}, bf16[512,256]{1,0:T(8,128)(2,1)S(1)}, u32[]{:S(2)}, u32[]{:S(2)}) collective-permute-start(bf16[512,256]{1,0:T(8,128)(2,1)S(1)} %get-tuple-element.49), channel_id=1, source_target_pairs={{0,4},{1,5},{2,6},{3,7},{4,0},{5,1},{6,2},{7,3},{8,12},{9,13},{10,... | collective-permute-start | bytes 786440 | tf_op jit(solution)/shard_map/ppermute | solution.py:118
  74.5 19.9 %collective-permute-start.21 = (bf16[512,256]{1,0:T(8,128)(2,1)S(1)}, bf16[512,256]{1,0:T(8,128)(2,1)S(1)}, u32[]{:S(2)}, u32[]{:S(2)}) collective-permute-start(bf16[512,256]{1,0:T(8,128)(2,1)S(1)} %get-tuple-element.50), channel_id=1, source_target_pairs={{0,6},{1,7},{2,4},{3,5},{4,2},{5,3},{6,0},{7,1},{8,14},{9,15},{10,... | collective-permute-start | bytes 786440 | tf_op jit(solution)/shard_map/ppermute | solution.py:118
  78.4 20.6 %collective-permute-start.25 = (bf16[512,256]{1,0:T(8,128)(2,1)S(1)}, bf16[512,256]{1,0:T(8,128)(2,1)S(1)}, u32[]{:S(2)}, u32[]{:S(2)}) collective-permute-start(bf16[512,256]{1,0:T(8,128)(2,1)S(1)} %get-tuple-element.53), channel_id=1, source_target_pairs={{0,4},{1,5},{2,6},{3,7},{4,0},{5,1},{6,2},{7,3},{8,12},{9,13},{10,... | collective-permute-start | bytes 786440 | tf_op jit(solution)/shard_map/ppermute | solution.py:118
  79.0 20.0 %collective-permute-start.26 = (bf16[512,256]{1,0:T(8,128)(2,1)S(1)}, bf16[512,256]{1,0:T(8,128)(2,1)S(1)}, u32[]{:S(2)}, u32[]{:S(2)}) collective-permute-start(bf16[512,256]{1,0:T(8,128)(2,1)S(1)} %get-tuple-element.54), channel_id=1, source_target_pairs={{0,6},{1,7},{2,4},{3,5},{4,2},{5,3},{6,0},{7,1},{8,14},{9,15},{10,... | collective-permute-start | bytes 786440 | tf_op jit(solution)/shard_map/ppermute | solution.py:118
  82.4 16.5 %collective-permute-start.27 = (bf16[512,256]{1,0:T(8,128)(2,1)S(1)}, bf16[512,256]{1,0:T(8,128)(2,1)S(1)}, u32[]{:S(2)}, u32[]{:S(2)}) collective-permute-start(bf16[512,256]{1,0:T(8,128)(2,1)S(1)} %get-tuple-element.56), channel_id=1, source_target_pairs={{0,2},{1,3},{2,0},{3,1},{4,6},{5,7},{6,4},{7,5},{8,10},{9,11},{10,... | collective-permute-start | bytes 786440 | tf_op jit(solution)/shard_map/ppermute | solution.py:118
  (10 other events, 29.9 us)

commit v4 on v3

--- a/solution.py
+++ b/solution.py
@@ -13,7 +13,7 @@
 ROUNDS = 4
 PAIR_ROWS = 128
 NZ, NY, NX, NC = 4, 2, 2, 2
-WINDOW = 9
+AFTER = {"a2": ("e1",), "c0": ("d0",), "c1": ("a2",), "d1": ("a3",), "first_d": ("b2", "y2", "e1",), "m2": ("a0", "b0",), "p_b0": ("a0",), "pp2": ("e1",), "second_d": ("pp2",), "second_x": ("l0",), "y2": ("y0",)}
 VMEM_LIMIT = 40 * 1024 * 1024
 FIRST_LIMIT = 62 * 1024 * 1024
 BOTH = ("panel", "feat")
@@ -306,7 +306,7 @@
 
 def collect_kernel(names, whole, split, *refs):
     pieces = dict(zip(names, refs))
-    send_ref, keep_ref, sems = refs[len(names) :]
+    send_ref, later_ref, keep_ref, sems = refs[len(names) :]
     z, _, _, c = place()
     for zz in range(NZ):
         for cc in range(NC):
@@ -323,7 +323,8 @@
                             target = keep_ref.at[kept]
                             kept += 1
                         else:
-                            target = send_ref.at[sent]
+                            room = send_ref.shape[0]
+                            target = send_ref.at[sent] if sent < room else later_ref.at[sent - room]
                             sent += 1
                         if name != LAST:
                             copies.append((pieces[name], target))
@@ -336,14 +337,14 @@
                     copy.wait()
 
 
-def tile_kernel(tiles, sent_ref, far_ref, kept_ref, *refs):
-    mine_ref, x_ref, y_ref, d_ref = refs[2:6] if len(refs) > 4 else refs
+def tile_kernel(tiles, mine, sent_ref, far_ref, kept_ref, *refs):
+    *lasts, here_ref, there_ref = refs[:2] if len(refs) == 2 else refs[:5]
     z, y, x, c = place()
     depth = sent_ref.shape[2]
     nt = (((1,), (1,)), ((), ()))
-    if len(refs) > 4:
-        last_ref, last_far_ref = refs[:2]
-        near2_ref, far2_ref = refs[6:]
+    if lasts:
+        last_ref, last_far_ref, far_later_ref = lasts
+        near2_ref, far2_ref = refs[5:]
         for part in range(2):
             here = ((z == 0) & (c == 1)) if part == 1 else ((z == 3) & (c == 0))
 
@@ -355,7 +356,7 @@
             @pl.when(jnp.logical_not(here))
             def _(part=part):
                 near2_ref[part] = kept_ref[2 + part]
-                far2_ref[part] = far_ref[NZ + 2 + part]
+                far2_ref[part] = far_later_ref[part]
 
     def rows_of(ref, p):
         return ref[0:NZ, pl.ds(p * PAIR_ROWS, PAIR_ROWS), :].reshape(P_SIZE, depth)
@@ -369,32 +370,35 @@
         return (near2_ref if near else far2_ref)[part, rows, :]
 
     for p in range(2):
-        for mine in (True, False):
-
-            @pl.when((y == p) if mine else (y != p))
-            def _(p=p, mine=mine):
-                left, left_far = rows_of(sent_ref, p), rows_of(far_ref, p)
-                for part, out_ref in ((x, mine_ref if mine else y_ref), (1 - x, x_ref if mine else d_ref)):
-                    near = jnp.concatenate([columns_of(d, q, part, True) for d, q in tiles[p]], axis=0)
-                    far = jnp.concatenate([columns_of(d, q, part, False) for d, q in tiles[p]], axis=0)
-                    total = lax.dot_general(left, near, nt, preferred_element_type=jnp.float32) + lax.dot_general(
-                        left_far, far, nt, preferred_element_type=jnp.float32
-                    )
-                    out_ref[...] = total.astype(out_ref.dtype)
+
+        @pl.when((y == p) if mine else (y != p))
+        def _(p=p):
+            left, left_far = rows_of(sent_ref, p), rows_of(far_ref, p)
+            for part, out_ref in ((x, here_ref), (1 - x, there_ref)):
+                near = jnp.concatenate([columns_of(d, q, part, True) for d, q in tiles[p]], axis=0)
+                far = jnp.concatenate([columns_of(d, q, part, False) for d, q in tiles[p]], axis=0)
+                total = lax.dot_general(left, near, nt, preferred_element_type=jnp.float32) + lax.dot_general(
+                    left_far, far, nt, preferred_element_type=jnp.float32
+                )
+                out_ref[...] = total.astype(out_ref.dtype)
 
 
 def plane_tiles(tiles, sent, far, kept, *last):
     columns = len(tiles[0]) * PAIR_ROWS
     part = bf16(P_SIZE, columns)
     room = (2, *sent.shape[1:])
-    mine, x_part, y_part, d_part = call(
-        functools.partial(tile_kernel, tiles),
-        (jax.ShapeDtypeStruct((P_SIZE, columns), jnp.float32), part, part, part),
-        [IN_VMEM] * (3 + len(last)),
-        (IN_VMEM,) * 4,
-        (2 * 4 * P_SIZE * columns * 2 * sent.shape[2], 8 * 1024 * 1024),
-        (pltpu.VMEM(room, jnp.bfloat16),) * 2 if last else (),
-    )(sent, far, kept, *last)
+
+    def half(mine):
+        return call(
+            functools.partial(tile_kernel, tiles, mine),
+            (jax.ShapeDtypeStruct(part.shape, jnp.float32) if mine else part, part),
+            [IN_VMEM] * (3 + len(last)),
+            (IN_VMEM,) * 2,
+            (2 * 2 * P_SIZE * columns * 2 * sent.shape[2], 8 * 1024 * 1024),
+            (pltpu.VMEM(room, jnp.bfloat16),) * 2 if last else (),
+        )(sent, far, kept, *last)
+
+    (y_part, d_part), (mine, x_part) = half(False), half(True)
     return mine, y_part, d_part, x_part
 
 
@@ -428,8 +432,18 @@
         ),
         FIRST_LIMIT,
     )(row_counts, assignment, center, weight, dosage)
-    with jax.named_scope("y0"):
-        came = [to_y(away)]
+    done = {}
+
+    def held(name, value):
+        first = [done[other] for other in AFTER.get(name, ()) if other in done]
+        return lax.optimization_barrier((value, *first))[0] if first else value
+
+    def move(name, send, value):
+        with jax.named_scope(name):
+            done[name] = send(held(name, value))
+        return done[name]
+
+    came = [move("y0", to_y, away)]
     own, *later = call(
         functools.partial(rest_kernel, slots),
         (bf16(capacity, half),) + tuple(bf16(n, half) for n in chunk_rows[1:]),
@@ -437,32 +451,21 @@
         (IN_VMEM,) * len(CHUNKS),
         (2 * capacity * capacity * width, 3 * capacity * width),
     )(slot, rows, center, weight, dosage)
-    for k, away in enumerate(later):
-        with jax.named_scope("y%d" % (k + 1)):
-            if k >= 1:
-                away, _ = lax.optimization_barrier((away, came[k - 1]))
-            came.append(to_y(away))
+    for k, away in enumerate(later, 1):
+        came.append(move("y%d" % k, to_y, away))
     pieces = {}
     z = lax.axis_index("panel") // NY
 
-    queues = {z_ends: [], z_middle: []}
-
-    def swap(move, name, value):
-        before = queues[move]
-        if len(before) >= WINDOW:
-            value, _ = lax.optimization_barrier((value, pieces[before[-WINDOW]]))
-        with jax.named_scope(name):
-            pieces[name] = move(value)
-        before.append(name)
-
-    ends = functools.partial(swap, z_ends)
-    middle = functools.partial(swap, z_middle)
+    def ends(name, value):
+        pieces[name] = move(name, z_ends, value)
+
+    def middle(name, value):
+        pieces[name] = move(name, z_middle, value)
 
     for chunk, other in zip(CHUNKS, came):
         if pieces:
             other, _ = lax.optimization_barrier((other, merged[-1]))
-        if len(chunk) == 2:
-            other, _, _ = lax.optimization_barrier((other, pieces["a0"], pieces["b0"]))
+        other = held("m%d" % chunk[0], other)
         merged = call(
             functools.partial(merge_kernel, slots, chunk),
             (bf16(group_rows, half),) * len(chunk),
@@ -476,14 +479,20 @@
                 ends("a%d" % step, piece)
             middle("b%d" % step, piece)
 
+    pieces["b0"] = held("p_b0", pieces["b0"])
     ends("a3", jnp.where((z == 0) | (z == 3), pieces["o3"], pieces["b0"]))
     pieces["a1"], pieces["b1"], _, _ = lax.optimization_barrier((pieces["a1"], pieces["b1"], pieces["a0"], pieces["b0"]))
-    for k in range(NZ):
-        middle("c%d" % k, pieces["a%d" % k])
-    for name, passed in (("d0", "b1"), ("d1", "b3"), ("e0", "c0"), ("e1", "c1")):
-        ends(name, pieces[passed])
-    with jax.named_scope("last"):
-        last = z_last(pieces["c3"], False), z_last(pieces["c3"], True)
+    middle("c1", pieces["a1"])
+    middle("c0", pieces["a0"])
+    middle("c2", pieces["a2"])
+    ends("d0", pieces["b1"])
+    middle("c3", pieces["a3"])
+    ends("e0", pieces["c0"])
+    ends("d1", pieces["b3"])
+    ends("e1", pieces["c1"])
+    last = [
+        move("l%d" % far, lambda value, far=far: z_last(value, far), pieces["c3"]) for far in (False, True)
+    ]
 
     names = set()
     for plane in range(NZ):
@@ -492,24 +501,29 @@
             names.add("o%d" % ORDER[plane].index(g))
             names.update(FOUND[plane][s][g] for s in range(NZ) if s != plane)
     names = sorted(names - {LAST})
-    sent, kept = call(
+    sent, sent_later, kept = call(
         functools.partial(collect_kernel, names, (0,), (1, 2)),
-        (bf16(2 * NZ, group_rows, half), bf16(NZ, group_rows, half)),
+        (bf16(NZ + 2, group_rows, half), bf16(2, group_rows, half), bf16(NZ, group_rows, half)),
         [ANYWHERE] * len(names),
-        (ANYWHERE, ANYWHERE),
+        (ANYWHERE,) * 3,
         (0, 4 * 3 * NZ * group_rows * half),
         (pltpu.SemaphoreType.DMA((3 * NZ,)),),
     )(*[pieces[name] for name in names])
-    far = to_core(sent)
+    far = move("pp", to_core, sent)
+    far_later = move("pp2", to_core, sent_later)
     first = plane_tiles((((1, 1), (1, 0)), ((0, 0), (1, 1))), sent, far, kept)
-    second = plane_tiles((((2, 1), (2, 0)), ((1, 0), (2, 1))), sent, far, kept, *last)
-
-    def exchanged(mine, y_part, d_part, x_part):
-        return mine, to_y(y_part), to_diagonal(d_part), to_x(x_part)
-
-    first = exchanged(*first)
-    x_part, _ = lax.optimization_barrier((second[3], first[3]))
-    second = exchanged(*second[:3], x_part)
+    second = plane_tiles((((2, 1), (2, 0)), ((1, 0), (2, 1))), sent, far, kept, *last, far_later)
+
+    def exchanged(name, mine, y_part, d_part, x_part):
+        return (
+            mine,
+            move(name + "y", to_y, y_part),
+            move(name + "d", to_diagonal, d_part),
+            move(name + "x", to_x, x_part),
+        )
+
+    first = exchanged("first_", *first)
+    second = exchanged("second_", *second)
 
     def total(parts):
         mine, *others = parts

time: 101 us -> 97.9 us (0.969)
  local copies, waits for them, and re-layouts: 5.33 us -> 2.41 us
  waiting for transfers between devices: 42.7 us -> 40.6 us
  starting transfers between devices: 39.6 us -> 41.2 us
    unnamed x12, local copies, waits for them, and re-layouts: 4.79 us -> 1.86 us
    ppermute x28 -> x29, waiting for transfers between devices: 42.7 us -> 40.6 us  [hop(): return lax.ppermute(value, BOTH, pairs)]
    ppermute x28 -> x29, starting transfers between devices: 39.6 us -> 41.2 us  [hop(): return lax.ppermute(value, BOTH, pairs)]
    pallas_call x3 -> x5, Pallas kernels: 3.4 us -> 3.46 us  [the longest x4 3.1 us: half(): call(functools.partial(tile_kernel, tiles, mine), (jax.ShapeDtypeStruct(p...]
  transfers between devices with their start and end apart: 28 -> 29, of which waited for: 11 -> 14; matrix products, arithmetic and copies ran while one was open for 0% -> 0% of each run, Pallas kernels for 8% -> 8%
where the time goes in v4:
time: 97.9 us; the launch traced here: 97.7 us
  starting transfers between devices  41.2 us (42%)
  waiting for transfers between devices  40.6 us (41%)
  Pallas kernels  10.7 us (11%)
  local copies, waits for them, and re-layouts  2.41 us (2%)
  other arithmetic  1.75 us (2%)
    ppermute x29, starting transfers between devices, hop(): return lax.ppermute(value, BOTH, pairs)  41.2 us
    ppermute x29, waiting for transfers between devices, hop(): return lax.ppermute(value, BOTH, pairs)  40.6 us
    pallas_call x4, Pallas kernels, half(): call(functools.partial(tile_kernel, tiles, mine), (jax.ShapeDtypeStruct(p...  3.1 us
    pallas_call x3, Pallas kernels, plane_shards(): call(functools.partial(merge_kernel, slots, chunk), (bf16(group_rows, hal...  2.8 us
    pallas_call x1, Pallas kernels, plane_shards(): call(functools.partial(first_kernel, slots), (jax.ShapeDtypeStruct((1, ca...  2.6 us
  transfers between devices with their start and end apart: 29, of which 14 were waited for; matrix products, arithmetic and copies ran while one was open for 0% of the time, Pallas kernels for 8%

profile of v4, /device:TPU:0, one launch (start us, length us, event | category | flops | bytes accessed | tf_op | source)
XLA Modules:
  0.0 97.7 jit_solution(17365702822734343596)
XLA Ops:
  0.8 2.6 %first_kernel.1 = (s32[1,896]{1,0:T(1,128)}, s32[8,128]{1,0:T(8,128)}, bf16[896,512]{1,0:T(8,128)(2,1)}, bf16[224,512]{1,0:T(8,128)(2,1)}) custom-call(s32[1]{0:T(128)S(6)} %copy.6.count_ref, s32[896]{0:T(1024)} %assign_hbm.1, f32[1,4096]{1,0:T(1,128)} %bitcast.2, f32[1,4096]{1,0:T(1,128)} %bitcast.4, bf16[896,1024]{1,0:T(8,128)(2,1)} %dosage_ref.1), custom_call_target="tpu_custom_call" | custom-call | flops 205520896 | bytes 2752512 | tf_op jit(solution)/shard_map/first_kernel/pallas_call | solution.py:415
  3.4 3.0 %collective-permute-start = (bf16[224,512]{1,0:T(8,128)(2,1)}, bf16[224,512]{1,0:T(8,128)(2,1)S(1)}, u32[]{:S(2)}, u32[]{:S(2)}) collective-permute-start(bf16[224,512]{1,0:T(8,128)(2,1)} %get-tuple-element.42), channel_id=1, source_target_pairs={{0,4},{1,5},{2,6},{3,7},{4,0},{5,1},{6,2},{7,3},{8,12},{9,13},{10,... | collective-permute-start | bytes 688136 | tf_op jit(solution)/shard_map/y0/ppermute | solution.py:118
  8.3 1.9 %rest_kernel.1 = (bf16[896,512]{1,0:T(8,128)(2,1)S(1)}, bf16[224,512]{1,0:T(8,128)(2,1)S(1)}, bf16[448,512]{1,0:T(8,128)(2,1)S(1)}) custom-call(s32[1,896]{1,0:T(1,128)S(1)} %copy-done.5, bf16[896,512]{1,0:T(8,128)(2,1)S(1)} %copy-done.4, f32[1,4096]{1,0:T(1,128)S(1)} %bitcast.3, f32[1,4096]{1,0:T(1,128)S(1)} %bitcast.5, bf16[896,1024]{1,0:T(8,128)(2,1)S(1)} %copy-done), custom_call_target="tpu_custom_call" | custom-call | flops 1644167168 | bytes 2752512 | tf_op jit(solution)/shard_map/rest_kernel/pallas_call | solution.py:447
  10.3 2.5 %collective-permute-done.other_ref = bf16[224,512]{1,0:T(8,128)(2,1)S(1)} collective-permute-done((bf16[224,512]{1,0:T(8,128)(2,1)}, bf16[224,512]{1,0:T(8,128)(2,1)S(1)}, u32[]{:S(2)}, u32[]{:S(2)}) %collective-permute-start) | collective-permute-done | bytes 229408 | tf_op jit(solution)/shard_map/y0/ppermute | solution.py:118
  12.8 2.4 %collective-permute-start.6 = (bf16[448,512]{1,0:T(8,128)(2,1)S(1)}, bf16[448,512]{1,0:T(8,128)(2,1)S(1)}, u32[]{:S(2)}, u32[]{:S(2)}) collective-permute-start(bf16[448,512]{1,0:T(8,128)(2,1)S(1)} %get-tuple-element.48), channel_id=1, source_target_pairs={{0,4},{1,5},{2,6},{3,7},{4,0},{5,1},{6,2},{7,3},{8,12},{9,13},{10,... | collective-permute-start | bytes 1376264 | tf_op jit(solution)/shard_map/y2/ppermute | solution.py:118
  16.0 1.5 %collective-permute-start.1 = (bf16[256,512]{1,0:T(8,128)(2,1)S(1)}, bf16[256,512]{1,0:T(8,128)(2,1)S(1)}, u32[]{:S(2)}, u32[]{:S(2)}) collective-permute-start(bf16[256,512]{1,0:T(8,128)(2,1)S(1)} %merge_kernel.3.refs_16_), channel_id=1, source_target_pairs={{0,8},{1,9},{2,10},{3,11},{4,12},{5,13},{6,14},{7,15},{8,0},{9,1},... | collective-permute-start | bytes 786440 | tf_op jit(solution)/shard_map/a0/ppermute | solution.py:118
  19.7 2.0 %collective-permute-start.3 = (bf16[256,512]{1,0:T(8,128)(2,1)S(1)}, bf16[256,512]{1,0:T(8,128)(2,1)S(1)}, u32[]{:S(2)}, u32[]{:S(2)}) collective-permute-start(bf16[256,512]{1,0:T(8,128)(2,1)S(1)} %merge_kernel.4.refs_17_), channel_id=1, source_target_pairs={{0,8},{1,9},{2,10},{3,11},{4,12},{5,13},{6,14},{7,15},{8,0},{9,1},... | collective-permute-start | bytes 786440 | tf_op jit(solution)/shard_map/a1/ppermute | solution.py:118
  21.7 5.5 %collective-permute-done.6.other_ref = bf16[448,512]{1,0:T(8,128)(2,1)S(1)} collective-permute-done((bf16[448,512]{1,0:T(8,128)(2,1)S(1)}, bf16[448,512]{1,0:T(8,128)(2,1)S(1)}, u32[]{:S(2)}, u32[]{:S(2)}) %collective-permute-start.6) | collective-permute-done | bytes 458784 | tf_op jit(solution)/shard_map/y2/ppermute | solution.py:118
  28.2 1.7 %collective-permute-start.7 = (bf16[256,512]{1,0:T(8,128)(2,1)S(1)}, bf16[256,512]{1,0:T(8,128)(2,1)S(1)}, u32[]{:S(2)}, u32[]{:S(2)}) collective-permute-start(bf16[256,512]{1,0:T(8,128)(2,1)S(1)} %get-tuple-element.51.refs_18_), channel_id=1, source_target_pairs={{0,8},{1,9},{2,10},{3,11},{4,12},{5,13},{6,14},{7,15},{8,0},{9,1},... | collective-permute-start | bytes 786440 | tf_op jit(solution)/shard_map/a2/ppermute | solution.py:118
  29.9 3.2 %collective-permute-start.8 = (bf16[256,512]{1,0:T(8,128)(2,1)S(1)}, bf16[256,512]{1,0:T(8,128)(2,1)S(1)}, u32[]{:S(2)}, u32[]{:S(2)}) collective-permute-start(bf16[256,512]{1,0:T(8,128)(2,1)S(1)} %broadcast_select_fusion), channel_id=1, source_target_pairs={{0,8},{1,9},{2,10},{3,11},{4,12},{5,13},{6,14},{7,15},{8,0},{9,1},... | collective-permute-start | bytes 786440 | tf_op jit(solution)/shard_map/a3/ppermute | solution.py:118
  33.6 3.4 %collective-permute-done.7.refs_2_ = bf16[256,512]{1,0:T(8,128)(2,1)S(1)} collective-permute-done((bf16[256,512]{1,0:T(8,128)(2,1)S(1)}, bf16[256,512]{1,0:T(8,128)(2,1)S(1)}, u32[]{:S(2)}, u32[]{:S(2)}) %collective-permute-start.7) | collective-permute-done | bytes 262176 | tf_op jit(solution)/shard_map/a2/ppermute | solution.py:118
  37.6 5.1 %collective-permute-done.8.refs_3_ = bf16[256,512]{1,0:T(8,128)(2,1)S(1)} collective-permute-done((bf16[256,512]{1,0:T(8,128)(2,1)S(1)}, bf16[256,512]{1,0:T(8,128)(2,1)S(1)}, u32[]{:S(2)}, u32[]{:S(2)}) %collective-permute-start.8) | collective-permute-done | bytes 262176 | tf_op jit(solution)/shard_map/a3/ppermute | solution.py:118
  42.7 2.1 %collective-permute-start.17 = (bf16[256,512]{1,0:T(8,128)(2,1)S(1)}, bf16[256,512]{1,0:T(8,128)(2,1)S(1)}, u32[]{:S(2)}, u32[]{:S(2)}) collective-permute-start(bf16[256,512]{1,0:T(8,128)(2,1)S(1)} %collective-permute-done.11.refs_8_), channel_id=1, source_target_pairs={{0,8},{1,9},{2,10},{3,11},{4,12},{5,13},{6,14},{7,15},{8,0},{9,1},... | collective-permute-start | bytes 786440 | tf_op jit(solution)/shard_map/e0/ppermute | solution.py:118
  45.9 2.4 %collective-permute-done.15.refs_12_ = bf16[256,512]{1,0:T(8,128)(2,1)S(1)} collective-permute-done((bf16[256,512]{1,0:T(8,128)(2,1)S(1)}, bf16[256,512]{1,0:T(8,128)(2,1)S(1)}, u32[]{:S(2)}, u32[]{:S(2)}) %collective-permute-start.15) | collective-permute-done | bytes 262176 | tf_op jit(solution)/shard_map/d0/ppermute | solution.py:118
  48.8 8.3 %collective-permute-start.18 = (bf16[256,512]{1,0:T(8,128)(2,1)S(1)}, bf16[256,512]{1,0:T(8,128)(2,1)S(1)}, u32[]{:S(2)}, u32[]{:S(2)}) collective-permute-start(bf16[256,512]{1,0:T(8,128)(2,1)S(1)} %collective-permute-done.12.refs_9_), channel_id=1, source_target_pairs={{0,8},{1,9},{2,10},{3,11},{4,12},{5,13},{6,14},{7,15},{8,0},{9,1},... | collective-permute-start | bytes 786440 | tf_op jit(solution)/shard_map/e1/ppermute | solution.py:118
  57.1 2.4 %collective-permute-done.16.refs_13_ = bf16[256,512]{1,0:T(8,128)(2,1)S(1)} collective-permute-done((bf16[256,512]{1,0:T(8,128)(2,1)S(1)}, bf16[256,512]{1,0:T(8,128)(2,1)S(1)}, u32[]{:S(2)}, u32[]{:S(2)}) %collective-permute-start.16) | collective-permute-done | bytes 262176 | tf_op jit(solution)/shard_map/d1/ppermute | solution.py:118
  59.5 3.7 %collective-permute-done.18.refs_15_ = bf16[256,512]{1,0:T(8,128)(2,1)S(1)} collective-permute-done((bf16[256,512]{1,0:T(8,128)(2,1)S(1)}, bf16[256,512]{1,0:T(8,128)(2,1)S(1)}, u32[]{:S(2)}, u32[]{:S(2)}) %collective-permute-start.18) | collective-permute-done | bytes 262176 | tf_op jit(solution)/shard_map/e1/ppermute | solution.py:118
  64.1 1.7 %collective-permute-start.23 = (bf16[256,512]{1,0:T(8,128)(2,1)S(1)}, bf16[256,512]{1,0:T(8,128)(2,1)S(1)}, u32[]{:S(2)}, u32[]{:S(2)}) collective-permute-start(bf16[256,512]{1,0:T(8,128)(2,1)S(1)} %collective-permute-done.14.refs_11_), channel_id=1, source_target_pairs={{0,2},{1,9},{2,0},{3,11},{4,6},{5,13},{6,4},{7,15},{8,10},{9,1},{1... | collective-permute-start | bytes 786440 | tf_op jit(solution)/shard_map/l0/ppermute | solution.py:118
  67.8 3.0 %collective-permute-start.21 = (bf16[512,256]{1,0:T(8,128)(2,1)S(1)}, bf16[512,256]{1,0:T(8,128)(2,1)S(1)}, u32[]{:S(2)}, u32[]{:S(2)}) collective-permute-start(bf16[512,256]{1,0:T(8,128)(2,1)S(1)} %get-tuple-element.61), channel_id=1, source_target_pairs={{0,6},{1,7},{2,4},{3,5},{4,2},{5,3},{6,0},{7,1},{8,14},{9,15},{10,... | collective-permute-start | bytes 786440 | tf_op jit(solution)/shard_map/first_d/ppermute | solution.py:118
  74.4 5.4 %collective-permute-start.27 = (bf16[512,256]{1,0:T(8,128)(2,1)S(1)}, bf16[512,256]{1,0:T(8,128)(2,1)S(1)}, u32[]{:S(2)}, u32[]{:S(2)}) collective-permute-start(bf16[512,256]{1,0:T(8,128)(2,1)S(1)} %get-tuple-element.68), channel_id=1, source_target_pairs={{0,6},{1,7},{2,4},{3,5},{4,2},{5,3},{6,0},{7,1},{8,14},{9,15},{10,... | collective-permute-start | bytes 786440 | tf_op jit(solution)/shard_map/second_d/ppermute | solution.py:118
  82.0 2.5 %collective-permute-start.28 = (bf16[512,256]{1,0:T(8,128)(2,1)S(1)}, bf16[512,256]{1,0:T(8,128)(2,1)S(1)}, u32[]{:S(2)}, u32[]{:S(2)}) collective-permute-start(bf16[512,256]{1,0:T(8,128)(2,1)S(1)} %get-tuple-element.70), channel_id=1, source_target_pairs={{0,2},{1,3},{2,0},{3,1},{4,6},{5,7},{6,4},{7,5},{8,10},{9,11},{10,... | collective-permute-start | bytes 786440 | tf_op jit(solution)/shard_map/second_x/ppermute | solution.py:118
  85.9 7.4 %collective-permute-done.27 = bf16[512,256]{1,0:T(8,128)(2,1)S(1)} collective-permute-done((bf16[512,256]{1,0:T(8,128)(2,1)S(1)}, bf16[512,256]{1,0:T(8,128)(2,1)S(1)}, u32[]{:S(2)}, u32[]{:S(2)}) %collective-permute-start.27) | collective-permute-done | bytes 262176 | tf_op jit(solution)/shard_map/second_d/ppermute | solution.py:118
  93.3 2.5 %collective-permute-done.26 = bf16[512,256]{1,0:T(8,128)(2,1)S(1)} collective-permute-done((bf16[512,256]{1,0:T(8,128)(2,1)S(1)}, bf16[512,256]{1,0:T(8,128)(2,1)S(1)}, u32[]{:S(2)}, u32[]{:S(2)}) %collective-permute-start.26) | collective-permute-done | bytes 262176 | tf_op jit(solution)/shard_map/second_y/ppermute | solution.py:118
  96.2 1.5 %maximum_multiply_fusion = f32[512,4,128]{2,1,0:T(4,128)} fusion(f32[512,2,128]{2,1,0:T(2,128)S(1)} %reshape.15, f32[512,2,128]{2,1,0:T(2,128)S(1)} %reshape.14), kind=kLoop, calls=%fused_computation | loop fusion | flops 524288 | bytes 2097152 | tf_op jit(solution)/shard_map/mul | solution.py:534
  (62 shorter events, 19.1 us)
Async XLA Ops:
  3.4 9.4 %collective-permute-start = (bf16[224,512]{1,0:T(8,128)(2,1)}, bf16[224,512]{1,0:T(8,128)(2,1)S(1)}, u32[]{:S(2)}, u32[]{:S(2)}) collective-permute-start(bf16[224,512]{1,0:T(8,128)(2,1)} %get-tuple-element.42), channel_id=1, source_target_pairs={{0,4},{1,5},{2,6},{3,7},{4,0},{5,1},{6,2},{7,3},{8,12},{9,13},{10,... | collective-permute-start | bytes 688136 | tf_op jit(solution)/shard_map/y0/ppermute | solution.py:118
  10.2 8.6 %collective-permute-start.2 = (bf16[224,512]{1,0:T(8,128)(2,1)S(1)}, bf16[224,512]{1,0:T(8,128)(2,1)S(1)}, u32[]{:S(2)}, u32[]{:S(2)}) collective-permute-start(bf16[224,512]{1,0:T(8,128)(2,1)S(1)} %get-tuple-element.43), channel_id=1, source_target_pairs={{0,4},{1,5},{2,6},{3,7},{4,0},{5,1},{6,2},{7,3},{8,12},{9,13},{10,... | collective-permute-start | bytes 688136 | tf_op jit(solution)/shard_map/y1/ppermute | solution.py:118
  12.8 14.4 %collective-permute-start.6 = (bf16[448,512]{1,0:T(8,128)(2,1)S(1)}, bf16[448,512]{1,0:T(8,128)(2,1)S(1)}, u32[]{:S(2)}, u32[]{:S(2)}) collective-permute-start(bf16[448,512]{1,0:T(8,128)(2,1)S(1)} %get-tuple-element.48), channel_id=1, source_target_pairs={{0,4},{1,5},{2,6},{3,7},{4,0},{5,1},{6,2},{7,3},{8,12},{9,13},{10,... | collective-permute-start | bytes 1376264 | tf_op jit(solution)/shard_map/y2/ppermute | solution.py:118
  16.0 11.1 %collective-permute-start.1 = (bf16[256,512]{1,0:T(8,128)(2,1)S(1)}, bf16[256,512]{1,0:T(8,128)(2,1)S(1)}, u32[]{:S(2)}, u32[]{:S(2)}) collective-permute-start(bf16[256,512]{1,0:T(8,128)(2,1)S(1)} %merge_kernel.3.refs_16_), channel_id=1, source_target_pairs={{0,8},{1,9},{2,10},{3,11},{4,12},{5,13},{6,14},{7,15},{8,0},{9,1},... | collective-permute-start | bytes 786440 | tf_op jit(solution)/shard_map/a0/ppermute | solution.py:118
  17.6 9.6 %collective-permute-start.5 = (bf16[256,512]{1,0:T(8,128)(2,1)S(1)}, bf16[256,512]{1,0:T(8,128)(2,1)S(1)}, u32[]{:S(2)}, u32[]{:S(2)}) collective-permute-start(bf16[256,512]{1,0:T(8,128)(2,1)S(1)} %merge_kernel.3.refs_16_), channel_id=1, source_target_pairs={{0,1},{1,0},{2,3},{3,2},{4,5},{5,4},{6,7},{7,6},{8,16},{9,17},{10,... | collective-permute-start | bytes 786440 | tf_op jit(solution)/shard_map/b0/ppermute | solution.py:118
  19.7 10.2 %collective-permute-start.3 = (bf16[256,512]{1,0:T(8,128)(2,1)S(1)}, bf16[256,512]{1,0:T(8,128)(2,1)S(1)}, u32[]{:S(2)}, u32[]{:S(2)}) collective-permute-start(bf16[256,512]{1,0:T(8,128)(2,1)S(1)} %merge_kernel.4.refs_17_), channel_id=1, source_target_pairs={{0,8},{1,9},{2,10},{3,11},{4,12},{5,13},{6,14},{7,15},{8,0},{9,1},... | collective-permute-start | bytes 786440 | tf_op jit(solution)/shard_map/a1/ppermute | solution.py:118
  28.2 8.9 %collective-permute-start.7 = (bf16[256,512]{1,0:T(8,128)(2,1)S(1)}, bf16[256,512]{1,0:T(8,128)(2,1)S(1)}, u32[]{:S(2)}, u32[]{:S(2)}) collective-permute-start(bf16[256,512]{1,0:T(8,128)(2,1)S(1)} %get-tuple-element.51.refs_18_), channel_id=1, source_target_pairs={{0,8},{1,9},{2,10},{3,11},{4,12},{5,13},{6,14},{7,15},{8,0},{9,1},... | collective-permute-start | bytes 786440 | tf_op jit(solution)/shard_map/a2/ppermute | solution.py:118
  29.9 12.7 %collective-permute-start.8 = (bf16[256,512]{1,0:T(8,128)(2,1)S(1)}, bf16[256,512]{1,0:T(8,128)(2,1)S(1)}, u32[]{:S(2)}, u32[]{:S(2)}) collective-permute-start(bf16[256,512]{1,0:T(8,128)(2,1)S(1)} %broadcast_select_fusion), channel_id=1, source_target_pairs={{0,8},{1,9},{2,10},{3,11},{4,12},{5,13},{6,14},{7,15},{8,0},{9,1},... | collective-permute-start | bytes 786440 | tf_op jit(solution)/shard_map/a3/ppermute | solution.py:118
  33.2 11.6 %collective-permute-start.10 = (bf16[256,512]{1,0:T(8,128)(2,1)S(1)}, bf16[256,512]{1,0:T(8,128)(2,1)S(1)}, u32[]{:S(2)}, u32[]{:S(2)}) collective-permute-start(bf16[256,512]{1,0:T(8,128)(2,1)S(1)} %get-tuple-element.52.refs_19_), channel_id=1, source_target_pairs={{0,1},{1,0},{2,3},{3,2},{4,5},{5,4},{6,7},{7,6},{8,16},{9,17},{10,... | collective-permute-start | bytes 786440 | tf_op jit(solution)/shard_map/b3/ppermute | solution.py:118
  33.2 15.1 %collective-permute-start.15 = (bf16[256,512]{1,0:T(8,128)(2,1)S(1)}, bf16[256,512]{1,0:T(8,128)(2,1)S(1)}, u32[]{:S(2)}, u32[]{:S(2)}) collective-permute-start(bf16[256,512]{1,0:T(8,128)(2,1)S(1)} %collective-permute-done.4.refs_5_), channel_id=1, source_target_pairs={{0,8},{1,9},{2,10},{3,11},{4,12},{5,13},{6,14},{7,15},{8,0},{9,1},... | collective-permute-start | bytes 786440 | tf_op jit(solution)/shard_map/d0/ppermute | solution.py:118
  37.0 11.2 %collective-permute-start.9 = (bf16[256,512]{1,0:T(8,128)(2,1)S(1)}, bf16[256,512]{1,0:T(8,128)(2,1)S(1)}, u32[]{:S(2)}, u32[]{:S(2)}) collective-permute-start(bf16[256,512]{1,0:T(8,128)(2,1)S(1)} %get-tuple-element.51.refs_18_), channel_id=1, source_target_pairs={{0,1},{1,0},{2,3},{3,2},{4,5},{5,4},{6,7},{7,6},{8,16},{9,17},{10,... | collective-permute-start | bytes 786440 | tf_op jit(solution)/shard_map/b2/ppermute | solution.py:118
  37.0 11.7 %collective-permute-start.12 = (bf16[256,512]{1,0:T(8,128)(2,1)S(1)}, bf16[256,512]{1,0:T(8,128)(2,1)S(1)}, u32[]{:S(2)}, u32[]{:S(2)}) collective-permute-start(bf16[256,512]{1,0:T(8,128)(2,1)S(1)} %collective-permute-done.3.refs_1_), channel_id=1, source_target_pairs={{0,1},{1,0},{2,3},{3,2},{4,5},{5,4},{6,7},{7,6},{8,16},{9,17},{10,... | collective-permute-start | bytes 786440 | tf_op jit(solution)/shard_map/c1/ppermute | solution.py:118
  42.7 14.5 %collective-permute-start.17 = (bf16[256,512]{1,0:T(8,128)(2,1)S(1)}, bf16[256,512]{1,0:T(8,128)(2,1)S(1)}, u32[]{:S(2)}, u32[]{:S(2)}) collective-permute-start(bf16[256,512]{1,0:T(8,128)(2,1)S(1)} %collective-permute-done.11.refs_8_), channel_id=1, source_target_pairs={{0,8},{1,9},{2,10},{3,11},{4,12},{5,13},{6,14},{7,15},{8,0},{9,1},... | collective-permute-start | bytes 786440 | tf_op jit(solution)/shard_map/e0/ppermute | solution.py:118
  44.8 14.7 %collective-permute-start.16 = (bf16[256,512]{1,0:T(8,128)(2,1)S(1)}, bf16[256,512]{1,0:T(8,128)(2,1)S(1)}, u32[]{:S(2)}, u32[]{:S(2)}) collective-permute-start(bf16[256,512]{1,0:T(8,128)(2,1)S(1)} %collective-permute-done.10.refs_7_), channel_id=1, source_target_pairs={{0,8},{1,9},{2,10},{3,11},{4,12},{5,13},{6,14},{7,15},{8,0},{9,1},... | collective-permute-start | bytes 786440 | tf_op jit(solution)/shard_map/d1/ppermute | solution.py:118
  48.3 11.2 %collective-permute-start.14 = (bf16[256,512]{1,0:T(8,128)(2,1)S(1)}, bf16[256,512]{1,0:T(8,128)(2,1)S(1)}, u32[]{:S(2)}, u32[]{:S(2)}) collective-permute-start(bf16[256,512]{1,0:T(8,128)(2,1)S(1)} %collective-permute-done.8.refs_3_), channel_id=1, source_target_pairs={{0,1},{1,0},{2,3},{3,2},{4,5},{5,4},{6,7},{7,6},{8,16},{9,17},{10,... | collective-permute-start | bytes 786440 | tf_op jit(solution)/shard_map/c3/ppermute | solution.py:118
  48.3 11.2 %collective-permute-start.13 = (bf16[256,512]{1,0:T(8,128)(2,1)S(1)}, bf16[256,512]{1,0:T(8,128)(2,1)S(1)}, u32[]{:S(2)}, u32[]{:S(2)}) collective-permute-start(bf16[256,512]{1,0:T(8,128)(2,1)S(1)} %collective-permute-done.7.refs_2_), channel_id=1, source_target_pairs={{0,1},{1,0},{2,3},{3,2},{4,5},{5,4},{6,7},{7,6},{8,16},{9,17},{10,... | collective-permute-start | bytes 786440 | tf_op jit(solution)/shard_map/c2/ppermute | solution.py:118
  48.8 14.4 %collective-permute-start.18 = (bf16[256,512]{1,0:T(8,128)(2,1)S(1)}, bf16[256,512]{1,0:T(8,128)(2,1)S(1)}, u32[]{:S(2)}, u32[]{:S(2)}) collective-permute-start(bf16[256,512]{1,0:T(8,128)(2,1)S(1)} %collective-permute-done.12.refs_9_), channel_id=1, source_target_pairs={{0,8},{1,9},{2,10},{3,11},{4,12},{5,13},{6,14},{7,15},{8,0},{9,1},... | collective-permute-start | bytes 786440 | tf_op jit(solution)/shard_map/e1/ppermute | solution.py:118
  63.6 9.9 %collective-permute-start.25 = (bf16[2,256,512]{2,1,0:T(8,128)(2,1)S(1)}, bf16[2,256,512]{2,1,0:T(8,128)(2,1)S(1)}, u32[]{:S(2)}, u32[]{:S(2)}) collective-permute-start(bf16[2,256,512]{2,1,0:T(8,128)(2,1)S(1)} %get-tuple-element.64), channel_id=1, source_target_pairs={{0,1},{1,0},{2,3},{3,2},{4,5},{5,4},{6,7},{7,6},{8,9},{9,8},{10,11... | collective-permute-start | bytes 1572872 | tf_op jit(solution)/shard_map/pp2/ppermute | solution.py:118
  67.8 14.2 %collective-permute-start.21 = (bf16[512,256]{1,0:T(8,128)(2,1)S(1)}, bf16[512,256]{1,0:T(8,128)(2,1)S(1)}, u32[]{:S(2)}, u32[]{:S(2)}) collective-permute-start(bf16[512,256]{1,0:T(8,128)(2,1)S(1)} %get-tuple-element.61), channel_id=1, source_target_pairs={{0,6},{1,7},{2,4},{3,5},{4,2},{5,3},{6,0},{7,1},{8,14},{9,15},{10,... | collective-permute-start | bytes 786440 | tf_op jit(solution)/shard_map/first_d/ppermute | solution.py:118
  70.8 14.7 %collective-permute-start.20 = (bf16[512,256]{1,0:T(8,128)(2,1)S(1)}, bf16[512,256]{1,0:T(8,128)(2,1)S(1)}, u32[]{:S(2)}, u32[]{:S(2)}) collective-permute-start(bf16[512,256]{1,0:T(8,128)(2,1)S(1)} %get-tuple-element.59), channel_id=1, source_target_pairs={{0,4},{1,5},{2,6},{3,7},{4,0},{5,1},{6,2},{7,3},{8,12},{9,13},{10,... | collective-permute-start | bytes 786440 | tf_op jit(solution)/shard_map/first_y/ppermute | solution.py:118
  71.7 13.8 %collective-permute-start.22 = (bf16[512,256]{1,0:T(8,128)(2,1)S(1)}, bf16[512,256]{1,0:T(8,128)(2,1)S(1)}, u32[]{:S(2)}, u32[]{:S(2)}) collective-permute-start(bf16[512,256]{1,0:T(8,128)(2,1)S(1)} %get-tuple-element.62), channel_id=1, source_target_pairs={{0,2},{1,3},{2,0},{3,1},{4,6},{5,7},{6,4},{7,5},{8,10},{9,11},{10,... | collective-permute-start | bytes 786440 | tf_op jit(solution)/shard_map/first_x/ppermute | solution.py:118
  74.4 18.9 %collective-permute-start.27 = (bf16[512,256]{1,0:T(8,128)(2,1)S(1)}, bf16[512,256]{1,0:T(8,128)(2,1)S(1)}, u32[]{:S(2)}, u32[]{:S(2)}) collective-permute-start(bf16[512,256]{1,0:T(8,128)(2,1)S(1)} %get-tuple-element.68), channel_id=1, source_target_pairs={{0,6},{1,7},{2,4},{3,5},{4,2},{5,3},{6,0},{7,1},{8,14},{9,15},{10,... | collective-permute-start | bytes 786440 | tf_op jit(solution)/shard_map/second_d/ppermute | solution.py:118
  79.7 16.0 %collective-permute-start.26 = (bf16[512,256]{1,0:T(8,128)(2,1)S(1)}, bf16[512,256]{1,0:T(8,128)(2,1)S(1)}, u32[]{:S(2)}, u32[]{:S(2)}) collective-permute-start(bf16[512,256]{1,0:T(8,128)(2,1)S(1)} %get-tuple-element.66), channel_id=1, source_target_pairs={{0,4},{1,5},{2,6},{3,7},{4,0},{5,1},{6,2},{7,3},{8,12},{9,13},{10,... | collective-permute-start | bytes 786440 | tf_op jit(solution)/shard_map/second_y/ppermute | solution.py:118
  82.0 13.8 %collective-permute-start.28 = (bf16[512,256]{1,0:T(8,128)(2,1)S(1)}, bf16[512,256]{1,0:T(8,128)(2,1)S(1)}, u32[]{:S(2)}, u32[]{:S(2)}) collective-permute-start(bf16[512,256]{1,0:T(8,128)(2,1)S(1)} %get-tuple-element.70), channel_id=1, source_target_pairs={{0,2},{1,3},{2,0},{3,1},{4,6},{5,7},{6,4},{7,5},{8,10},{9,11},{10,... | collective-permute-start | bytes 786440 | tf_op jit(solution)/shard_map/second_x/ppermute | solution.py:118
  (11 other events, 62.2 us)

commit v5 on v4

--- a/solution.py
+++ b/solution.py
@@ -522,7 +522,20 @@
             move(name + "x", to_x, x_part),
         )
 
-    first = exchanged("first_", *first)
+    mine, y_part, d_part, x_part = first
+    here, there = slice(0, PAIR_ROWS), slice(PAIR_ROWS, 2 * PAIR_ROWS)
+
+    def beside(one, other):
+        return jnp.concatenate([one, other], axis=1)
+
+    def plus(one, other):
+        return (one.astype(jnp.float32) + other.astype(jnp.float32)).astype(jnp.bfloat16)
+
+    over_y = move("first_y", to_y, beside(d_part[:, there], y_part[:, there]))
+    over_x = move("first_x", to_x, beside(d_part[:, here], x_part[:, here]))
+    then_y = move("then_y", to_y, plus(y_part[:, here], over_x[:, here]))
+    then_x = move("then_x", to_x, plus(x_part[:, there], over_y[:, here]))
+    first = mine, beside(then_y, over_y[:, there]), beside(over_x[:, there], then_x)
     second = exchanged("second_", *second)
 
     def total(parts):

time: 97.9 us -> 95.9 us (0.980)
  waiting for transfers between devices: 40.6 us -> 37 us
  starting transfers between devices: 41.2 us -> 42.7 us
    ppermute x29 -> x30, waiting for transfers between devices: 40.6 us -> 37 us  [hop(): return lax.ppermute(value, BOTH, pairs)]
    ppermute x29 -> x30, starting transfers between devices: 41.2 us -> 42.7 us  [hop(): return lax.ppermute(value, BOTH, pairs)]
  transfers between devices with their start and end apart: 29 -> 30, of which waited for: 14 -> 13; matrix products, arithmetic and copies ran while one was open for 0% -> 1% of each run, Pallas kernels for 8% -> 8%
where the time goes in v5:
time: 95.9 us; the launch traced here: 95.7 us
  starting transfers between devices  42.7 us (45%)
  waiting for transfers between devices  37 us (39%)
  Pallas kernels  10.7 us (11%)
  local copies, waits for them, and re-layouts  2.47 us (3%)
  other arithmetic  1.88 us (2%)
  between operations  1.01 us (1%)
    ppermute x30, starting transfers between devices, hop(): return lax.ppermute(value, BOTH, pairs)  42.7 us
    ppermute x30, waiting for transfers between devices, hop(): return lax.ppermute(value, BOTH, pairs)  37 us
    pallas_call x4, Pallas kernels, half(): call(functools.partial(tile_kernel, tiles, mine), (jax.ShapeDtypeStruct(p...  3.1 us
    pallas_call x3, Pallas kernels, plane_shards(): call(functools.partial(merge_kernel, slots, chunk), (bf16(group_rows, hal...  2.8 us
    pallas_call x1, Pallas kernels, plane_shards(): call(functools.partial(first_kernel, slots), (jax.ShapeDtypeStruct((1, ca...  2.59 us
  transfers between devices with their start and end apart: 30, of which 13 were waited for; matrix products, arithmetic and copies ran while one was open for 1% of the time, Pallas kernels for 8%

profile of v5, /device:TPU:0, one launch (start us, length us, event | category | flops | bytes accessed | tf_op | source)
XLA Modules:
  0.0 95.7 jit_solution(9690709520788584795)
XLA Ops:
  0.8 2.6 %first_kernel.1 = (s32[1,896]{1,0:T(1,128)}, s32[8,128]{1,0:T(8,128)}, bf16[896,512]{1,0:T(8,128)(2,1)}, bf16[224,512]{1,0:T(8,128)(2,1)}) custom-call(s32[1]{0:T(128)S(6)} %copy.6.count_ref, s32[896]{0:T(1024)} %assign_hbm.1, f32[1,4096]{1,0:T(1,128)} %bitcast.2, f32[1,4096]{1,0:T(1,128)} %bitcast.4, bf16[896,1024]{1,0:T(8,128)(2,1)} %dosage_ref.1), custom_call_target="tpu_custom_call" | custom-call | flops 205520896 | bytes 2752512 | tf_op jit(solution)/shard_map/first_kernel/pallas_call | solution.py:415
  3.4 3.0 %collective-permute-start = (bf16[224,512]{1,0:T(8,128)(2,1)}, bf16[224,512]{1,0:T(8,128)(2,1)S(1)}, u32[]{:S(2)}, u32[]{:S(2)}) collective-permute-start(bf16[224,512]{1,0:T(8,128)(2,1)} %get-tuple-element.41), channel_id=1, source_target_pairs={{0,4},{1,5},{2,6},{3,7},{4,0},{5,1},{6,2},{7,3},{8,12},{9,13},{10,... | collective-permute-start | bytes 688136 | tf_op jit(solution)/shard_map/y0/ppermute | solution.py:118
  8.3 1.9 %rest_kernel.1 = (bf16[896,512]{1,0:T(8,128)(2,1)S(1)}, bf16[224,512]{1,0:T(8,128)(2,1)S(1)}, bf16[448,512]{1,0:T(8,128)(2,1)S(1)}) custom-call(s32[1,896]{1,0:T(1,128)S(1)} %copy-done.5, bf16[896,512]{1,0:T(8,128)(2,1)S(1)} %copy-done.4, f32[1,4096]{1,0:T(1,128)S(1)} %bitcast.3, f32[1,4096]{1,0:T(1,128)S(1)} %bitcast.5, bf16[896,1024]{1,0:T(8,128)(2,1)S(1)} %copy-done), custom_call_target="tpu_custom_call" | custom-call | flops 1644167168 | bytes 2752512 | tf_op jit(solution)/shard_map/rest_kernel/pallas_call | solution.py:447
  10.3 2.5 %collective-permute-done.other_ref = bf16[224,512]{1,0:T(8,128)(2,1)S(1)} collective-permute-done((bf16[224,512]{1,0:T(8,128)(2,1)}, bf16[224,512]{1,0:T(8,128)(2,1)S(1)}, u32[]{:S(2)}, u32[]{:S(2)}) %collective-permute-start) | collective-permute-done | bytes 229408 | tf_op jit(solution)/shard_map/y0/ppermute | solution.py:118
  12.8 2.4 %collective-permute-start.6 = (bf16[448,512]{1,0:T(8,128)(2,1)S(1)}, bf16[448,512]{1,0:T(8,128)(2,1)S(1)}, u32[]{:S(2)}, u32[]{:S(2)}) collective-permute-start(bf16[448,512]{1,0:T(8,128)(2,1)S(1)} %get-tuple-element.47), channel_id=1, source_target_pairs={{0,4},{1,5},{2,6},{3,7},{4,0},{5,1},{6,2},{7,3},{8,12},{9,13},{10,... | collective-permute-start | bytes 1376264 | tf_op jit(solution)/shard_map/y2/ppermute | solution.py:118
  16.0 1.5 %collective-permute-start.1 = (bf16[256,512]{1,0:T(8,128)(2,1)S(1)}, bf16[256,512]{1,0:T(8,128)(2,1)S(1)}, u32[]{:S(2)}, u32[]{:S(2)}) collective-permute-start(bf16[256,512]{1,0:T(8,128)(2,1)S(1)} %merge_kernel.3.refs_16_), channel_id=1, source_target_pairs={{0,8},{1,9},{2,10},{3,11},{4,12},{5,13},{6,14},{7,15},{8,0},{9,1},... | collective-permute-start | bytes 786440 | tf_op jit(solution)/shard_map/a0/ppermute | solution.py:118
  19.6 2.0 %collective-permute-start.3 = (bf16[256,512]{1,0:T(8,128)(2,1)S(1)}, bf16[256,512]{1,0:T(8,128)(2,1)S(1)}, u32[]{:S(2)}, u32[]{:S(2)}) collective-permute-start(bf16[256,512]{1,0:T(8,128)(2,1)S(1)} %merge_kernel.4.refs_17_), channel_id=1, source_target_pairs={{0,8},{1,9},{2,10},{3,11},{4,12},{5,13},{6,14},{7,15},{8,0},{9,1},... | collective-permute-start | bytes 786440 | tf_op jit(solution)/shard_map/a1/ppermute | solution.py:118
  21.7 5.5 %collective-permute-done.6.other_ref = bf16[448,512]{1,0:T(8,128)(2,1)S(1)} collective-permute-done((bf16[448,512]{1,0:T(8,128)(2,1)S(1)}, bf16[448,512]{1,0:T(8,128)(2,1)S(1)}, u32[]{:S(2)}, u32[]{:S(2)}) %collective-permute-start.6) | collective-permute-done | bytes 458784 | tf_op jit(solution)/shard_map/y2/ppermute | solution.py:118
  28.2 1.7 %collective-permute-start.7 = (bf16[256,512]{1,0:T(8,128)(2,1)S(1)}, bf16[256,512]{1,0:T(8,128)(2,1)S(1)}, u32[]{:S(2)}, u32[]{:S(2)}) collective-permute-start(bf16[256,512]{1,0:T(8,128)(2,1)S(1)} %get-tuple-element.50.refs_18_), channel_id=1, source_target_pairs={{0,8},{1,9},{2,10},{3,11},{4,12},{5,13},{6,14},{7,15},{8,0},{9,1},... | collective-permute-start | bytes 786440 | tf_op jit(solution)/shard_map/a2/ppermute | solution.py:118
  29.9 3.2 %collective-permute-start.8 = (bf16[256,512]{1,0:T(8,128)(2,1)S(1)}, bf16[256,512]{1,0:T(8,128)(2,1)S(1)}, u32[]{:S(2)}, u32[]{:S(2)}) collective-permute-start(bf16[256,512]{1,0:T(8,128)(2,1)S(1)} %broadcast_select_fusion), channel_id=1, source_target_pairs={{0,8},{1,9},{2,10},{3,11},{4,12},{5,13},{6,14},{7,15},{8,0},{9,1},... | collective-permute-start | bytes 786440 | tf_op jit(solution)/shard_map/a3/ppermute | solution.py:118
  33.6 3.4 %collective-permute-done.7.refs_2_ = bf16[256,512]{1,0:T(8,128)(2,1)S(1)} collective-permute-done((bf16[256,512]{1,0:T(8,128)(2,1)S(1)}, bf16[256,512]{1,0:T(8,128)(2,1)S(1)}, u32[]{:S(2)}, u32[]{:S(2)}) %collective-permute-start.7) | collective-permute-done | bytes 262176 | tf_op jit(solution)/shard_map/a2/ppermute | solution.py:118
  37.6 5.1 %collective-permute-done.8.refs_3_ = bf16[256,512]{1,0:T(8,128)(2,1)S(1)} collective-permute-done((bf16[256,512]{1,0:T(8,128)(2,1)S(1)}, bf16[256,512]{1,0:T(8,128)(2,1)S(1)}, u32[]{:S(2)}, u32[]{:S(2)}) %collective-permute-start.8) | collective-permute-done | bytes 262176 | tf_op jit(solution)/shard_map/a3/ppermute | solution.py:118
  42.7 2.1 %collective-permute-start.17 = (bf16[256,512]{1,0:T(8,128)(2,1)S(1)}, bf16[256,512]{1,0:T(8,128)(2,1)S(1)}, u32[]{:S(2)}, u32[]{:S(2)}) collective-permute-start(bf16[256,512]{1,0:T(8,128)(2,1)S(1)} %collective-permute-done.11.refs_8_), channel_id=1, source_target_pairs={{0,8},{1,9},{2,10},{3,11},{4,12},{5,13},{6,14},{7,15},{8,0},{9,1},... | collective-permute-start | bytes 786440 | tf_op jit(solution)/shard_map/e0/ppermute | solution.py:118
  45.9 2.4 %collective-permute-done.15.refs_12_ = bf16[256,512]{1,0:T(8,128)(2,1)S(1)} collective-permute-done((bf16[256,512]{1,0:T(8,128)(2,1)S(1)}, bf16[256,512]{1,0:T(8,128)(2,1)S(1)}, u32[]{:S(2)}, u32[]{:S(2)}) %collective-permute-start.15) | collective-permute-done | bytes 262176 | tf_op jit(solution)/shard_map/d0/ppermute | solution.py:118
  48.8 8.3 %collective-permute-start.18 = (bf16[256,512]{1,0:T(8,128)(2,1)S(1)}, bf16[256,512]{1,0:T(8,128)(2,1)S(1)}, u32[]{:S(2)}, u32[]{:S(2)}) collective-permute-start(bf16[256,512]{1,0:T(8,128)(2,1)S(1)} %collective-permute-done.12.refs_9_), channel_id=1, source_target_pairs={{0,8},{1,9},{2,10},{3,11},{4,12},{5,13},{6,14},{7,15},{8,0},{9,1},... | collective-permute-start | bytes 786440 | tf_op jit(solution)/shard_map/e1/ppermute | solution.py:118
  57.1 2.4 %collective-permute-done.16.refs_13_ = bf16[256,512]{1,0:T(8,128)(2,1)S(1)} collective-permute-done((bf16[256,512]{1,0:T(8,128)(2,1)S(1)}, bf16[256,512]{1,0:T(8,128)(2,1)S(1)}, u32[]{:S(2)}, u32[]{:S(2)}) %collective-permute-start.16) | collective-permute-done | bytes 262176 | tf_op jit(solution)/shard_map/d1/ppermute | solution.py:118
  59.5 3.7 %collective-permute-done.18.refs_15_ = bf16[256,512]{1,0:T(8,128)(2,1)S(1)} collective-permute-done((bf16[256,512]{1,0:T(8,128)(2,1)S(1)}, bf16[256,512]{1,0:T(8,128)(2,1)S(1)}, u32[]{:S(2)}, u32[]{:S(2)}) %collective-permute-start.18) | collective-permute-done | bytes 262176 | tf_op jit(solution)/shard_map/e1/ppermute | solution.py:118
  63.6 1.7 %collective-permute-start.24 = (bf16[256,512]{1,0:T(8,128)(2,1)S(1)}, bf16[256,512]{1,0:T(8,128)(2,1)S(1)}, u32[]{:S(2)}, u32[]{:S(2)}) collective-permute-start(bf16[256,512]{1,0:T(8,128)(2,1)S(1)} %collective-permute-done.14.refs_11_), channel_id=1, source_target_pairs={{0,2},{1,9},{2,0},{3,11},{4,6},{5,13},{6,4},{7,15},{8,10},{9,1},{1... | collective-permute-start | bytes 786440 | tf_op jit(solution)/shard_map/l0/ppermute | solution.py:118
  65.7 2.5 %collective-permute-start.26 = (bf16[2,256,512]{2,1,0:T(8,128)(2,1)S(1)}, bf16[2,256,512]{2,1,0:T(8,128)(2,1)S(1)}, u32[]{:S(2)}, u32[]{:S(2)}) collective-permute-start(bf16[2,256,512]{2,1,0:T(8,128)(2,1)S(1)} %get-tuple-element.62), channel_id=1, source_target_pairs={{0,1},{1,0},{2,3},{3,2},{4,5},{5,4},{6,7},{7,6},{8,9},{9,8},{10,11... | collective-permute-start | bytes 1572872 | tf_op jit(solution)/shard_map/pp2/ppermute | solution.py:118
  69.0 1.9 %collective-permute-start.22 = (bf16[512,256]{1,0:T(8,128)(2,1)S(1)}, bf16[512,256]{1,0:T(8,128)(2,1)S(1)}, u32[]{:S(2)}, u32[]{:S(2)}) collective-permute-start(bf16[512,256]{1,0:T(8,128)(2,1)S(1)} %pad_maximum_fusion.1), channel_id=1, source_target_pairs={{0,4},{1,5},{2,6},{3,7},{4,0},{5,1},{6,2},{7,3},{8,12},{9,13},{10,... | collective-permute-start | bytes 786440 | tf_op jit(solution)/shard_map/first_y/ppermute | solution.py:118
  73.7 4.3 %collective-permute-start.28 = (bf16[512,256]{1,0:T(8,128)(2,1)S(1)}, bf16[512,256]{1,0:T(8,128)(2,1)S(1)}, u32[]{:S(2)}, u32[]{:S(2)}) collective-permute-start(bf16[512,256]{1,0:T(8,128)(2,1)S(1)} %get-tuple-element.66), channel_id=1, source_target_pairs={{0,6},{1,7},{2,4},{3,5},{4,2},{5,3},{6,0},{7,1},{8,14},{9,15},{10,... | collective-permute-start | bytes 786440 | tf_op jit(solution)/shard_map/second_d/ppermute | solution.py:118
  81.1 2.1 %collective-permute-start.21 = (bf16[512,128]{1,0:T(8,128)(2,1)S(1)}, bf16[512,128]{1,0:T(8,128)(2,1)S(1)}, u32[]{:S(2)}, u32[]{:S(2)}) collective-permute-start(bf16[512,128]{1,0:T(8,128)(2,1)S(1)} %add_convert_fusion.1), channel_id=1, source_target_pairs={{0,4},{1,5},{2,6},{3,7},{4,0},{5,1},{6,2},{7,3},{8,12},{9,13},{10,... | collective-permute-start | bytes 393224 | tf_op jit(solution)/shard_map/then_y/ppermute | solution.py:118
  83.1 3.1 %collective-permute-done.28 = bf16[512,256]{1,0:T(8,128)(2,1)S(1)} collective-permute-done((bf16[512,256]{1,0:T(8,128)(2,1)S(1)}, bf16[512,256]{1,0:T(8,128)(2,1)S(1)}, u32[]{:S(2)}, u32[]{:S(2)}) %collective-permute-start.28) | collective-permute-done | bytes 262176 | tf_op jit(solution)/shard_map/second_d/ppermute | solution.py:118
  86.2 5.0 %collective-permute-done.27 = bf16[512,256]{1,0:T(8,128)(2,1)S(1)} collective-permute-done((bf16[512,256]{1,0:T(8,128)(2,1)S(1)}, bf16[512,256]{1,0:T(8,128)(2,1)S(1)}, u32[]{:S(2)}, u32[]{:S(2)}) %collective-permute-start.27) | collective-permute-done | bytes 262176 | tf_op jit(solution)/shard_map/second_y/ppermute | solution.py:118
  (73 shorter events, 20.5 us)
Async XLA Ops:
  3.4 9.4 %collective-permute-start = (bf16[224,512]{1,0:T(8,128)(2,1)}, bf16[224,512]{1,0:T(8,128)(2,1)S(1)}, u32[]{:S(2)}, u32[]{:S(2)}) collective-permute-start(bf16[224,512]{1,0:T(8,128)(2,1)} %get-tuple-element.41), channel_id=1, source_target_pairs={{0,4},{1,5},{2,6},{3,7},{4,0},{5,1},{6,2},{7,3},{8,12},{9,13},{10,... | collective-permute-start | bytes 688136 | tf_op jit(solution)/shard_map/y0/ppermute | solution.py:118
  12.8 14.4 %collective-permute-start.6 = (bf16[448,512]{1,0:T(8,128)(2,1)S(1)}, bf16[448,512]{1,0:T(8,128)(2,1)S(1)}, u32[]{:S(2)}, u32[]{:S(2)}) collective-permute-start(bf16[448,512]{1,0:T(8,128)(2,1)S(1)} %get-tuple-element.47), channel_id=1, source_target_pairs={{0,4},{1,5},{2,6},{3,7},{4,0},{5,1},{6,2},{7,3},{8,12},{9,13},{10,... | collective-permute-start | bytes 1376264 | tf_op jit(solution)/shard_map/y2/ppermute | solution.py:118
  16.0 11.1 %collective-permute-start.1 = (bf16[256,512]{1,0:T(8,128)(2,1)S(1)}, bf16[256,512]{1,0:T(8,128)(2,1)S(1)}, u32[]{:S(2)}, u32[]{:S(2)}) collective-permute-start(bf16[256,512]{1,0:T(8,128)(2,1)S(1)} %merge_kernel.3.refs_16_), channel_id=1, source_target_pairs={{0,8},{1,9},{2,10},{3,11},{4,12},{5,13},{6,14},{7,15},{8,0},{9,1},... | collective-permute-start | bytes 786440 | tf_op jit(solution)/shard_map/a0/ppermute | solution.py:118
  17.6 9.6 %collective-permute-start.5 = (bf16[256,512]{1,0:T(8,128)(2,1)S(1)}, bf16[256,512]{1,0:T(8,128)(2,1)S(1)}, u32[]{:S(2)}, u32[]{:S(2)}) collective-permute-start(bf16[256,512]{1,0:T(8,128)(2,1)S(1)} %merge_kernel.3.refs_16_), channel_id=1, source_target_pairs={{0,1},{1,0},{2,3},{3,2},{4,5},{5,4},{6,7},{7,6},{8,16},{9,17},{10,... | collective-permute-start | bytes 786440 | tf_op jit(solution)/shard_map/b0/ppermute | solution.py:118
  19.6 10.2 %collective-permute-start.3 = (bf16[256,512]{1,0:T(8,128)(2,1)S(1)}, bf16[256,512]{1,0:T(8,128)(2,1)S(1)}, u32[]{:S(2)}, u32[]{:S(2)}) collective-permute-start(bf16[256,512]{1,0:T(8,128)(2,1)S(1)} %merge_kernel.4.refs_17_), channel_id=1, source_target_pairs={{0,8},{1,9},{2,10},{3,11},{4,12},{5,13},{6,14},{7,15},{8,0},{9,1},... | collective-permute-start | bytes 786440 | tf_op jit(solution)/shard_map/a1/ppermute | solution.py:118
  28.2 8.9 %collective-permute-start.7 = (bf16[256,512]{1,0:T(8,128)(2,1)S(1)}, bf16[256,512]{1,0:T(8,128)(2,1)S(1)}, u32[]{:S(2)}, u32[]{:S(2)}) collective-permute-start(bf16[256,512]{1,0:T(8,128)(2,1)S(1)} %get-tuple-element.50.refs_18_), channel_id=1, source_target_pairs={{0,8},{1,9},{2,10},{3,11},{4,12},{5,13},{6,14},{7,15},{8,0},{9,1},... | collective-permute-start | bytes 786440 | tf_op jit(solution)/shard_map/a2/ppermute | solution.py:118
  29.9 12.7 %collective-permute-start.8 = (bf16[256,512]{1,0:T(8,128)(2,1)S(1)}, bf16[256,512]{1,0:T(8,128)(2,1)S(1)}, u32[]{:S(2)}, u32[]{:S(2)}) collective-permute-start(bf16[256,512]{1,0:T(8,128)(2,1)S(1)} %broadcast_select_fusion), channel_id=1, source_target_pairs={{0,8},{1,9},{2,10},{3,11},{4,12},{5,13},{6,14},{7,15},{8,0},{9,1},... | collective-permute-start | bytes 786440 | tf_op jit(solution)/shard_map/a3/ppermute | solution.py:118
  33.1 11.6 %collective-permute-start.10 = (bf16[256,512]{1,0:T(8,128)(2,1)S(1)}, bf16[256,512]{1,0:T(8,128)(2,1)S(1)}, u32[]{:S(2)}, u32[]{:S(2)}) collective-permute-start(bf16[256,512]{1,0:T(8,128)(2,1)S(1)} %get-tuple-element.51.refs_19_), channel_id=1, source_target_pairs={{0,1},{1,0},{2,3},{3,2},{4,5},{5,4},{6,7},{7,6},{8,16},{9,17},{10,... | collective-permute-start | bytes 786440 | tf_op jit(solution)/shard_map/b3/ppermute | solution.py:118
  33.1 15.1 %collective-permute-start.15 = (bf16[256,512]{1,0:T(8,128)(2,1)S(1)}, bf16[256,512]{1,0:T(8,128)(2,1)S(1)}, u32[]{:S(2)}, u32[]{:S(2)}) collective-permute-start(bf16[256,512]{1,0:T(8,128)(2,1)S(1)} %collective-permute-done.4.refs_5_), channel_id=1, source_target_pairs={{0,8},{1,9},{2,10},{3,11},{4,12},{5,13},{6,14},{7,15},{8,0},{9,1},... | collective-permute-start | bytes 786440 | tf_op jit(solution)/shard_map/d0/ppermute | solution.py:118
  37.0 11.2 %collective-permute-start.9 = (bf16[256,512]{1,0:T(8,128)(2,1)S(1)}, bf16[256,512]{1,0:T(8,128)(2,1)S(1)}, u32[]{:S(2)}, u32[]{:S(2)}) collective-permute-start(bf16[256,512]{1,0:T(8,128)(2,1)S(1)} %get-tuple-element.50.refs_18_), channel_id=1, source_target_pairs={{0,1},{1,0},{2,3},{3,2},{4,5},{5,4},{6,7},{7,6},{8,16},{9,17},{10,... | collective-permute-start | bytes 786440 | tf_op jit(solution)/shard_map/b2/ppermute | solution.py:118
  37.0 11.7 %collective-permute-start.12 = (bf16[256,512]{1,0:T(8,128)(2,1)S(1)}, bf16[256,512]{1,0:T(8,128)(2,1)S(1)}, u32[]{:S(2)}, u32[]{:S(2)}) collective-permute-start(bf16[256,512]{1,0:T(8,128)(2,1)S(1)} %collective-permute-done.3.refs_1_), channel_id=1, source_target_pairs={{0,1},{1,0},{2,3},{3,2},{4,5},{5,4},{6,7},{7,6},{8,16},{9,17},{10,... | collective-permute-start | bytes 786440 | tf_op jit(solution)/shard_map/c1/ppermute | solution.py:118
  42.7 14.5 %collective-permute-start.17 = (bf16[256,512]{1,0:T(8,128)(2,1)S(1)}, bf16[256,512]{1,0:T(8,128)(2,1)S(1)}, u32[]{:S(2)}, u32[]{:S(2)}) collective-permute-start(bf16[256,512]{1,0:T(8,128)(2,1)S(1)} %collective-permute-done.11.refs_8_), channel_id=1, source_target_pairs={{0,8},{1,9},{2,10},{3,11},{4,12},{5,13},{6,14},{7,15},{8,0},{9,1},... | collective-permute-start | bytes 786440 | tf_op jit(solution)/shard_map/e0/ppermute | solution.py:118
  44.8 14.8 %collective-permute-start.16 = (bf16[256,512]{1,0:T(8,128)(2,1)S(1)}, bf16[256,512]{1,0:T(8,128)(2,1)S(1)}, u32[]{:S(2)}, u32[]{:S(2)}) collective-permute-start(bf16[256,512]{1,0:T(8,128)(2,1)S(1)} %collective-permute-done.10.refs_7_), channel_id=1, source_target_pairs={{0,8},{1,9},{2,10},{3,11},{4,12},{5,13},{6,14},{7,15},{8,0},{9,1},... | collective-permute-start | bytes 786440 | tf_op jit(solution)/shard_map/d1/ppermute | solution.py:118
  48.3 11.2 %collective-permute-start.14 = (bf16[256,512]{1,0:T(8,128)(2,1)S(1)}, bf16[256,512]{1,0:T(8,128)(2,1)S(1)}, u32[]{:S(2)}, u32[]{:S(2)}) collective-permute-start(bf16[256,512]{1,0:T(8,128)(2,1)S(1)} %collective-permute-done.8.refs_3_), channel_id=1, source_target_pairs={{0,1},{1,0},{2,3},{3,2},{4,5},{5,4},{6,7},{7,6},{8,16},{9,17},{10,... | collective-permute-start | bytes 786440 | tf_op jit(solution)/shard_map/c3/ppermute | solution.py:118
  48.3 11.2 %collective-permute-start.13 = (bf16[256,512]{1,0:T(8,128)(2,1)S(1)}, bf16[256,512]{1,0:T(8,128)(2,1)S(1)}, u32[]{:S(2)}, u32[]{:S(2)}) collective-permute-start(bf16[256,512]{1,0:T(8,128)(2,1)S(1)} %collective-permute-done.7.refs_2_), channel_id=1, source_target_pairs={{0,1},{1,0},{2,3},{3,2},{4,5},{5,4},{6,7},{7,6},{8,16},{9,17},{10,... | collective-permute-start | bytes 786440 | tf_op jit(solution)/shard_map/c2/ppermute | solution.py:118
  48.8 14.4 %collective-permute-start.18 = (bf16[256,512]{1,0:T(8,128)(2,1)S(1)}, bf16[256,512]{1,0:T(8,128)(2,1)S(1)}, u32[]{:S(2)}, u32[]{:S(2)}) collective-permute-start(bf16[256,512]{1,0:T(8,128)(2,1)S(1)} %collective-permute-done.12.refs_9_), channel_id=1, source_target_pairs={{0,8},{1,9},{2,10},{3,11},{4,12},{5,13},{6,14},{7,15},{8,0},{9,1},... | collective-permute-start | bytes 786440 | tf_op jit(solution)/shard_map/e1/ppermute | solution.py:118
  63.6 8.8 %collective-permute-start.24 = (bf16[256,512]{1,0:T(8,128)(2,1)S(1)}, bf16[256,512]{1,0:T(8,128)(2,1)S(1)}, u32[]{:S(2)}, u32[]{:S(2)}) collective-permute-start(bf16[256,512]{1,0:T(8,128)(2,1)S(1)} %collective-permute-done.14.refs_11_), channel_id=1, source_target_pairs={{0,2},{1,9},{2,0},{3,11},{4,6},{5,13},{6,4},{7,15},{8,10},{9,1},{1... | collective-permute-start | bytes 786440 | tf_op jit(solution)/shard_map/l0/ppermute | solution.py:118
  69.0 10.5 %collective-permute-start.22 = (bf16[512,256]{1,0:T(8,128)(2,1)S(1)}, bf16[512,256]{1,0:T(8,128)(2,1)S(1)}, u32[]{:S(2)}, u32[]{:S(2)}) collective-permute-start(bf16[512,256]{1,0:T(8,128)(2,1)S(1)} %pad_maximum_fusion.1), channel_id=1, source_target_pairs={{0,4},{1,5},{2,6},{3,7},{4,0},{5,1},{6,2},{7,3},{8,12},{9,13},{10,... | collective-permute-start | bytes 786440 | tf_op jit(solution)/shard_map/first_y/ppermute | solution.py:118
  71.8 9.3 %collective-permute-start.20 = (bf16[512,256]{1,0:T(8,128)(2,1)S(1)}, bf16[512,256]{1,0:T(8,128)(2,1)S(1)}, u32[]{:S(2)}, u32[]{:S(2)}) collective-permute-start(bf16[512,256]{1,0:T(8,128)(2,1)S(1)} %pad_maximum_fusion), channel_id=1, source_target_pairs={{0,2},{1,3},{2,0},{3,1},{4,6},{5,7},{6,4},{7,5},{8,10},{9,11},{10,... | collective-permute-start | bytes 786440 | tf_op jit(solution)/shard_map/first_x/ppermute | solution.py:118
  73.7 12.6 %collective-permute-start.28 = (bf16[512,256]{1,0:T(8,128)(2,1)S(1)}, bf16[512,256]{1,0:T(8,128)(2,1)S(1)}, u32[]{:S(2)}, u32[]{:S(2)}) collective-permute-start(bf16[512,256]{1,0:T(8,128)(2,1)S(1)} %get-tuple-element.66), channel_id=1, source_target_pairs={{0,6},{1,7},{2,4},{3,5},{4,2},{5,3},{6,0},{7,1},{8,14},{9,15},{10,... | collective-permute-start | bytes 786440 | tf_op jit(solution)/shard_map/second_d/ppermute | solution.py:118
  78.0 13.3 %collective-permute-start.27 = (bf16[512,256]{1,0:T(8,128)(2,1)S(1)}, bf16[512,256]{1,0:T(8,128)(2,1)S(1)}, u32[]{:S(2)}, u32[]{:S(2)}) collective-permute-start(bf16[512,256]{1,0:T(8,128)(2,1)S(1)} %get-tuple-element.64), channel_id=1, source_target_pairs={{0,4},{1,5},{2,6},{3,7},{4,0},{5,1},{6,2},{7,3},{8,12},{9,13},{10,... | collective-permute-start | bytes 786440 | tf_op jit(solution)/shard_map/second_y/ppermute | solution.py:118
  78.8 13.5 %collective-permute-start.29 = (bf16[512,256]{1,0:T(8,128)(2,1)S(1)}, bf16[512,256]{1,0:T(8,128)(2,1)S(1)}, u32[]{:S(2)}, u32[]{:S(2)}) collective-permute-start(bf16[512,256]{1,0:T(8,128)(2,1)S(1)} %get-tuple-element.68), channel_id=1, source_target_pairs={{0,2},{1,3},{2,0},{3,1},{4,6},{5,7},{6,4},{7,5},{8,10},{9,11},{10,... | collective-permute-start | bytes 786440 | tf_op jit(solution)/shard_map/second_x/ppermute | solution.py:118
  79.6 14.3 %collective-permute-start.23 = (bf16[512,128]{1,0:T(8,128)(2,1)S(1)}, bf16[512,128]{1,0:T(8,128)(2,1)S(1)}, u32[]{:S(2)}, u32[]{:S(2)}) collective-permute-start(bf16[512,128]{1,0:T(8,128)(2,1)S(1)} %add_convert_fusion), channel_id=1, source_target_pairs={{0,2},{1,3},{2,0},{3,1},{4,6},{5,7},{6,4},{7,5},{8,10},{9,11},{10,... | collective-permute-start | bytes 393224 | tf_op jit(solution)/shard_map/then_x/ppermute | solution.py:118
  81.1 12.8 %collective-permute-start.21 = (bf16[512,128]{1,0:T(8,128)(2,1)S(1)}, bf16[512,128]{1,0:T(8,128)(2,1)S(1)}, u32[]{:S(2)}, u32[]{:S(2)}) collective-permute-start(bf16[512,128]{1,0:T(8,128)(2,1)S(1)} %add_convert_fusion.1), channel_id=1, source_target_pairs={{0,4},{1,5},{2,6},{3,7},{4,0},{5,1},{6,2},{7,3},{8,12},{9,13},{10,... | collective-permute-start | bytes 393224 | tf_op jit(solution)/shard_map/then_y/ppermute | solution.py:118
  (12 other events, 71.3 us)

commit v6 on v5

--- a/solution.py
+++ b/solution.py
@@ -522,7 +522,6 @@
             move(name + "x", to_x, x_part),
         )
 
-    mine, y_part, d_part, x_part = first
     here, there = slice(0, PAIR_ROWS), slice(PAIR_ROWS, 2 * PAIR_ROWS)
 
     def beside(one, other):
@@ -531,12 +530,15 @@
     def plus(one, other):
         return (one.astype(jnp.float32) + other.astype(jnp.float32)).astype(jnp.bfloat16)
 
-    over_y = move("first_y", to_y, beside(d_part[:, there], y_part[:, there]))
-    over_x = move("first_x", to_x, beside(d_part[:, here], x_part[:, here]))
-    then_y = move("then_y", to_y, plus(y_part[:, here], over_x[:, here]))
-    then_x = move("then_x", to_x, plus(x_part[:, there], over_y[:, here]))
-    first = mine, beside(then_y, over_y[:, there]), beside(over_x[:, there], then_x)
-    second = exchanged("second_", *second)
+    def passed(name, mine, y_part, d_part, x_part):
+        over_y = move(name + "y", to_y, beside(d_part[:, there], y_part[:, there]))
+        over_x = move(name + "x", to_x, beside(d_part[:, here], x_part[:, here]))
+        then_y = move(name + "then_y", to_y, plus(y_part[:, here], over_x[:, here]))
+        then_x = move(name + "then_x", to_x, plus(x_part[:, there], over_y[:, here]))
+        return mine, beside(then_y, over_y[:, there]), beside(over_x[:, there], then_x)
+
+    first = passed("first_", *first)
+    second = passed("second_", *second)
 
     def total(parts):
         mine, *others = parts

time: 95.9 us -> 94 us (0.980)
  waiting for transfers between devices: 37 us -> 33.8 us
    ppermute x30 -> x31, waiting for transfers between devices: 37 us -> 33.8 us  [hop(): return lax.ppermute(value, BOTH, pairs)]
    ppermute x30 -> x31, starting transfers between devices: 42.7 us -> 43.6 us  [hop(): return lax.ppermute(value, BOTH, pairs)]
  transfers between devices with their start and end apart: 30 -> 31, of which waited for: 13 -> 14; matrix products, arithmetic and copies ran while one was open for 1% -> 1% of each run, Pallas kernels for 8% -> 8%
where the time goes in v6:
time: 94 us; the launch traced here: 93.7 us
  starting transfers between devices  43.6 us (46%)
  waiting for transfers between devices  33.8 us (36%)
  Pallas kernels  10.7 us (11%)
  local copies, waits for them, and re-layouts  2.54 us (3%)
  other arithmetic  1.98 us (2%)
  between operations  1.07 us (1%)
    ppermute x31, starting transfers between devices, hop(): return lax.ppermute(value, BOTH, pairs)  43.6 us
    ppermute x31, waiting for transfers between devices, hop(): return lax.ppermute(value, BOTH, pairs)  33.8 us
    pallas_call x4, Pallas kernels, half(): call(functools.partial(tile_kernel, tiles, mine), (jax.ShapeDtypeStruct(p...  3.1 us
    pallas_call x3, Pallas kernels, plane_shards(): call(functools.partial(merge_kernel, slots, chunk), (bf16(group_rows, hal...  2.8 us
    pallas_call x1, Pallas kernels, plane_shards(): call(functools.partial(first_kernel, slots), (jax.ShapeDtypeStruct((1, ca...  2.59 us
  transfers between devices with their start and end apart: 31, of which 14 were waited for; matrix products, arithmetic and copies ran while one was open for 1% of the time, Pallas kernels for 8%

profile of v6, /device:TPU:0, one launch (start us, length us, event | category | flops | bytes accessed | tf_op | source)
XLA Modules:
  0.0 93.7 jit_solution(7452421669309869070)
XLA Ops:
  0.8 2.6 %first_kernel.1 = (s32[1,896]{1,0:T(1,128)}, s32[8,128]{1,0:T(8,128)}, bf16[896,512]{1,0:T(8,128)(2,1)}, bf16[224,512]{1,0:T(8,128)(2,1)}) custom-call(s32[1]{0:T(128)S(6)} %copy.6.count_ref, s32[896]{0:T(1024)} %assign_hbm.1, f32[1,4096]{1,0:T(1,128)} %bitcast.2, f32[1,4096]{1,0:T(1,128)} %bitcast.4, bf16[896,1024]{1,0:T(8,128)(2,1)} %dosage_ref.1), custom_call_target="tpu_custom_call" | custom-call | flops 205520896 | bytes 2752512 | tf_op jit(solution)/shard_map/first_kernel/pallas_call | solution.py:415
  3.4 3.0 %collective-permute-start = (bf16[224,512]{1,0:T(8,128)(2,1)}, bf16[224,512]{1,0:T(8,128)(2,1)S(1)}, u32[]{:S(2)}, u32[]{:S(2)}) collective-permute-start(bf16[224,512]{1,0:T(8,128)(2,1)} %get-tuple-element.40), channel_id=1, source_target_pairs={{0,4},{1,5},{2,6},{3,7},{4,0},{5,1},{6,2},{7,3},{8,12},{9,13},{10,... | collective-permute-start | bytes 688136 | tf_op jit(solution)/shard_map/y0/ppermute | solution.py:118
  8.3 1.9 %rest_kernel.1 = (bf16[896,512]{1,0:T(8,128)(2,1)S(1)}, bf16[224,512]{1,0:T(8,128)(2,1)S(1)}, bf16[448,512]{1,0:T(8,128)(2,1)S(1)}) custom-call(s32[1,896]{1,0:T(1,128)S(1)} %copy-done.5, bf16[896,512]{1,0:T(8,128)(2,1)S(1)} %copy-done.4, f32[1,4096]{1,0:T(1,128)S(1)} %bitcast.3, f32[1,4096]{1,0:T(1,128)S(1)} %bitcast.5, bf16[896,1024]{1,0:T(8,128)(2,1)S(1)} %copy-done), custom_call_target="tpu_custom_call" | custom-call | flops 1644167168 | bytes 2752512 | tf_op jit(solution)/shard_map/rest_kernel/pallas_call | solution.py:447
  10.3 2.5 %collective-permute-done.other_ref = bf16[224,512]{1,0:T(8,128)(2,1)S(1)} collective-permute-done((bf16[224,512]{1,0:T(8,128)(2,1)}, bf16[224,512]{1,0:T(8,128)(2,1)S(1)}, u32[]{:S(2)}, u32[]{:S(2)}) %collective-permute-start) | collective-permute-done | bytes 229408 | tf_op jit(solution)/shard_map/y0/ppermute | solution.py:118
  12.8 2.4 %collective-permute-start.6 = (bf16[448,512]{1,0:T(8,128)(2,1)S(1)}, bf16[448,512]{1,0:T(8,128)(2,1)S(1)}, u32[]{:S(2)}, u32[]{:S(2)}) collective-permute-start(bf16[448,512]{1,0:T(8,128)(2,1)S(1)} %get-tuple-element.46), channel_id=1, source_target_pairs={{0,4},{1,5},{2,6},{3,7},{4,0},{5,1},{6,2},{7,3},{8,12},{9,13},{10,... | collective-permute-start | bytes 1376264 | tf_op jit(solution)/shard_map/y2/ppermute | solution.py:118
  19.7 2.0 %collective-permute-start.3 = (bf16[256,512]{1,0:T(8,128)(2,1)S(1)}, bf16[256,512]{1,0:T(8,128)(2,1)S(1)}, u32[]{:S(2)}, u32[]{:S(2)}) collective-permute-start(bf16[256,512]{1,0:T(8,128)(2,1)S(1)} %merge_kernel.4.refs_17_), channel_id=1, source_target_pairs={{0,8},{1,9},{2,10},{3,11},{4,12},{5,13},{6,14},{7,15},{8,0},{9,1},... | collective-permute-start | bytes 786440 | tf_op jit(solution)/shard_map/a1/ppermute | solution.py:118
  21.6 5.5 %collective-permute-done.6.other_ref = bf16[448,512]{1,0:T(8,128)(2,1)S(1)} collective-permute-done((bf16[448,512]{1,0:T(8,128)(2,1)S(1)}, bf16[448,512]{1,0:T(8,128)(2,1)S(1)}, u32[]{:S(2)}, u32[]{:S(2)}) %collective-permute-start.6) | collective-permute-done | bytes 458784 | tf_op jit(solution)/shard_map/y2/ppermute | solution.py:118
  28.2 1.7 %collective-permute-start.7 = (bf16[256,512]{1,0:T(8,128)(2,1)S(1)}, bf16[256,512]{1,0:T(8,128)(2,1)S(1)}, u32[]{:S(2)}, u32[]{:S(2)}) collective-permute-start(bf16[256,512]{1,0:T(8,128)(2,1)S(1)} %get-tuple-element.49.refs_18_), channel_id=1, source_target_pairs={{0,8},{1,9},{2,10},{3,11},{4,12},{5,13},{6,14},{7,15},{8,0},{9,1},... | collective-permute-start | bytes 786440 | tf_op jit(solution)/shard_map/a2/ppermute | solution.py:118
  29.9 3.2 %collective-permute-start.8 = (bf16[256,512]{1,0:T(8,128)(2,1)S(1)}, bf16[256,512]{1,0:T(8,128)(2,1)S(1)}, u32[]{:S(2)}, u32[]{:S(2)}) collective-permute-start(bf16[256,512]{1,0:T(8,128)(2,1)S(1)} %broadcast_select_fusion), channel_id=1, source_target_pairs={{0,8},{1,9},{2,10},{3,11},{4,12},{5,13},{6,14},{7,15},{8,0},{9,1},... | collective-permute-start | bytes 786440 | tf_op jit(solution)/shard_map/a3/ppermute | solution.py:118
  33.6 3.5 %collective-permute-done.7.refs_2_ = bf16[256,512]{1,0:T(8,128)(2,1)S(1)} collective-permute-done((bf16[256,512]{1,0:T(8,128)(2,1)S(1)}, bf16[256,512]{1,0:T(8,128)(2,1)S(1)}, u32[]{:S(2)}, u32[]{:S(2)}) %collective-permute-start.7) | collective-permute-done | bytes 262176 | tf_op jit(solution)/shard_map/a2/ppermute | solution.py:118
  37.6 5.1 %collective-permute-done.8.refs_3_ = bf16[256,512]{1,0:T(8,128)(2,1)S(1)} collective-permute-done((bf16[256,512]{1,0:T(8,128)(2,1)S(1)}, bf16[256,512]{1,0:T(8,128)(2,1)S(1)}, u32[]{:S(2)}, u32[]{:S(2)}) %collective-permute-start.8) | collective-permute-done | bytes 262176 | tf_op jit(solution)/shard_map/a3/ppermute | solution.py:118
  42.7 2.1 %collective-permute-start.17 = (bf16[256,512]{1,0:T(8,128)(2,1)S(1)}, bf16[256,512]{1,0:T(8,128)(2,1)S(1)}, u32[]{:S(2)}, u32[]{:S(2)}) collective-permute-start(bf16[256,512]{1,0:T(8,128)(2,1)S(1)} %collective-permute-done.11.refs_8_), channel_id=1, source_target_pairs={{0,8},{1,9},{2,10},{3,11},{4,12},{5,13},{6,14},{7,15},{8,0},{9,1},... | collective-permute-start | bytes 786440 | tf_op jit(solution)/shard_map/e0/ppermute | solution.py:118
  45.9 2.4 %collective-permute-done.15.refs_12_ = bf16[256,512]{1,0:T(8,128)(2,1)S(1)} collective-permute-done((bf16[256,512]{1,0:T(8,128)(2,1)S(1)}, bf16[256,512]{1,0:T(8,128)(2,1)S(1)}, u32[]{:S(2)}, u32[]{:S(2)}) %collective-permute-start.15) | collective-permute-done | bytes 262176 | tf_op jit(solution)/shard_map/d0/ppermute | solution.py:118
  48.8 8.3 %collective-permute-start.18 = (bf16[256,512]{1,0:T(8,128)(2,1)S(1)}, bf16[256,512]{1,0:T(8,128)(2,1)S(1)}, u32[]{:S(2)}, u32[]{:S(2)}) collective-permute-start(bf16[256,512]{1,0:T(8,128)(2,1)S(1)} %collective-permute-done.12.refs_9_), channel_id=1, source_target_pairs={{0,8},{1,9},{2,10},{3,11},{4,12},{5,13},{6,14},{7,15},{8,0},{9,1},... | collective-permute-start | bytes 786440 | tf_op jit(solution)/shard_map/e1/ppermute | solution.py:118
  57.1 2.4 %collective-permute-done.16.refs_13_ = bf16[256,512]{1,0:T(8,128)(2,1)S(1)} collective-permute-done((bf16[256,512]{1,0:T(8,128)(2,1)S(1)}, bf16[256,512]{1,0:T(8,128)(2,1)S(1)}, u32[]{:S(2)}, u32[]{:S(2)}) %collective-permute-start.16) | collective-permute-done | bytes 262176 | tf_op jit(solution)/shard_map/d1/ppermute | solution.py:118
  59.5 3.7 %collective-permute-done.18.refs_15_ = bf16[256,512]{1,0:T(8,128)(2,1)S(1)} collective-permute-done((bf16[256,512]{1,0:T(8,128)(2,1)S(1)}, bf16[256,512]{1,0:T(8,128)(2,1)S(1)}, u32[]{:S(2)}, u32[]{:S(2)}) %collective-permute-start.18) | collective-permute-done | bytes 262176 | tf_op jit(solution)/shard_map/e1/ppermute | solution.py:118
  63.6 1.7 %collective-permute-start.24 = (bf16[256,512]{1,0:T(8,128)(2,1)S(1)}, bf16[256,512]{1,0:T(8,128)(2,1)S(1)}, u32[]{:S(2)}, u32[]{:S(2)}) collective-permute-start(bf16[256,512]{1,0:T(8,128)(2,1)S(1)} %collective-permute-done.14.refs_11_), channel_id=1, source_target_pairs={{0,2},{1,9},{2,0},{3,11},{4,6},{5,13},{6,4},{7,15},{8,10},{9,1},{1... | collective-permute-start | bytes 786440 | tf_op jit(solution)/shard_map/l0/ppermute | solution.py:118
  65.7 2.4 %collective-permute-start.26 = (bf16[2,256,512]{2,1,0:T(8,128)(2,1)S(1)}, bf16[2,256,512]{2,1,0:T(8,128)(2,1)S(1)}, u32[]{:S(2)}, u32[]{:S(2)}) collective-permute-start(bf16[2,256,512]{2,1,0:T(8,128)(2,1)S(1)} %get-tuple-element.61), channel_id=1, source_target_pairs={{0,1},{1,0},{2,3},{3,2},{4,5},{5,4},{6,7},{7,6},{8,9},{9,8},{10,11... | collective-permute-start | bytes 1572872 | tf_op jit(solution)/shard_map/pp2/ppermute | solution.py:118
  69.0 2.0 %collective-permute-start.22 = (bf16[512,256]{1,0:T(8,128)(2,1)S(1)}, bf16[512,256]{1,0:T(8,128)(2,1)S(1)}, u32[]{:S(2)}, u32[]{:S(2)}) collective-permute-start(bf16[512,256]{1,0:T(8,128)(2,1)S(1)} %pad_maximum_fusion.1), channel_id=1, source_target_pairs={{0,4},{1,5},{2,6},{3,7},{4,0},{5,1},{6,2},{7,3},{8,12},{9,13},{10,... | collective-permute-start | bytes 786440 | tf_op jit(solution)/shard_map/first_y/ppermute | solution.py:118
  73.8 2.4 %collective-permute-start.29 = (bf16[512,256]{1,0:T(8,128)(2,1)S(1)}, bf16[512,256]{1,0:T(8,128)(2,1)S(1)}, u32[]{:S(2)}, u32[]{:S(2)}) collective-permute-start(bf16[512,256]{1,0:T(8,128)(2,1)S(1)} %pad_maximum_fusion.3), channel_id=1, source_target_pairs={{0,4},{1,5},{2,6},{3,7},{4,0},{5,1},{6,2},{7,3},{8,12},{9,13},{10,... | collective-permute-start | bytes 786440 | tf_op jit(solution)/shard_map/second_y/ppermute | solution.py:118
  77.0 2.5 %collective-permute-start.27 = (bf16[512,256]{1,0:T(8,128)(2,1)S(1)}, bf16[512,256]{1,0:T(8,128)(2,1)S(1)}, u32[]{:S(2)}, u32[]{:S(2)}) collective-permute-start(bf16[512,256]{1,0:T(8,128)(2,1)S(1)} %pad_maximum_fusion.2), channel_id=1, source_target_pairs={{0,2},{1,3},{2,0},{3,1},{4,6},{5,7},{6,4},{7,5},{8,10},{9,11},{10,... | collective-permute-start | bytes 786440 | tf_op jit(solution)/shard_map/second_x/ppermute | solution.py:118
  80.8 2.5 %collective-permute-done.29 = bf16[512,256]{1,0:T(8,128)(2,1)S(1)} collective-permute-done((bf16[512,256]{1,0:T(8,128)(2,1)S(1)}, bf16[512,256]{1,0:T(8,128)(2,1)S(1)}, u32[]{:S(2)}, u32[]{:S(2)}) %collective-permute-start.29) | collective-permute-done | bytes 262176 | tf_op jit(solution)/shard_map/second_y/ppermute | solution.py:118
  83.4 2.5 %collective-permute-start.30 = (bf16[512,128]{1,0:T(8,128)(2,1)S(1)}, bf16[512,128]{1,0:T(8,128)(2,1)S(1)}, u32[]{:S(2)}, u32[]{:S(2)}) collective-permute-start(bf16[512,128]{1,0:T(8,128)(2,1)S(1)} %add_convert_fusion), channel_id=1, source_target_pairs={{0,2},{1,3},{2,0},{3,1},{4,6},{5,7},{6,4},{7,5},{8,10},{9,11},{10,... | collective-permute-start | bytes 393224 | tf_op jit(solution)/shard_map/second_then_x/ppermute | solution.py:118
  87.8 1.8 %collective-permute-done.23 = bf16[512,128]{1,0:T(8,128)(2,1)S(1)} collective-permute-done((bf16[512,128]{1,0:T(8,128)(2,1)S(1)}, bf16[512,128]{1,0:T(8,128)(2,1)S(1)}, u32[]{:S(2)}, u32[]{:S(2)}) %collective-permute-start.23) | collective-permute-done | bytes 131104 | tf_op jit(solution)/shard_map/first_then_x/ppermute | solution.py:118
  (84 shorter events, 22.7 us)
Async XLA Ops:
  3.4 9.4 %collective-permute-start = (bf16[224,512]{1,0:T(8,128)(2,1)}, bf16[224,512]{1,0:T(8,128)(2,1)S(1)}, u32[]{:S(2)}, u32[]{:S(2)}) collective-permute-start(bf16[224,512]{1,0:T(8,128)(2,1)} %get-tuple-element.40), channel_id=1, source_target_pairs={{0,4},{1,5},{2,6},{3,7},{4,0},{5,1},{6,2},{7,3},{8,12},{9,13},{10,... | collective-permute-start | bytes 688136 | tf_op jit(solution)/shard_map/y0/ppermute | solution.py:118
  10.2 8.6 %collective-permute-start.2 = (bf16[224,512]{1,0:T(8,128)(2,1)S(1)}, bf16[224,512]{1,0:T(8,128)(2,1)S(1)}, u32[]{:S(2)}, u32[]{:S(2)}) collective-permute-start(bf16[224,512]{1,0:T(8,128)(2,1)S(1)} %get-tuple-element.41), channel_id=1, source_target_pairs={{0,4},{1,5},{2,6},{3,7},{4,0},{5,1},{6,2},{7,3},{8,12},{9,13},{10,... | collective-permute-start | bytes 688136 | tf_op jit(solution)/shard_map/y1/ppermute | solution.py:118
  12.8 14.4 %collective-permute-start.6 = (bf16[448,512]{1,0:T(8,128)(2,1)S(1)}, bf16[448,512]{1,0:T(8,128)(2,1)S(1)}, u32[]{:S(2)}, u32[]{:S(2)}) collective-permute-start(bf16[448,512]{1,0:T(8,128)(2,1)S(1)} %get-tuple-element.46), channel_id=1, source_target_pairs={{0,4},{1,5},{2,6},{3,7},{4,0},{5,1},{6,2},{7,3},{8,12},{9,13},{10,... | collective-permute-start | bytes 1376264 | tf_op jit(solution)/shard_map/y2/ppermute | solution.py:118
  16.0 11.1 %collective-permute-start.1 = (bf16[256,512]{1,0:T(8,128)(2,1)S(1)}, bf16[256,512]{1,0:T(8,128)(2,1)S(1)}, u32[]{:S(2)}, u32[]{:S(2)}) collective-permute-start(bf16[256,512]{1,0:T(8,128)(2,1)S(1)} %merge_kernel.3.refs_16_), channel_id=1, source_target_pairs={{0,8},{1,9},{2,10},{3,11},{4,12},{5,13},{6,14},{7,15},{8,0},{9,1},... | collective-permute-start | bytes 786440 | tf_op jit(solution)/shard_map/a0/ppermute | solution.py:118
  17.5 9.6 %collective-permute-start.5 = (bf16[256,512]{1,0:T(8,128)(2,1)S(1)}, bf16[256,512]{1,0:T(8,128)(2,1)S(1)}, u32[]{:S(2)}, u32[]{:S(2)}) collective-permute-start(bf16[256,512]{1,0:T(8,128)(2,1)S(1)} %merge_kernel.3.refs_16_), channel_id=1, source_target_pairs={{0,1},{1,0},{2,3},{3,2},{4,5},{5,4},{6,7},{7,6},{8,16},{9,17},{10,... | collective-permute-start | bytes 786440 | tf_op jit(solution)/shard_map/b0/ppermute | solution.py:118
  19.7 10.2 %collective-permute-start.3 = (bf16[256,512]{1,0:T(8,128)(2,1)S(1)}, bf16[256,512]{1,0:T(8,128)(2,1)S(1)}, u32[]{:S(2)}, u32[]{:S(2)}) collective-permute-start(bf16[256,512]{1,0:T(8,128)(2,1)S(1)} %merge_kernel.4.refs_17_), channel_id=1, source_target_pairs={{0,8},{1,9},{2,10},{3,11},{4,12},{5,13},{6,14},{7,15},{8,0},{9,1},... | collective-permute-start | bytes 786440 | tf_op jit(solution)/shard_map/a1/ppermute | solution.py:118
  21.6 8.2 %collective-permute-start.4 = (bf16[256,512]{1,0:T(8,128)(2,1)S(1)}, bf16[256,512]{1,0:T(8,128)(2,1)S(1)}, u32[]{:S(2)}, u32[]{:S(2)}) collective-permute-start(bf16[256,512]{1,0:T(8,128)(2,1)S(1)} %merge_kernel.4.refs_17_), channel_id=1, source_target_pairs={{0,1},{1,0},{2,3},{3,2},{4,5},{5,4},{6,7},{7,6},{8,16},{9,17},{10,... | collective-permute-start | bytes 786440 | tf_op jit(solution)/shard_map/b1/ppermute | solution.py:118
  28.2 8.9 %collective-permute-start.7 = (bf16[256,512]{1,0:T(8,128)(2,1)S(1)}, bf16[256,512]{1,0:T(8,128)(2,1)S(1)}, u32[]{:S(2)}, u32[]{:S(2)}) collective-permute-start(bf16[256,512]{1,0:T(8,128)(2,1)S(1)} %get-tuple-element.49.refs_18_), channel_id=1, source_target_pairs={{0,8},{1,9},{2,10},{3,11},{4,12},{5,13},{6,14},{7,15},{8,0},{9,1},... | collective-permute-start | bytes 786440 | tf_op jit(solution)/shard_map/a2/ppermute | solution.py:118
  29.9 12.7 %collective-permute-start.8 = (bf16[256,512]{1,0:T(8,128)(2,1)S(1)}, bf16[256,512]{1,0:T(8,128)(2,1)S(1)}, u32[]{:S(2)}, u32[]{:S(2)}) collective-permute-start(bf16[256,512]{1,0:T(8,128)(2,1)S(1)} %broadcast_select_fusion), channel_id=1, source_target_pairs={{0,8},{1,9},{2,10},{3,11},{4,12},{5,13},{6,14},{7,15},{8,0},{9,1},... | collective-permute-start | bytes 786440 | tf_op jit(solution)/shard_map/a3/ppermute | solution.py:118
  33.1 11.6 %collective-permute-start.10 = (bf16[256,512]{1,0:T(8,128)(2,1)S(1)}, bf16[256,512]{1,0:T(8,128)(2,1)S(1)}, u32[]{:S(2)}, u32[]{:S(2)}) collective-permute-start(bf16[256,512]{1,0:T(8,128)(2,1)S(1)} %get-tuple-element.50.refs_19_), channel_id=1, source_target_pairs={{0,1},{1,0},{2,3},{3,2},{4,5},{5,4},{6,7},{7,6},{8,16},{9,17},{10,... | collective-permute-start | bytes 786440 | tf_op jit(solution)/shard_map/b3/ppermute | solution.py:118
  33.1 15.1 %collective-permute-start.15 = (bf16[256,512]{1,0:T(8,128)(2,1)S(1)}, bf16[256,512]{1,0:T(8,128)(2,1)S(1)}, u32[]{:S(2)}, u32[]{:S(2)}) collective-permute-start(bf16[256,512]{1,0:T(8,128)(2,1)S(1)} %collective-permute-done.4.refs_5_), channel_id=1, source_target_pairs={{0,8},{1,9},{2,10},{3,11},{4,12},{5,13},{6,14},{7,15},{8,0},{9,1},... | collective-permute-start | bytes 786440 | tf_op jit(solution)/shard_map/d0/ppermute | solution.py:118
  37.1 11.2 %collective-permute-start.9 = (bf16[256,512]{1,0:T(8,128)(2,1)S(1)}, bf16[256,512]{1,0:T(8,128)(2,1)S(1)}, u32[]{:S(2)}, u32[]{:S(2)}) collective-permute-start(bf16[256,512]{1,0:T(8,128)(2,1)S(1)} %get-tuple-element.49.refs_18_), channel_id=1, source_target_pairs={{0,1},{1,0},{2,3},{3,2},{4,5},{5,4},{6,7},{7,6},{8,16},{9,17},{10,... | collective-permute-start | bytes 786440 | tf_op jit(solution)/shard_map/b2/ppermute | solution.py:118
  37.1 11.7 %collective-permute-start.12 = (bf16[256,512]{1,0:T(8,128)(2,1)S(1)}, bf16[256,512]{1,0:T(8,128)(2,1)S(1)}, u32[]{:S(2)}, u32[]{:S(2)}) collective-permute-start(bf16[256,512]{1,0:T(8,128)(2,1)S(1)} %collective-permute-done.3.refs_1_), channel_id=1, source_target_pairs={{0,1},{1,0},{2,3},{3,2},{4,5},{5,4},{6,7},{7,6},{8,16},{9,17},{10,... | collective-permute-start | bytes 786440 | tf_op jit(solution)/shard_map/c1/ppermute | solution.py:118
  42.7 14.4 %collective-permute-start.17 = (bf16[256,512]{1,0:T(8,128)(2,1)S(1)}, bf16[256,512]{1,0:T(8,128)(2,1)S(1)}, u32[]{:S(2)}, u32[]{:S(2)}) collective-permute-start(bf16[256,512]{1,0:T(8,128)(2,1)S(1)} %collective-permute-done.11.refs_8_), channel_id=1, source_target_pairs={{0,8},{1,9},{2,10},{3,11},{4,12},{5,13},{6,14},{7,15},{8,0},{9,1},... | collective-permute-start | bytes 786440 | tf_op jit(solution)/shard_map/e0/ppermute | solution.py:118
  44.8 14.8 %collective-permute-start.16 = (bf16[256,512]{1,0:T(8,128)(2,1)S(1)}, bf16[256,512]{1,0:T(8,128)(2,1)S(1)}, u32[]{:S(2)}, u32[]{:S(2)}) collective-permute-start(bf16[256,512]{1,0:T(8,128)(2,1)S(1)} %collective-permute-done.10.refs_7_), channel_id=1, source_target_pairs={{0,8},{1,9},{2,10},{3,11},{4,12},{5,13},{6,14},{7,15},{8,0},{9,1},... | collective-permute-start | bytes 786440 | tf_op jit(solution)/shard_map/d1/ppermute | solution.py:118
  48.3 11.2 %collective-permute-start.14 = (bf16[256,512]{1,0:T(8,128)(2,1)S(1)}, bf16[256,512]{1,0:T(8,128)(2,1)S(1)}, u32[]{:S(2)}, u32[]{:S(2)}) collective-permute-start(bf16[256,512]{1,0:T(8,128)(2,1)S(1)} %collective-permute-done.8.refs_3_), channel_id=1, source_target_pairs={{0,1},{1,0},{2,3},{3,2},{4,5},{5,4},{6,7},{7,6},{8,16},{9,17},{10,... | collective-permute-start | bytes 786440 | tf_op jit(solution)/shard_map/c3/ppermute | solution.py:118
  48.3 11.2 %collective-permute-start.13 = (bf16[256,512]{1,0:T(8,128)(2,1)S(1)}, bf16[256,512]{1,0:T(8,128)(2,1)S(1)}, u32[]{:S(2)}, u32[]{:S(2)}) collective-permute-start(bf16[256,512]{1,0:T(8,128)(2,1)S(1)} %collective-permute-done.7.refs_2_), channel_id=1, source_target_pairs={{0,1},{1,0},{2,3},{3,2},{4,5},{5,4},{6,7},{7,6},{8,16},{9,17},{10,... | collective-permute-start | bytes 786440 | tf_op jit(solution)/shard_map/c2/ppermute | solution.py:118
  48.8 14.4 %collective-permute-start.18 = (bf16[256,512]{1,0:T(8,128)(2,1)S(1)}, bf16[256,512]{1,0:T(8,128)(2,1)S(1)}, u32[]{:S(2)}, u32[]{:S(2)}) collective-permute-start(bf16[256,512]{1,0:T(8,128)(2,1)S(1)} %collective-permute-done.12.refs_9_), channel_id=1, source_target_pairs={{0,8},{1,9},{2,10},{3,11},{4,12},{5,13},{6,14},{7,15},{8,0},{9,1},... | collective-permute-start | bytes 786440 | tf_op jit(solution)/shard_map/e1/ppermute | solution.py:118
  63.6 8.8 %collective-permute-start.24 = (bf16[256,512]{1,0:T(8,128)(2,1)S(1)}, bf16[256,512]{1,0:T(8,128)(2,1)S(1)}, u32[]{:S(2)}, u32[]{:S(2)}) collective-permute-start(bf16[256,512]{1,0:T(8,128)(2,1)S(1)} %collective-permute-done.14.refs_11_), channel_id=1, source_target_pairs={{0,2},{1,9},{2,0},{3,11},{4,6},{5,13},{6,4},{7,15},{8,10},{9,1},{1... | collective-permute-start | bytes 786440 | tf_op jit(solution)/shard_map/l0/ppermute | solution.py:118
  69.0 10.6 %collective-permute-start.22 = (bf16[512,256]{1,0:T(8,128)(2,1)S(1)}, bf16[512,256]{1,0:T(8,128)(2,1)S(1)}, u32[]{:S(2)}, u32[]{:S(2)}) collective-permute-start(bf16[512,256]{1,0:T(8,128)(2,1)S(1)} %pad_maximum_fusion.1), channel_id=1, source_target_pairs={{0,4},{1,5},{2,6},{3,7},{4,0},{5,1},{6,2},{7,3},{8,12},{9,13},{10,... | collective-permute-start | bytes 786440 | tf_op jit(solution)/shard_map/first_y/ppermute | solution.py:118
  73.8 9.5 %collective-permute-start.29 = (bf16[512,256]{1,0:T(8,128)(2,1)S(1)}, bf16[512,256]{1,0:T(8,128)(2,1)S(1)}, u32[]{:S(2)}, u32[]{:S(2)}) collective-permute-start(bf16[512,256]{1,0:T(8,128)(2,1)S(1)} %pad_maximum_fusion.3), channel_id=1, source_target_pairs={{0,4},{1,5},{2,6},{3,7},{4,0},{5,1},{6,2},{7,3},{8,12},{9,13},{10,... | collective-permute-start | bytes 786440 | tf_op jit(solution)/shard_map/second_y/ppermute | solution.py:118
  77.0 9.8 %collective-permute-start.27 = (bf16[512,256]{1,0:T(8,128)(2,1)S(1)}, bf16[512,256]{1,0:T(8,128)(2,1)S(1)}, u32[]{:S(2)}, u32[]{:S(2)}) collective-permute-start(bf16[512,256]{1,0:T(8,128)(2,1)S(1)} %pad_maximum_fusion.2), channel_id=1, source_target_pairs={{0,2},{1,3},{2,0},{3,1},{4,6},{5,7},{6,4},{7,5},{8,10},{9,11},{10,... | collective-permute-start | bytes 786440 | tf_op jit(solution)/shard_map/second_x/ppermute | solution.py:118
  79.6 10.0 %collective-permute-start.23 = (bf16[512,128]{1,0:T(8,128)(2,1)S(1)}, bf16[512,128]{1,0:T(8,128)(2,1)S(1)}, u32[]{:S(2)}, u32[]{:S(2)}) collective-permute-start(bf16[512,128]{1,0:T(8,128)(2,1)S(1)} %add_convert_fusion.2), channel_id=1, source_target_pairs={{0,2},{1,3},{2,0},{3,1},{4,6},{5,7},{6,4},{7,5},{8,10},{9,11},{10,... | collective-permute-start | bytes 393224 | tf_op jit(solution)/shard_map/first_then_x/ppermute | solution.py:118
  79.8 9.8 %collective-permute-start.21 = (bf16[512,128]{1,0:T(8,128)(2,1)S(1)}, bf16[512,128]{1,0:T(8,128)(2,1)S(1)}, u32[]{:S(2)}, u32[]{:S(2)}) collective-permute-start(bf16[512,128]{1,0:T(8,128)(2,1)S(1)} %add_convert_fusion.3), channel_id=1, source_target_pairs={{0,4},{1,5},{2,6},{3,7},{4,0},{5,1},{6,2},{7,3},{8,12},{9,13},{10,... | collective-permute-start | bytes 393224 | tf_op jit(solution)/shard_map/first_then_y/ppermute | solution.py:118
  (13 other events, 75.1 us)

commit v7 on v6

--- a/solution.py
+++ b/solution.py
@@ -383,6 +383,12 @@
                 out_ref[...] = total.astype(out_ref.dtype)
 
 
+def finish_kernel(later_ref, first_ref, out_ref):
+    scale = 1.0 / math.sqrt(F)
+    both = jnp.concatenate([first_ref[...], later_ref[...]], axis=1) * scale
+    out_ref[...] = both.reshape(P_SIZE, ROUNDS, PAIR_ROWS)
+
+
 def plane_tiles(tiles, sent, far, kept, *last):
     columns = len(tiles[0]) * PAIR_ROWS
     part = bf16(P_SIZE, columns)
@@ -544,9 +550,15 @@
         mine, *others = parts
         for other in others:
             mine = mine + other.astype(jnp.float32)
-        return mine.reshape(P_SIZE, 2, PAIR_ROWS)
-
-    return jnp.concatenate([total(first), total(second)], axis=1) * (1.0 / math.sqrt(F))
+        return mine
+
+    return call(
+        functools.partial(finish_kernel),
+        jax.ShapeDtypeStruct((P_SIZE, ROUNDS, PAIR_ROWS), jnp.float32),
+        [IN_VMEM] * 2,
+        IN_VMEM,
+        (8 * P_SIZE * P_SIZE, 4 * 1024 * 1024),
+    )(total(second), total(first))
 
 
 def solution(mesh):

time: 94 us -> 93.3 us (level)
  other arithmetic: 1.98 us -> 0.47 us
  Pallas kernels: 10.7 us -> 11.8 us
    mul x1 -> x0, other arithmetic: 1.51 us -> none  [plane_shards(): jnp.concatenate([total(first), total(second)], axis=1)]
    pallas_call x0 -> x1, Pallas kernels: none -> 1.15 us  [plane_shards(): call(functools.partial(finish_kernel), jax.ShapeDtypeStruct((P_SIZE, ROUN...]
where the time goes in v7:
time: 93.3 us; the launch traced here: 93.1 us
  starting transfers between devices  43.6 us (47%)
  waiting for transfers between devices  34.1 us (37%)
  Pallas kernels  11.8 us (13%)
  local copies, waits for them, and re-layouts  2 us (2%)
  between operations  1.05 us (1%)
    ppermute x31, starting transfers between devices, hop(): return lax.ppermute(value, BOTH, pairs)  43.6 us
    ppermute x31, waiting for transfers between devices, hop(): return lax.ppermute(value, BOTH, pairs)  34.1 us
    pallas_call x4, Pallas kernels, half(): call(functools.partial(tile_kernel, tiles, mine), (jax.ShapeDtypeStruct(p...  3.1 us
    pallas_call x3, Pallas kernels, plane_shards(): call(functools.partial(merge_kernel, slots, chunk), (bf16(group_rows, hal...  2.8 us
    pallas_call x1, Pallas kernels, plane_shards(): call(functools.partial(first_kernel, slots), (jax.ShapeDtypeStruct((1, ca...  2.59 us
    unnamed x12, local copies, waits for them, and re-layouts  1.87 us
  transfers between devices with their start and end apart: 31, of which 14 were waited for; matrix products, arithmetic and copies ran while one was open for 1% of the time, Pallas kernels for 8%

profile of v7, /device:TPU:0, one launch (start us, length us, event | category | flops | bytes accessed | tf_op | source)
XLA Modules:
  0.0 93.1 jit_solution(7796825320293580623)
XLA Ops:
  0.8 2.6 %first_kernel.1 = (s32[1,896]{1,0:T(1,128)}, s32[8,128]{1,0:T(8,128)}, bf16[896,512]{1,0:T(8,128)(2,1)}, bf16[224,512]{1,0:T(8,128)(2,1)}) custom-call(s32[1]{0:T(128)S(6)} %copy.6.count_ref, s32[896]{0:T(1024)} %assign_hbm.1, f32[1,4096]{1,0:T(1,128)} %bitcast.2, f32[1,4096]{1,0:T(1,128)} %bitcast.4, bf16[896,1024]{1,0:T(8,128)(2,1)} %dosage_ref.1), custom_call_target="tpu_custom_call" | custom-call | flops 205520896 | bytes 2752512 | tf_op jit(solution)/shard_map/first_kernel/pallas_call | solution.py:421
  3.4 3.0 %collective-permute-start = (bf16[224,512]{1,0:T(8,128)(2,1)}, bf16[224,512]{1,0:T(8,128)(2,1)S(1)}, u32[]{:S(2)}, u32[]{:S(2)}) collective-permute-start(bf16[224,512]{1,0:T(8,128)(2,1)} %get-tuple-element.40), channel_id=1, source_target_pairs={{0,4},{1,5},{2,6},{3,7},{4,0},{5,1},{6,2},{7,3},{8,12},{9,13},{10,... | collective-permute-start | bytes 688136 | tf_op jit(solution)/shard_map/y0/ppermute | solution.py:118
  8.3 1.9 %rest_kernel.1 = (bf16[896,512]{1,0:T(8,128)(2,1)S(1)}, bf16[224,512]{1,0:T(8,128)(2,1)S(1)}, bf16[448,512]{1,0:T(8,128)(2,1)S(1)}) custom-call(s32[1,896]{1,0:T(1,128)S(1)} %copy-done.5, bf16[896,512]{1,0:T(8,128)(2,1)S(1)} %copy-done.4, f32[1,4096]{1,0:T(1,128)S(1)} %bitcast.3, f32[1,4096]{1,0:T(1,128)S(1)} %bitcast.5, bf16[896,1024]{1,0:T(8,128)(2,1)S(1)} %copy-done), custom_call_target="tpu_custom_call" | custom-call | flops 1644167168 | bytes 2752512 | tf_op jit(solution)/shard_map/rest_kernel/pallas_call | solution.py:453
  10.3 2.5 %collective-permute-done.other_ref = bf16[224,512]{1,0:T(8,128)(2,1)S(1)} collective-permute-done((bf16[224,512]{1,0:T(8,128)(2,1)}, bf16[224,512]{1,0:T(8,128)(2,1)S(1)}, u32[]{:S(2)}, u32[]{:S(2)}) %collective-permute-start) | collective-permute-done | bytes 229408 | tf_op jit(solution)/shard_map/y0/ppermute | solution.py:118
  12.8 2.4 %collective-permute-start.6 = (bf16[448,512]{1,0:T(8,128)(2,1)S(1)}, bf16[448,512]{1,0:T(8,128)(2,1)S(1)}, u32[]{:S(2)}, u32[]{:S(2)}) collective-permute-start(bf16[448,512]{1,0:T(8,128)(2,1)S(1)} %get-tuple-element.46), channel_id=1, source_target_pairs={{0,4},{1,5},{2,6},{3,7},{4,0},{5,1},{6,2},{7,3},{8,12},{9,13},{10,... | collective-permute-start | bytes 1376264 | tf_op jit(solution)/shard_map/y2/ppermute | solution.py:118
  19.7 2.0 %collective-permute-start.3 = (bf16[256,512]{1,0:T(8,128)(2,1)S(1)}, bf16[256,512]{1,0:T(8,128)(2,1)S(1)}, u32[]{:S(2)}, u32[]{:S(2)}) collective-permute-start(bf16[256,512]{1,0:T(8,128)(2,1)S(1)} %merge_kernel.4.refs_17_), channel_id=1, source_target_pairs={{0,8},{1,9},{2,10},{3,11},{4,12},{5,13},{6,14},{7,15},{8,0},{9,1},... | collective-permute-start | bytes 786440 | tf_op jit(solution)/shard_map/a1/ppermute | solution.py:118
  21.6 5.5 %collective-permute-done.6.other_ref = bf16[448,512]{1,0:T(8,128)(2,1)S(1)} collective-permute-done((bf16[448,512]{1,0:T(8,128)(2,1)S(1)}, bf16[448,512]{1,0:T(8,128)(2,1)S(1)}, u32[]{:S(2)}, u32[]{:S(2)}) %collective-permute-start.6) | collective-permute-done | bytes 458784 | tf_op jit(solution)/shard_map/y2/ppermute | solution.py:118
  28.2 1.7 %collective-permute-start.7 = (bf16[256,512]{1,0:T(8,128)(2,1)S(1)}, bf16[256,512]{1,0:T(8,128)(2,1)S(1)}, u32[]{:S(2)}, u32[]{:S(2)}) collective-permute-start(bf16[256,512]{1,0:T(8,128)(2,1)S(1)} %get-tuple-element.49.refs_18_), channel_id=1, source_target_pairs={{0,8},{1,9},{2,10},{3,11},{4,12},{5,13},{6,14},{7,15},{8,0},{9,1},... | collective-permute-start | bytes 786440 | tf_op jit(solution)/shard_map/a2/ppermute | solution.py:118
  29.9 3.2 %collective-permute-start.8 = (bf16[256,512]{1,0:T(8,128)(2,1)S(1)}, bf16[256,512]{1,0:T(8,128)(2,1)S(1)}, u32[]{:S(2)}, u32[]{:S(2)}) collective-permute-start(bf16[256,512]{1,0:T(8,128)(2,1)S(1)} %broadcast_select_fusion), channel_id=1, source_target_pairs={{0,8},{1,9},{2,10},{3,11},{4,12},{5,13},{6,14},{7,15},{8,0},{9,1},... | collective-permute-start | bytes 786440 | tf_op jit(solution)/shard_map/a3/ppermute | solution.py:118
  33.6 3.5 %collective-permute-done.7.refs_2_ = bf16[256,512]{1,0:T(8,128)(2,1)S(1)} collective-permute-done((bf16[256,512]{1,0:T(8,128)(2,1)S(1)}, bf16[256,512]{1,0:T(8,128)(2,1)S(1)}, u32[]{:S(2)}, u32[]{:S(2)}) %collective-permute-start.7) | collective-permute-done | bytes 262176 | tf_op jit(solution)/shard_map/a2/ppermute | solution.py:118
  37.6 5.1 %collective-permute-done.8.refs_3_ = bf16[256,512]{1,0:T(8,128)(2,1)S(1)} collective-permute-done((bf16[256,512]{1,0:T(8,128)(2,1)S(1)}, bf16[256,512]{1,0:T(8,128)(2,1)S(1)}, u32[]{:S(2)}, u32[]{:S(2)}) %collective-permute-start.8) | collective-permute-done | bytes 262176 | tf_op jit(solution)/shard_map/a3/ppermute | solution.py:118
  42.7 2.1 %collective-permute-start.17 = (bf16[256,512]{1,0:T(8,128)(2,1)S(1)}, bf16[256,512]{1,0:T(8,128)(2,1)S(1)}, u32[]{:S(2)}, u32[]{:S(2)}) collective-permute-start(bf16[256,512]{1,0:T(8,128)(2,1)S(1)} %collective-permute-done.11.refs_8_), channel_id=1, source_target_pairs={{0,8},{1,9},{2,10},{3,11},{4,12},{5,13},{6,14},{7,15},{8,0},{9,1},... | collective-permute-start | bytes 786440 | tf_op jit(solution)/shard_map/e0/ppermute | solution.py:118
  45.9 2.4 %collective-permute-done.15.refs_12_ = bf16[256,512]{1,0:T(8,128)(2,1)S(1)} collective-permute-done((bf16[256,512]{1,0:T(8,128)(2,1)S(1)}, bf16[256,512]{1,0:T(8,128)(2,1)S(1)}, u32[]{:S(2)}, u32[]{:S(2)}) %collective-permute-start.15) | collective-permute-done | bytes 262176 | tf_op jit(solution)/shard_map/d0/ppermute | solution.py:118
  48.8 8.3 %collective-permute-start.18 = (bf16[256,512]{1,0:T(8,128)(2,1)S(1)}, bf16[256,512]{1,0:T(8,128)(2,1)S(1)}, u32[]{:S(2)}, u32[]{:S(2)}) collective-permute-start(bf16[256,512]{1,0:T(8,128)(2,1)S(1)} %collective-permute-done.12.refs_9_), channel_id=1, source_target_pairs={{0,8},{1,9},{2,10},{3,11},{4,12},{5,13},{6,14},{7,15},{8,0},{9,1},... | collective-permute-start | bytes 786440 | tf_op jit(solution)/shard_map/e1/ppermute | solution.py:118
  57.1 2.4 %collective-permute-done.16.refs_13_ = bf16[256,512]{1,0:T(8,128)(2,1)S(1)} collective-permute-done((bf16[256,512]{1,0:T(8,128)(2,1)S(1)}, bf16[256,512]{1,0:T(8,128)(2,1)S(1)}, u32[]{:S(2)}, u32[]{:S(2)}) %collective-permute-start.16) | collective-permute-done | bytes 262176 | tf_op jit(solution)/shard_map/d1/ppermute | solution.py:118
  59.5 3.7 %collective-permute-done.18.refs_15_ = bf16[256,512]{1,0:T(8,128)(2,1)S(1)} collective-permute-done((bf16[256,512]{1,0:T(8,128)(2,1)S(1)}, bf16[256,512]{1,0:T(8,128)(2,1)S(1)}, u32[]{:S(2)}, u32[]{:S(2)}) %collective-permute-start.18) | collective-permute-done | bytes 262176 | tf_op jit(solution)/shard_map/e1/ppermute | solution.py:118
  63.6 1.7 %collective-permute-start.20 = (bf16[256,512]{1,0:T(8,128)(2,1)S(1)}, bf16[256,512]{1,0:T(8,128)(2,1)S(1)}, u32[]{:S(2)}, u32[]{:S(2)}) collective-permute-start(bf16[256,512]{1,0:T(8,128)(2,1)S(1)} %collective-permute-done.14.refs_11_), channel_id=1, source_target_pairs={{0,2},{1,9},{2,0},{3,11},{4,6},{5,13},{6,4},{7,15},{8,10},{9,1},{1... | collective-permute-start | bytes 786440 | tf_op jit(solution)/shard_map/l0/ppermute | solution.py:118
  65.7 2.4 %collective-permute-start.22 = (bf16[2,256,512]{2,1,0:T(8,128)(2,1)S(1)}, bf16[2,256,512]{2,1,0:T(8,128)(2,1)S(1)}, u32[]{:S(2)}, u32[]{:S(2)}) collective-permute-start(bf16[2,256,512]{2,1,0:T(8,128)(2,1)S(1)} %get-tuple-element.57), channel_id=1, source_target_pairs={{0,1},{1,0},{2,3},{3,2},{4,5},{5,4},{6,7},{7,6},{8,9},{9,8},{10,11... | collective-permute-start | bytes 1572872 | tf_op jit(solution)/shard_map/pp2/ppermute | solution.py:118
  69.0 2.0 %collective-permute-start.29 = (bf16[512,256]{1,0:T(8,128)(2,1)S(1)}, bf16[512,256]{1,0:T(8,128)(2,1)S(1)}, u32[]{:S(2)}, u32[]{:S(2)}) collective-permute-start(bf16[512,256]{1,0:T(8,128)(2,1)S(1)} %pad_maximum_fusion.3), channel_id=1, source_target_pairs={{0,4},{1,5},{2,6},{3,7},{4,0},{5,1},{6,2},{7,3},{8,12},{9,13},{10,... | collective-permute-start | bytes 786440 | tf_op jit(solution)/shard_map/first_y/ppermute | solution.py:118
  73.8 2.4 %collective-permute-start.25 = (bf16[512,256]{1,0:T(8,128)(2,1)S(1)}, bf16[512,256]{1,0:T(8,128)(2,1)S(1)}, u32[]{:S(2)}, u32[]{:S(2)}) collective-permute-start(bf16[512,256]{1,0:T(8,128)(2,1)S(1)} %pad_maximum_fusion.1), channel_id=1, source_target_pairs={{0,4},{1,5},{2,6},{3,7},{4,0},{5,1},{6,2},{7,3},{8,12},{9,13},{10,... | collective-permute-start | bytes 786440 | tf_op jit(solution)/shard_map/second_y/ppermute | solution.py:118
  77.0 2.5 %collective-permute-start.23 = (bf16[512,256]{1,0:T(8,128)(2,1)S(1)}, bf16[512,256]{1,0:T(8,128)(2,1)S(1)}, u32[]{:S(2)}, u32[]{:S(2)}) collective-permute-start(bf16[512,256]{1,0:T(8,128)(2,1)S(1)} %pad_maximum_fusion), channel_id=1, source_target_pairs={{0,2},{1,3},{2,0},{3,1},{4,6},{5,7},{6,4},{7,5},{8,10},{9,11},{10,... | collective-permute-start | bytes 786440 | tf_op jit(solution)/shard_map/second_x/ppermute | solution.py:118
  80.8 2.5 %collective-permute-done.25 = bf16[512,256]{1,0:T(8,128)(2,1)S(1)} collective-permute-done((bf16[512,256]{1,0:T(8,128)(2,1)S(1)}, bf16[512,256]{1,0:T(8,128)(2,1)S(1)}, u32[]{:S(2)}, u32[]{:S(2)}) %collective-permute-start.25) | collective-permute-done | bytes 262176 | tf_op jit(solution)/shard_map/second_y/ppermute | solution.py:118
  83.4 2.5 %collective-permute-start.26 = (bf16[512,128]{1,0:T(8,128)(2,1)S(1)}, bf16[512,128]{1,0:T(8,128)(2,1)S(1)}, u32[]{:S(2)}, u32[]{:S(2)}) collective-permute-start(bf16[512,128]{1,0:T(8,128)(2,1)S(1)} %add_convert_fusion.2), channel_id=1, source_target_pairs={{0,2},{1,3},{2,0},{3,1},{4,6},{5,7},{6,4},{7,5},{8,10},{9,11},{10,... | collective-permute-start | bytes 393224 | tf_op jit(solution)/shard_map/second_then_x/ppermute | solution.py:118
  87.8 1.8 %collective-permute-done.30 = bf16[512,128]{1,0:T(8,128)(2,1)S(1)} collective-permute-done((bf16[512,128]{1,0:T(8,128)(2,1)S(1)}, bf16[512,128]{1,0:T(8,128)(2,1)S(1)}, u32[]{:S(2)}, u32[]{:S(2)}) %collective-permute-start.30) | collective-permute-done | bytes 131104 | tf_op jit(solution)/shard_map/first_then_x/ppermute | solution.py:118
  (82 shorter events, 22.1 us)
Async XLA Ops:
  3.4 9.4 %collective-permute-start = (bf16[224,512]{1,0:T(8,128)(2,1)}, bf16[224,512]{1,0:T(8,128)(2,1)S(1)}, u32[]{:S(2)}, u32[]{:S(2)}) collective-permute-start(bf16[224,512]{1,0:T(8,128)(2,1)} %get-tuple-element.40), channel_id=1, source_target_pairs={{0,4},{1,5},{2,6},{3,7},{4,0},{5,1},{6,2},{7,3},{8,12},{9,13},{10,... | collective-permute-start | bytes 688136 | tf_op jit(solution)/shard_map/y0/ppermute | solution.py:118
  10.2 8.6 %collective-permute-start.2 = (bf16[224,512]{1,0:T(8,128)(2,1)S(1)}, bf16[224,512]{1,0:T(8,128)(2,1)S(1)}, u32[]{:S(2)}, u32[]{:S(2)}) collective-permute-start(bf16[224,512]{1,0:T(8,128)(2,1)S(1)} %get-tuple-element.41), channel_id=1, source_target_pairs={{0,4},{1,5},{2,6},{3,7},{4,0},{5,1},{6,2},{7,3},{8,12},{9,13},{10,... | collective-permute-start | bytes 688136 | tf_op jit(solution)/shard_map/y1/ppermute | solution.py:118
  12.8 14.4 %collective-permute-start.6 = (bf16[448,512]{1,0:T(8,128)(2,1)S(1)}, bf16[448,512]{1,0:T(8,128)(2,1)S(1)}, u32[]{:S(2)}, u32[]{:S(2)}) collective-permute-start(bf16[448,512]{1,0:T(8,128)(2,1)S(1)} %get-tuple-element.46), channel_id=1, source_target_pairs={{0,4},{1,5},{2,6},{3,7},{4,0},{5,1},{6,2},{7,3},{8,12},{9,13},{10,... | collective-permute-start | bytes 1376264 | tf_op jit(solution)/shard_map/y2/ppermute | solution.py:118
  16.0 11.1 %collective-permute-start.1 = (bf16[256,512]{1,0:T(8,128)(2,1)S(1)}, bf16[256,512]{1,0:T(8,128)(2,1)S(1)}, u32[]{:S(2)}, u32[]{:S(2)}) collective-permute-start(bf16[256,512]{1,0:T(8,128)(2,1)S(1)} %merge_kernel.3.refs_16_), channel_id=1, source_target_pairs={{0,8},{1,9},{2,10},{3,11},{4,12},{5,13},{6,14},{7,15},{8,0},{9,1},... | collective-permute-start | bytes 786440 | tf_op jit(solution)/shard_map/a0/ppermute | solution.py:118
  17.5 9.6 %collective-permute-start.5 = (bf16[256,512]{1,0:T(8,128)(2,1)S(1)}, bf16[256,512]{1,0:T(8,128)(2,1)S(1)}, u32[]{:S(2)}, u32[]{:S(2)}) collective-permute-start(bf16[256,512]{1,0:T(8,128)(2,1)S(1)} %merge_kernel.3.refs_16_), channel_id=1, source_target_pairs={{0,1},{1,0},{2,3},{3,2},{4,5},{5,4},{6,7},{7,6},{8,16},{9,17},{10,... | collective-permute-start | bytes 786440 | tf_op jit(solution)/shard_map/b0/ppermute | solution.py:118
  19.7 10.2 %collective-permute-start.3 = (bf16[256,512]{1,0:T(8,128)(2,1)S(1)}, bf16[256,512]{1,0:T(8,128)(2,1)S(1)}, u32[]{:S(2)}, u32[]{:S(2)}) collective-permute-start(bf16[256,512]{1,0:T(8,128)(2,1)S(1)} %merge_kernel.4.refs_17_), channel_id=1, source_target_pairs={{0,8},{1,9},{2,10},{3,11},{4,12},{5,13},{6,14},{7,15},{8,0},{9,1},... | collective-permute-start | bytes 786440 | tf_op jit(solution)/shard_map/a1/ppermute | solution.py:118
  21.6 8.2 %collective-permute-start.4 = (bf16[256,512]{1,0:T(8,128)(2,1)S(1)}, bf16[256,512]{1,0:T(8,128)(2,1)S(1)}, u32[]{:S(2)}, u32[]{:S(2)}) collective-permute-start(bf16[256,512]{1,0:T(8,128)(2,1)S(1)} %merge_kernel.4.refs_17_), channel_id=1, source_target_pairs={{0,1},{1,0},{2,3},{3,2},{4,5},{5,4},{6,7},{7,6},{8,16},{9,17},{10,... | collective-permute-start | bytes 786440 | tf_op jit(solution)/shard_map/b1/ppermute | solution.py:118
  28.2 8.9 %collective-permute-start.7 = (bf16[256,512]{1,0:T(8,128)(2,1)S(1)}, bf16[256,512]{1,0:T(8,128)(2,1)S(1)}, u32[]{:S(2)}, u32[]{:S(2)}) collective-permute-start(bf16[256,512]{1,0:T(8,128)(2,1)S(1)} %get-tuple-element.49.refs_18_), channel_id=1, source_target_pairs={{0,8},{1,9},{2,10},{3,11},{4,12},{5,13},{6,14},{7,15},{8,0},{9,1},... | collective-permute-start | bytes 786440 | tf_op jit(solution)/shard_map/a2/ppermute | solution.py:118
  29.9 12.7 %collective-permute-start.8 = (bf16[256,512]{1,0:T(8,128)(2,1)S(1)}, bf16[256,512]{1,0:T(8,128)(2,1)S(1)}, u32[]{:S(2)}, u32[]{:S(2)}) collective-permute-start(bf16[256,512]{1,0:T(8,128)(2,1)S(1)} %broadcast_select_fusion), channel_id=1, source_target_pairs={{0,8},{1,9},{2,10},{3,11},{4,12},{5,13},{6,14},{7,15},{8,0},{9,1},... | collective-permute-start | bytes 786440 | tf_op jit(solution)/shard_map/a3/ppermute | solution.py:118
  33.1 11.6 %collective-permute-start.10 = (bf16[256,512]{1,0:T(8,128)(2,1)S(1)}, bf16[256,512]{1,0:T(8,128)(2,1)S(1)}, u32[]{:S(2)}, u32[]{:S(2)}) collective-permute-start(bf16[256,512]{1,0:T(8,128)(2,1)S(1)} %get-tuple-element.50.refs_19_), channel_id=1, source_target_pairs={{0,1},{1,0},{2,3},{3,2},{4,5},{5,4},{6,7},{7,6},{8,16},{9,17},{10,... | collective-permute-start | bytes 786440 | tf_op jit(solution)/shard_map/b3/ppermute | solution.py:118
  33.1 15.1 %collective-permute-start.15 = (bf16[256,512]{1,0:T(8,128)(2,1)S(1)}, bf16[256,512]{1,0:T(8,128)(2,1)S(1)}, u32[]{:S(2)}, u32[]{:S(2)}) collective-permute-start(bf16[256,512]{1,0:T(8,128)(2,1)S(1)} %collective-permute-done.4.refs_5_), channel_id=1, source_target_pairs={{0,8},{1,9},{2,10},{3,11},{4,12},{5,13},{6,14},{7,15},{8,0},{9,1},... | collective-permute-start | bytes 786440 | tf_op jit(solution)/shard_map/d0/ppermute | solution.py:118
  37.1 11.2 %collective-permute-start.9 = (bf16[256,512]{1,0:T(8,128)(2,1)S(1)}, bf16[256,512]{1,0:T(8,128)(2,1)S(1)}, u32[]{:S(2)}, u32[]{:S(2)}) collective-permute-start(bf16[256,512]{1,0:T(8,128)(2,1)S(1)} %get-tuple-element.49.refs_18_), channel_id=1, source_target_pairs={{0,1},{1,0},{2,3},{3,2},{4,5},{5,4},{6,7},{7,6},{8,16},{9,17},{10,... | collective-permute-start | bytes 786440 | tf_op jit(solution)/shard_map/b2/ppermute | solution.py:118
  37.1 11.7 %collective-permute-start.12 = (bf16[256,512]{1,0:T(8,128)(2,1)S(1)}, bf16[256,512]{1,0:T(8,128)(2,1)S(1)}, u32[]{:S(2)}, u32[]{:S(2)}) collective-permute-start(bf16[256,512]{1,0:T(8,128)(2,1)S(1)} %collective-permute-done.3.refs_1_), channel_id=1, source_target_pairs={{0,1},{1,0},{2,3},{3,2},{4,5},{5,4},{6,7},{7,6},{8,16},{9,17},{10,... | collective-permute-start | bytes 786440 | tf_op jit(solution)/shard_map/c1/ppermute | solution.py:118
  42.7 14.4 %collective-permute-start.17 = (bf16[256,512]{1,0:T(8,128)(2,1)S(1)}, bf16[256,512]{1,0:T(8,128)(2,1)S(1)}, u32[]{:S(2)}, u32[]{:S(2)}) collective-permute-start(bf16[256,512]{1,0:T(8,128)(2,1)S(1)} %collective-permute-done.11.refs_8_), channel_id=1, source_target_pairs={{0,8},{1,9},{2,10},{3,11},{4,12},{5,13},{6,14},{7,15},{8,0},{9,1},... | collective-permute-start | bytes 786440 | tf_op jit(solution)/shard_map/e0/ppermute | solution.py:118
  44.8 14.8 %collective-permute-start.16 = (bf16[256,512]{1,0:T(8,128)(2,1)S(1)}, bf16[256,512]{1,0:T(8,128)(2,1)S(1)}, u32[]{:S(2)}, u32[]{:S(2)}) collective-permute-start(bf16[256,512]{1,0:T(8,128)(2,1)S(1)} %collective-permute-done.10.refs_7_), channel_id=1, source_target_pairs={{0,8},{1,9},{2,10},{3,11},{4,12},{5,13},{6,14},{7,15},{8,0},{9,1},... | collective-permute-start | bytes 786440 | tf_op jit(solution)/shard_map/d1/ppermute | solution.py:118
  48.3 11.2 %collective-permute-start.14 = (bf16[256,512]{1,0:T(8,128)(2,1)S(1)}, bf16[256,512]{1,0:T(8,128)(2,1)S(1)}, u32[]{:S(2)}, u32[]{:S(2)}) collective-permute-start(bf16[256,512]{1,0:T(8,128)(2,1)S(1)} %collective-permute-done.8.refs_3_), channel_id=1, source_target_pairs={{0,1},{1,0},{2,3},{3,2},{4,5},{5,4},{6,7},{7,6},{8,16},{9,17},{10,... | collective-permute-start | bytes 786440 | tf_op jit(solution)/shard_map/c3/ppermute | solution.py:118
  48.3 11.2 %collective-permute-start.13 = (bf16[256,512]{1,0:T(8,128)(2,1)S(1)}, bf16[256,512]{1,0:T(8,128)(2,1)S(1)}, u32[]{:S(2)}, u32[]{:S(2)}) collective-permute-start(bf16[256,512]{1,0:T(8,128)(2,1)S(1)} %collective-permute-done.7.refs_2_), channel_id=1, source_target_pairs={{0,1},{1,0},{2,3},{3,2},{4,5},{5,4},{6,7},{7,6},{8,16},{9,17},{10,... | collective-permute-start | bytes 786440 | tf_op jit(solution)/shard_map/c2/ppermute | solution.py:118
  48.8 14.4 %collective-permute-start.18 = (bf16[256,512]{1,0:T(8,128)(2,1)S(1)}, bf16[256,512]{1,0:T(8,128)(2,1)S(1)}, u32[]{:S(2)}, u32[]{:S(2)}) collective-permute-start(bf16[256,512]{1,0:T(8,128)(2,1)S(1)} %collective-permute-done.12.refs_9_), channel_id=1, source_target_pairs={{0,8},{1,9},{2,10},{3,11},{4,12},{5,13},{6,14},{7,15},{8,0},{9,1},... | collective-permute-start | bytes 786440 | tf_op jit(solution)/shard_map/e1/ppermute | solution.py:118
  63.6 8.8 %collective-permute-start.20 = (bf16[256,512]{1,0:T(8,128)(2,1)S(1)}, bf16[256,512]{1,0:T(8,128)(2,1)S(1)}, u32[]{:S(2)}, u32[]{:S(2)}) collective-permute-start(bf16[256,512]{1,0:T(8,128)(2,1)S(1)} %collective-permute-done.14.refs_11_), channel_id=1, source_target_pairs={{0,2},{1,9},{2,0},{3,11},{4,6},{5,13},{6,4},{7,15},{8,10},{9,1},{1... | collective-permute-start | bytes 786440 | tf_op jit(solution)/shard_map/l0/ppermute | solution.py:118
  69.0 10.6 %collective-permute-start.29 = (bf16[512,256]{1,0:T(8,128)(2,1)S(1)}, bf16[512,256]{1,0:T(8,128)(2,1)S(1)}, u32[]{:S(2)}, u32[]{:S(2)}) collective-permute-start(bf16[512,256]{1,0:T(8,128)(2,1)S(1)} %pad_maximum_fusion.3), channel_id=1, source_target_pairs={{0,4},{1,5},{2,6},{3,7},{4,0},{5,1},{6,2},{7,3},{8,12},{9,13},{10,... | collective-permute-start | bytes 786440 | tf_op jit(solution)/shard_map/first_y/ppermute | solution.py:118
  73.8 9.5 %collective-permute-start.25 = (bf16[512,256]{1,0:T(8,128)(2,1)S(1)}, bf16[512,256]{1,0:T(8,128)(2,1)S(1)}, u32[]{:S(2)}, u32[]{:S(2)}) collective-permute-start(bf16[512,256]{1,0:T(8,128)(2,1)S(1)} %pad_maximum_fusion.1), channel_id=1, source_target_pairs={{0,4},{1,5},{2,6},{3,7},{4,0},{5,1},{6,2},{7,3},{8,12},{9,13},{10,... | collective-permute-start | bytes 786440 | tf_op jit(solution)/shard_map/second_y/ppermute | solution.py:118
  77.0 9.8 %collective-permute-start.23 = (bf16[512,256]{1,0:T(8,128)(2,1)S(1)}, bf16[512,256]{1,0:T(8,128)(2,1)S(1)}, u32[]{:S(2)}, u32[]{:S(2)}) collective-permute-start(bf16[512,256]{1,0:T(8,128)(2,1)S(1)} %pad_maximum_fusion), channel_id=1, source_target_pairs={{0,2},{1,3},{2,0},{3,1},{4,6},{5,7},{6,4},{7,5},{8,10},{9,11},{10,... | collective-permute-start | bytes 786440 | tf_op jit(solution)/shard_map/second_x/ppermute | solution.py:118
  79.6 10.0 %collective-permute-start.30 = (bf16[512,128]{1,0:T(8,128)(2,1)S(1)}, bf16[512,128]{1,0:T(8,128)(2,1)S(1)}, u32[]{:S(2)}, u32[]{:S(2)}) collective-permute-start(bf16[512,128]{1,0:T(8,128)(2,1)S(1)} %add_convert_fusion), channel_id=1, source_target_pairs={{0,2},{1,3},{2,0},{3,1},{4,6},{5,7},{6,4},{7,5},{8,10},{9,11},{10,... | collective-permute-start | bytes 393224 | tf_op jit(solution)/shard_map/first_then_x/ppermute | solution.py:118
  79.8 9.8 %collective-permute-start.28 = (bf16[512,128]{1,0:T(8,128)(2,1)S(1)}, bf16[512,128]{1,0:T(8,128)(2,1)S(1)}, u32[]{:S(2)}, u32[]{:S(2)}) collective-permute-start(bf16[512,128]{1,0:T(8,128)(2,1)S(1)} %add_convert_fusion.1), channel_id=1, source_target_pairs={{0,4},{1,5},{2,6},{3,7},{4,0},{5,1},{6,2},{7,3},{8,12},{9,13},{10,... | collective-permute-start | bytes 393224 | tf_op jit(solution)/shard_map/first_then_y/ppermute | solution.py:118
  (13 other events, 75.1 us)
